TPU v7x, 32 devices: a whole 2x2x4 slice. The times are simulated.
32 devices in a mesh: groups: 2 (over x), tm: 16 (over z, y, core).
Axes of the slice: x: 2, y: 2, z: 4, core: 2. Of those that a mesh axis runs over, the one named last changes fastest.
Arguments:
- signal: float32 [64, 16384], P(None, ('groups', 'tm')), parts along dimension 1, may hold values from -32 to 32
- dictionary: bfloat16 [256, 64, 128], replicated, may hold values from -4 to 4
- step: float32 [1], replicated, may hold values from 0.04 to 0.08
Outputs:
- codes: float32 [256, 16384], P(None, ('groups', 'tm')), parts along dimension 1
- new_dictionary: float32 [512, 64, 128], P(('groups', 'tm')), parts along dimension 0
- loss: float32 [2], P('groups'), parts along dimension 0
There are 2 independent parts, one for each index of `groups`. A program takes and returns all parts, laid end to end along the dimension named above; an argument that names none is the same for every part. Nothing has to cross between parts.
All inputs are finite; a program needn't handle non-finite values.
Results may differ from a plain program's by a relative error of at most 0.0022.
Values may be sent and summed in bfloat16 or wider, within the bound.
No kernel may reach another device: no remote copies, remote signals or barrier semaphores. Data moves between devices by JAX's collectives and lax.ppermute only.
A program may use at most 128 MiB of HBM per device.

v0:
```python
import math

import jax
import jax.numpy as jnp
from jax import lax
from jax.experimental import pallas as pl
from jax.experimental.pallas import tpu as pltpu
from jax.sharding import PartitionSpec as P

ATOMS = 256
CHANNELS = 64
ATOM_LEN = 128
SPARSITY = 0.05
DICT_RATE = 0.5
EPSILON = 1e-06

SCALE = 1.0 / math.sqrt(CHANNELS * ATOM_LEN)
FINE = 16
COARSE = ATOM_LEN // FINE
WIDE = FINE * CHANNELS
HALO = 2 * ATOM_LEN
F32 = jnp.float32
BF16 = jnp.bfloat16
VMEM_LIMIT = 56 * 1024 * 1024


def vmem():
    return pl.BlockSpec(memory_space=pltpu.VMEM)


def smem():
    return pl.BlockSpec(memory_space=pltpu.SMEM)


def kernel_params():
    return pltpu.CompilerParams(vmem_limit_bytes=VMEM_LIMIT)


def shifted(value, axis, steps):
    count = lax.axis_size(axis)
    leading, last = (max(0, -steps), min(count, count - steps))
    return lax.ppermute(value, axis, [(source, source + steps) for source in range(leading, last)])


def swapped(value, bit):
    count = lax.axis_size("tm")
    return lax.ppermute(value, "tm", [(i, i ^ bit) for i in range(count)])


def fill_windows(pairs, windows, rows):
    for step in range(FINE // 2):
        windows[0:rows, step * 128 : (step + 1) * 128] = pairs[
            2 * step : 2 * step + rows, :
        ].astype(BF16)


def adjoint(windows, lags, total, start, rows):
    for coarse in range(COARSE):
        part = jnp.dot(
            windows[start + coarse * FINE : start + coarse * FINE + rows, :],
            lags[coarse * WIDE : (coarse + 1) * WIDE, :],
            preferred_element_type=F32,
        )
        if coarse == 0:
            total[0:rows, :] = part
        else:
            total[0:rows, :] += part


def first_kernel(left, middle, right, lags, gradient, largest, pairs, windows):
    width = middle.shape[1]
    rows = width + 3 * ATOM_LEN
    whole = jnp.concatenate([left[...], middle[...], right[...]], 1)
    whole = -whole
    both = jnp.concatenate([whole, pltpu.roll(whole, whole.shape[1] - 1, 1)], 0)
    pairs[0 : width + 2 * HALO, :] = both.T
    fill_windows(pairs, windows, width + 2 * HALO - FINE)
    adjoint(windows, lags, gradient, 0, rows)
    own = jnp.abs(gradient[HALO : HALO + width, :]) * SCALE
    folded = jnp.max(own.reshape(width // 8, 8, ATOMS), 0)
    largest[...] = jnp.maximum(folded[:, :128], folded[:, 128:])


def forward(codes, lags, spread, start, rows, first):
    for coarse in range(COARSE):
        low = start - coarse * FINE
        part = lax.dot_general(
            codes[low : low + rows, :],
            lags[coarse * WIDE : (coarse + 1) * WIDE, :],
            (((1,), (1,)), ((), ())),
            preferred_element_type=F32,
        )
        if coarse == 0:
            spread[0:rows, :] = part
        else:
            spread[0:rows, :] += part
    keep = rows - FINE
    total = spread[FINE : FINE + keep, 0:128]
    odd = spread[FINE - 1 : FINE - 1 + keep, 0:128]
    for step in range(1, FINE // 2):
        lanes = slice(step * 128, (step + 1) * 128)
        total = total + spread[FINE - 2 * step : FINE - 2 * step + keep, lanes]
        odd = odd + spread[FINE - 1 - 2 * step : FINE - 1 - 2 * step + keep, lanes]
    return total[:, 0:64] + odd[:, 64:128]


def soft(moved, bound):
    return jnp.where(moved > 0, 1.0, -1.0) * jnp.maximum(jnp.abs(moved) - bound, 0.0)


def second_kernel(
    left, middle, right, lags, gradient, peak, step, valid,
    codes_out, ahead_out, resid_out, loss_out,
    signal, codes, codes_low, pairs, windows, spread,
):
    width = middle.shape[1]
    step_size = step[0]
    threshold = SPARSITY * jnp.max(peak[...])
    bound = step_size * threshold
    low, high = valid[0], valid[1]
    whole = jnp.concatenate([left[...], middle[...], right[...]], 1)
    signal[...] = whole.T

    def row(start, count):
        return lax.broadcasted_iota(jnp.int32, (count, 1), 0) + start

    rows1 = width + 3 * ATOM_LEN
    moved = -step_size * (gradient[...] * SCALE)
    updated = jnp.where(row(0, rows1) >= low, soft(moved, bound), 0.0)
    codes[...] = updated
    codes_low[...] = updated.astype(BF16)
    rows2 = width + 2 * ATOM_LEN
    model = forward(codes_low, lags, spread, ATOM_LEN - FINE, rows2 + FINE, 0)
    resid = model * SCALE - signal[ATOM_LEN : ATOM_LEN + rows2, :]
    resid = jnp.where(row(ATOM_LEN, rows2) < high, resid, 0.0)
    pairs[0:rows2, 0:64] = resid
    pairs[0 : rows2 - 1, 64:128] = pairs[1:rows2, 0:64]
    fill_windows(pairs, windows, rows2 - FINE)
    rows3 = width + ATOM_LEN
    adjoint(windows, lags, spread.at[:, 0:ATOMS], 0, rows3)
    before = codes[ATOM_LEN : ATOM_LEN + rows3, :]
    moved = before - step_size * (spread[0:rows3, 0:ATOMS] * SCALE)
    updated = jnp.where(row(ATOM_LEN, rows3) >= low, soft(moved, bound), 0.0)
    codes[0:rows3, :] = updated
    codes_low[0:rows3, :] = updated.astype(BF16)
    turned = updated.T
    ahead_out[...] = turned.astype(BF16)
    codes_out[...] = turned[:, ATOM_LEN:]
    sparse = jnp.sum(jnp.abs(codes[ATOM_LEN:rows3, :]))
    model = forward(codes_low, lags, spread, ATOM_LEN - FINE, width + FINE, 0)
    resid = model * SCALE - signal[HALO : HALO + width, :]
    resid_out[...] = resid.T.astype(BF16)
    loss = 0.5 * jnp.sum(resid * resid) + threshold * sparse
    loss_out[...] = jnp.full((8, 128), loss, F32)


def correlate_kernel(codes, resid, out, pairs, windows):
    blocks, atoms, length = codes.shape
    width = resid.shape[2]
    rows = width + 2 * FINE
    used = width + FINE
    pairs[...] = jnp.zeros_like(pairs)

    def one(block, carry):
        piece = resid[block].astype(F32)
        pairs[FINE : FINE + width, 0:64] = piece.T
        pairs[0 : FINE + width, 64:128] = pairs[1 : FINE + width + 1, 0:64]
        fill_windows(pairs, windows, used)
        held = codes[block].astype(F32)
        stack = []
        for coarse in range(COARSE):
            start = ATOM_LEN - FINE - coarse * FINE
            turned = held if start == 0 else pltpu.roll(held, length - start, 1)
            stack.append(turned[:, 0:used].astype(BF16))
        part = jnp.dot(jnp.concatenate(stack, 0), windows[0:used, :], preferred_element_type=F32)
        out[...] += part
        return carry

    out[...] = jnp.zeros_like(out)
    lax.fori_loop(0, blocks, one, 0)


def body(signal, dictionary, step):
    width = signal.shape[1]
    count = lax.axis_size("tm")
    me = lax.axis_index("tm")
    left = shifted(signal[:, width - HALO :], "tm", 1)
    right = shifted(signal[:, :HALO], "tm", -1)
    lags = jnp.transpose(dictionary, (2, 1, 0)).reshape(ATOM_LEN * CHANNELS, ATOMS)
    rows1 = width + 3 * ATOM_LEN
    span = width + 2 * HALO

    gradient, peak = pl.pallas_call(
        first_kernel,
        out_shape=(
            jax.ShapeDtypeStruct((rows1, ATOMS), F32),
            jax.ShapeDtypeStruct((8, 128), F32),
        ),
        in_specs=[vmem()] * 4,
        out_specs=(vmem(), vmem()),
        scratch_shapes=[pltpu.VMEM((span, 128), F32), pltpu.VMEM((span, WIDE), BF16)],
        compiler_params=kernel_params(),
    )(left, signal, right, lags)

    bit = 1
    while bit < count:
        peak = jnp.maximum(peak, swapped(peak, bit))
        bit *= 2

    valid = jnp.stack(
        [jnp.where(me == 0, HALO, 0), jnp.where(me == count - 1, HALO + width, span)]
    ).astype(jnp.int32)
    codes, ahead, resid, loss = pl.pallas_call(
        second_kernel,
        out_shape=(
            jax.ShapeDtypeStruct((ATOMS, width), F32),
            jax.ShapeDtypeStruct((ATOMS, width + ATOM_LEN), BF16),
            jax.ShapeDtypeStruct((CHANNELS, width), BF16),
            jax.ShapeDtypeStruct((8, 128), F32),
        ),
        in_specs=[vmem()] * 6 + [smem()] * 2,
        out_specs=(vmem(),) * 4,
        scratch_shapes=[
            pltpu.VMEM((span, CHANNELS), F32),
            pltpu.VMEM((rows1, ATOMS), F32),
            pltpu.VMEM((rows1, ATOMS), BF16),
            pltpu.VMEM((rows1, 128), F32),
            pltpu.VMEM((rows1, WIDE), BF16),
            pltpu.VMEM((rows1, WIDE), F32),
        ],
        compiler_params=kernel_params(),
    )(left, signal, right, lags, gradient, peak, step, valid)

    owned = ATOMS // count

    def correlate(codes_blocks, resid_blocks):
        atoms = codes_blocks.shape[1]
        out = pl.pallas_call(
            correlate_kernel,
            out_shape=jax.ShapeDtypeStruct((COARSE * atoms, WIDE), F32),
            in_specs=[vmem()] * 2,
            out_specs=vmem(),
            scratch_shapes=[
                pltpu.VMEM((width + 3 * FINE, 128), F32),
                pltpu.VMEM((width + 2 * FINE, WIDE), BF16),
            ],
            compiler_params=kernel_params(),
        )(codes_blocks, resid_blocks)
        return out.reshape(COARSE, atoms, WIDE)

    if count == 16:
        groups = [[2 * i + core for i in range(8)] for core in range(2)]
        pieces = jnp.concatenate(
            [
                ahead.reshape(8, 2 * owned, width + ATOM_LEN),
                jnp.broadcast_to(
                    jnp.pad(resid, ((0, 0), (0, ATOM_LEN)))[None],
                    (8, CHANNELS, width + ATOM_LEN),
                ),
            ],
            1,
        )
        taken = lax.all_to_all(pieces, "tm", 0, 0, axis_index_groups=groups, tiled=False)
        part = correlate(taken[:, : 2 * owned], taken[:, 2 * owned :, :width])
        core = me % 2
        give = lax.dynamic_slice_in_dim(part, (1 - core) * owned, owned, 1)
        keep = lax.dynamic_slice_in_dim(part, core * owned, owned, 1)
        summed = keep + swapped(give, 1)
    else:
        part = correlate(ahead[None], resid[None])
        summed = lax.psum_scatter(part, "tm", scatter_dimension=1, tiled=True)
    atom_gradient = (
        summed.reshape(COARSE, owned, FINE, CHANNELS)
        .transpose(1, 3, 0, 2)
        .reshape(owned, CHANNELS, ATOM_LEN)
    )
    own_atoms = lax.dynamic_slice_in_dim(dictionary, me * owned, owned, 0).astype(F32)
    normed = atom_gradient / jnp.sqrt(
        jnp.mean(atom_gradient * atom_gradient, axis=(1, 2), keepdims=True) + EPSILON
    )
    shifted_atoms = own_atoms - DICT_RATE * normed
    new_dictionary = shifted_atoms / jnp.sqrt(
        jnp.mean(shifted_atoms * shifted_atoms, axis=(1, 2), keepdims=True) + EPSILON
    )
    bit = 1
    while bit < count:
        loss = loss + swapped(loss, bit)
        bit *= 2
    loss = loss[0, :1] / (CHANNELS * width * count)
    return (codes, new_dictionary, loss)


def solution(mesh):
    return jax.shard_map(
        body,
        mesh=mesh,
        in_specs=(P(None, ("groups", "tm")), P(), P()),
        out_specs=(P(None, ("groups", "tm")), P(("groups", "tm"), None, None), P("groups")),
        check_vma=False,
    )
```

profile of v0, /device:TPU:0, one launch (start us, length us, event | category | flops | bytes accessed | tf_op | source)
XLA Modules:
  0.0 119.3 jit_solution(14320741478493590558)
XLA Ops:
  0.6 0.9 fusion.3
  1.5 2.4 %collective-permute-start = (f32[64,256]{1,0:T(8,128)S(1)}, f32[64,256]{1,0:T(8,128)S(1)}, u32[]{:S(2)}, u32[]{:S(2)}) collective-permute-start(f32[64,256]{1,0:T(8,128)S(1)} %get-tuple-element.19), channel_id=1, source_target_pairs={{0,1},{1,2},{2,3},{3,4},{4,5},{5,6},{6,7},{7,8},{8,9},{9,10},{10,1... | collective-permute-start | bytes 196616 | tf_op jit(solution)/shard_map/ppermute | solution.py:42
  3.9 1.3 %collective-permute-start.1 = (f32[64,256]{1,0:T(8,128)S(1)}, f32[64,256]{1,0:T(8,128)S(1)}, u32[]{:S(2)}, u32[]{:S(2)}) collective-permute-start(f32[64,256]{1,0:T(8,128)S(1)} %get-tuple-element.18), channel_id=1, source_target_pairs={{1,0},{2,1},{3,2},{4,3},{5,4},{6,5},{7,6},{8,7},{9,8},{10,9},{11,1... | collective-permute-start | bytes 196616 | tf_op jit(solution)/shard_map/ppermute | solution.py:42
  5.2 7.3 %copy.8 = bf16[128,64,256]{2,1,0:T(8,128)(2,1)} copy(bf16[128,64,256]{0,1,2:T(8,128)(2,1)} %bitcast.26) | data formatting | bytes 8388608 | tf_op jit(solution)/shard_map/transpose | solution.py:189
  12.5 0.6 copy-done
  13.2 7.6 %shard_map.58 = (f32[896,256]{1,0:T(8,128)}, f32[8,128]{1,0:T(8,128)}) custom-call(f32[64,256]{1,0:T(8,128)} %copy-done, f32[64,512]{1,0:T(8,128)} %middle.3, f32[64,256]{1,0:T(8,128)} %copy-done.1, bf16[8192,256]{1,0:T(8,128)(2,1)} %bitcast.24), custom_call_target="tpu_custom_call" | custom-call | tf_op jit(solution)/shard_map/pallas_call | solution.py:193
  20.8 3.3 %collective-permute-start.2 = (f32[8,128]{1,0:T(8,128)}, f32[8,128]{1,0:T(8,128)S(1)}, u32[]{:S(2)}, u32[]{:S(2)}) collective-permute-start(f32[8,128]{1,0:T(8,128)} %get-tuple-element.10), channel_id=1, source_target_pairs={{0,1},{1,0},{2,3},{3,2},{4,5},{5,4},{6,7},{7,6},{8,9},{9,8},{10,11... | collective-permute-start | bytes 12296 | tf_op jit(solution)/shard_map/ppermute | solution.py:47
  24.0 1.0 collective-permute-done.2
  25.1 0.7 max.12
  25.8 2.0 %collective-permute-start.3 = (f32[8,128]{1,0:T(8,128)S(1)}, f32[8,128]{1,0:T(8,128)S(1)}, u32[]{:S(2)}, u32[]{:S(2)}) collective-permute-start(f32[8,128]{1,0:T(8,128)S(1)} %max.12), channel_id=1, source_target_pairs={{0,2},{1,3},{2,0},{3,1},{4,6},{5,7},{6,4},{7,5},{8,10},{9,11},{10,... | collective-permute-start | bytes 12296 | tf_op jit(solution)/shard_map/ppermute | solution.py:47
  27.7 1.6 %collective-permute-done.3 = f32[8,128]{1,0:T(8,128)S(1)} collective-permute-done((f32[8,128]{1,0:T(8,128)S(1)}, f32[8,128]{1,0:T(8,128)S(1)}, u32[]{:S(2)}, u32[]{:S(2)}) %collective-permute-start.3) | collective-permute-done | bytes 4128 | tf_op jit(solution)/shard_map/ppermute | solution.py:47
  29.4 2.9 %collective-permute-start.4 = (f32[8,128]{1,0:T(8,128)S(1)}, f32[8,128]{1,0:T(8,128)S(1)}, u32[]{:S(2)}, u32[]{:S(2)}) collective-permute-start(f32[8,128]{1,0:T(8,128)S(1)} %max.13), channel_id=1, source_target_pairs={{0,4},{1,5},{2,6},{3,7},{4,0},{5,1},{6,2},{7,3},{8,12},{9,13},{10,... | collective-permute-start | bytes 12296 | tf_op jit(solution)/shard_map/ppermute | solution.py:47
  32.3 1.6 %collective-permute-done.4 = f32[8,128]{1,0:T(8,128)S(1)} collective-permute-done((f32[8,128]{1,0:T(8,128)S(1)}, f32[8,128]{1,0:T(8,128)S(1)}, u32[]{:S(2)}, u32[]{:S(2)}) %collective-permute-start.4) | collective-permute-done | bytes 4128 | tf_op jit(solution)/shard_map/ppermute | solution.py:47
  33.9 3.0 %collective-permute-start.5 = (f32[8,128]{1,0:T(8,128)S(1)}, f32[8,128]{1,0:T(8,128)S(1)}, u32[]{:S(2)}, u32[]{:S(2)}) collective-permute-start(f32[8,128]{1,0:T(8,128)S(1)} %max.14), channel_id=1, source_target_pairs={{0,8},{1,9},{2,10},{3,11},{4,12},{5,13},{6,14},{7,15},{8,0},{9,1},... | collective-permute-start | bytes 12296 | tf_op jit(solution)/shard_map/ppermute | solution.py:47
  36.9 0.7 pad_add_fusion.valid
  39.1 18.3 %shard_map.59 = (f32[256,512]{1,0:T(8,128)}, bf16[256,640]{1,0:T(8,128)(2,1)}, bf16[64,512]{1,0:T(8,128)(2,1)}, f32[8,128]{1,0:T(8,128)}) custom-call(f32[64,256]{1,0:T(8,128)} %copy-done, f32[64,512]{1,0:T(8,128)} %middle.3, f32[64,256]{1,0:T(8,128)} %copy-done.1, bf16[8192,256]{1,0:T(8,128)(2,1)} %bitcast.25, f32[896,256]{1,0:T(8,128)} %get-tuple-element.9.gradient, ...), custom_call_target="tpu_custom_call" | custom-call | tf_op jit(solution)/shard_map/pallas_call | solution.py:213
  57.4 0.8 pad.4
  58.3 2.0 %pad_maximum_fusion = bf16[8,96,640]{2,1,0:T(8,128)(2,1)} fusion(bf16[8,64,640]{2,1,0:T(8,128)(2,1)S(1)} %broadcast_in_dim.2, bf16[8,32,640]{2,1,0:T(8,128)(2,1)} %bitcast.29), kind=kLoop, calls=%fused_computation.6 | loop fusion | flops 1966080 | bytes 1966080 | tf_op jit(solution)/shard_map/concatenate | solution.py:253
  60.3 5.3 %all-to-all-start = ((bf16[8,96,640]{2,1,0:T(8,128)(2,1)}), bf16[8,96,640]{2,1,0:T(8,128)(2,1)S(1)}, u32[]{:S(2)}, u32[]{:S(2)}) async-start(bf16[8,96,640]{2,1,0:T(8,128)(2,1)} %pad_maximum_fusion), calls=%async_computation | async-start | bytes 1966080 | tf_op jit(solution)/shard_map/all_to_all | solution.py:263
  65.6 21.5 %all-to-all-done = bf16[8,96,640]{2,1,0:T(8,128)(2,1)S(1)} async-done(((bf16[8,96,640]{2,1,0:T(8,128)(2,1)}), bf16[8,96,640]{2,1,0:T(8,128)(2,1)S(1)}, u32[]{:S(2)}, u32[]{:S(2)}) %all-to-all-start) | async-done | bytes 983072 | tf_op jit(solution)/shard_map/all_to_all | solution.py:263
  87.0 0.8 slice.21.resid
  87.9 0.8 slice.20.codes
  88.6 9.8 %shard_map.60 = f32[256,1024]{1,0:T(8,128)} custom-call(bf16[8,32,640]{2,1,0:T(8,128)(2,1)} %slice.20.codes, bf16[8,64,512]{2,1,0:T(8,128)(2,1)} %slice.21.resid), custom_call_target="tpu_custom_call" | custom-call | tf_op jit(solution)/shard_map/pallas_call | solution.py:238
  98.5 1.1 constant_dynamic-slice_fusion
  100.1 1.4 %collective-permute-done.7 = f32[8,128]{1,0:T(8,128)S(1)} collective-permute-done((f32[8,128]{1,0:T(8,128)S(1)}, f32[8,128]{1,0:T(8,128)S(1)}, u32[]{:S(2)}, u32[]{:S(2)}) %collective-permute-start.7) | collective-permute-done | bytes 4128 | tf_op jit(solution)/shard_map/ppermute | solution.py:47
  101.5 1.2 %collective-permute-start.8 = (f32[8,128]{1,0:T(8,128)S(1)}, f32[8,128]{1,0:T(8,128)S(1)}, u32[]{:S(2)}, u32[]{:S(2)}) collective-permute-start(f32[8,128]{1,0:T(8,128)S(1)} %add.53), channel_id=1, source_target_pairs={{0,2},{1,3},{2,0},{3,1},{4,6},{5,7},{6,4},{7,5},{8,10},{9,11},{10,... | collective-permute-start | bytes 12296 | tf_op jit(solution)/shard_map/ppermute | solution.py:47
  102.7 2.4 %collective-permute-done.8 = f32[8,128]{1,0:T(8,128)S(1)} collective-permute-done((f32[8,128]{1,0:T(8,128)S(1)}, f32[8,128]{1,0:T(8,128)S(1)}, u32[]{:S(2)}, u32[]{:S(2)}) %collective-permute-start.8) | collective-permute-done | bytes 4128 | tf_op jit(solution)/shard_map/ppermute | solution.py:47
  105.1 3.6 %collective-permute-done.9 = f32[8,128]{1,0:T(8,128)S(1)} collective-permute-done((f32[8,128]{1,0:T(8,128)S(1)}, f32[8,128]{1,0:T(8,128)S(1)}, u32[]{:S(2)}, u32[]{:S(2)}) %collective-permute-start.9) | collective-permute-done | bytes 4128 | tf_op jit(solution)/shard_map/ppermute | solution.py:47
  108.7 1.0 constant_dynamic-slice_fusion.1
  110.0 3.2 %collective-permute-done.10 = f32[8,128]{1,0:T(8,128)S(1)} collective-permute-done((f32[8,128]{1,0:T(8,128)S(1)}, f32[8,128]{1,0:T(8,128)S(1)}, u32[]{:S(2)}, u32[]{:S(2)}) %collective-permute-start.10) | collective-permute-done | bytes 4128 | tf_op jit(solution)/shard_map/ppermute | solution.py:47
  114.4 1.1 dynamic-slice_add_fusion
  117.1 1.1 copy.11
  (30 shorter events, 3.9 us)
Async XLA Ops:
  1.5 11.0 %collective-permute-start = (f32[64,256]{1,0:T(8,128)S(1)}, f32[64,256]{1,0:T(8,128)S(1)}, u32[]{:S(2)}, u32[]{:S(2)}) collective-permute-start(f32[64,256]{1,0:T(8,128)S(1)} %get-tuple-element.19), channel_id=1, source_target_pairs={{0,1},{1,2},{2,3},{3,4},{4,5},{5,6},{6,7},{7,8},{8,9},{9,10},{10,1... | collective-permute-start | bytes 196616 | tf_op jit(solution)/shard_map/ppermute | solution.py:42
  3.9 8.6 %collective-permute-start.1 = (f32[64,256]{1,0:T(8,128)S(1)}, f32[64,256]{1,0:T(8,128)S(1)}, u32[]{:S(2)}, u32[]{:S(2)}) collective-permute-start(f32[64,256]{1,0:T(8,128)S(1)} %get-tuple-element.18), channel_id=1, source_target_pairs={{1,0},{2,1},{3,2},{4,3},{5,4},{6,5},{7,6},{8,7},{9,8},{10,9},{11,1... | collective-permute-start | bytes 196616 | tf_op jit(solution)/shard_map/ppermute | solution.py:42
  12.5 0.6 copy-start
  12.5 0.6 copy-start.1
  20.8 4.3 %collective-permute-start.2 = (f32[8,128]{1,0:T(8,128)}, f32[8,128]{1,0:T(8,128)S(1)}, u32[]{:S(2)}, u32[]{:S(2)}) collective-permute-start(f32[8,128]{1,0:T(8,128)} %get-tuple-element.10), channel_id=1, source_target_pairs={{0,1},{1,0},{2,3},{3,2},{4,5},{5,4},{6,7},{7,6},{8,9},{9,8},{10,11... | collective-permute-start | bytes 12296 | tf_op jit(solution)/shard_map/ppermute | solution.py:47
  25.8 3.6 %collective-permute-start.3 = (f32[8,128]{1,0:T(8,128)S(1)}, f32[8,128]{1,0:T(8,128)S(1)}, u32[]{:S(2)}, u32[]{:S(2)}) collective-permute-start(f32[8,128]{1,0:T(8,128)S(1)} %max.12), channel_id=1, source_target_pairs={{0,2},{1,3},{2,0},{3,1},{4,6},{5,7},{6,4},{7,5},{8,10},{9,11},{10,... | collective-permute-start | bytes 12296 | tf_op jit(solution)/shard_map/ppermute | solution.py:47
  29.4 4.5 %collective-permute-start.4 = (f32[8,128]{1,0:T(8,128)S(1)}, f32[8,128]{1,0:T(8,128)S(1)}, u32[]{:S(2)}, u32[]{:S(2)}) collective-permute-start(f32[8,128]{1,0:T(8,128)S(1)} %max.13), channel_id=1, source_target_pairs={{0,4},{1,5},{2,6},{3,7},{4,0},{5,1},{6,2},{7,3},{8,12},{9,13},{10,... | collective-permute-start | bytes 12296 | tf_op jit(solution)/shard_map/ppermute | solution.py:47
  33.9 4.6 %collective-permute-start.5 = (f32[8,128]{1,0:T(8,128)S(1)}, f32[8,128]{1,0:T(8,128)S(1)}, u32[]{:S(2)}, u32[]{:S(2)}) collective-permute-start(f32[8,128]{1,0:T(8,128)S(1)} %max.14), channel_id=1, source_target_pairs={{0,8},{1,9},{2,10},{3,11},{4,12},{5,13},{6,14},{7,15},{8,0},{9,1},... | collective-permute-start | bytes 12296 | tf_op jit(solution)/shard_map/ppermute | solution.py:47
  58.3 41.3 %copy-start.2 = (f32[8,128]{1,0:T(8,128)S(1)}, f32[8,128]{1,0:T(8,128)}, u32[]{:S(2)}) copy-start(f32[8,128]{1,0:T(8,128)} %get-tuple-element.14) | copy-start | bytes 12292
  60.3 26.7 %all-to-all-start = ((bf16[8,96,640]{2,1,0:T(8,128)(2,1)}), bf16[8,96,640]{2,1,0:T(8,128)(2,1)S(1)}, u32[]{:S(2)}, u32[]{:S(2)}) async-start(bf16[8,96,640]{2,1,0:T(8,128)(2,1)} %pad_maximum_fusion), calls=%async_computation | async-start | bytes 1966080 | tf_op jit(solution)/shard_map/all_to_all | solution.py:263
  99.5 14.9 %collective-permute-start.6 = (f32[8,16,1024]{2,1,0:T(8,128)S(1)}, f32[8,16,1024]{2,1,0:T(8,128)S(1)}, u32[]{:S(2)}, u32[]{:S(2)}) collective-permute-start(f32[8,16,1024]{2,1,0:T(8,128)S(1)} %constant_dynamic-slice_fusion), channel_id=1, source_target_pairs={{0,1},{1,0},{2,3},{3,2},{4,5},{5,4},{6,7},{7,6},{8,9},{9,8},{10,11... | collective-permute-start | bytes 1572872 | tf_op jit(solution)/shard_map/ppermute | solution.py:47
  99.6 1.9 %collective-permute-start.7 = (f32[8,128]{1,0:T(8,128)S(1)}, f32[8,128]{1,0:T(8,128)S(1)}, u32[]{:S(2)}, u32[]{:S(2)}) collective-permute-start(f32[8,128]{1,0:T(8,128)S(1)} %copy-done.2), channel_id=1, source_target_pairs={{0,1},{1,0},{2,3},{3,2},{4,5},{5,4},{6,7},{7,6},{8,9},{9,8},{10,11... | collective-permute-start | bytes 12296 | tf_op jit(solution)/shard_map/ppermute | solution.py:47
  101.5 3.6 %collective-permute-start.8 = (f32[8,128]{1,0:T(8,128)S(1)}, f32[8,128]{1,0:T(8,128)S(1)}, u32[]{:S(2)}, u32[]{:S(2)}) collective-permute-start(f32[8,128]{1,0:T(8,128)S(1)} %add.53), channel_id=1, source_target_pairs={{0,2},{1,3},{2,0},{3,1},{4,6},{5,7},{6,4},{7,5},{8,10},{9,11},{10,... | collective-permute-start | bytes 12296 | tf_op jit(solution)/shard_map/ppermute | solution.py:47
  105.1 3.6 %collective-permute-start.9 = (f32[8,128]{1,0:T(8,128)S(1)}, f32[8,128]{1,0:T(8,128)S(1)}, u32[]{:S(2)}, u32[]{:S(2)}) collective-permute-start(f32[8,128]{1,0:T(8,128)S(1)} %add.54), channel_id=1, source_target_pairs={{0,4},{1,5},{2,6},{3,7},{4,0},{5,1},{6,2},{7,3},{8,12},{9,13},{10,... | collective-permute-start | bytes 12296 | tf_op jit(solution)/shard_map/ppermute | solution.py:47
  108.7 4.5 %collective-permute-start.10 = (f32[8,128]{1,0:T(8,128)S(1)}, f32[8,128]{1,0:T(8,128)S(1)}, u32[]{:S(2)}, u32[]{:S(2)}) collective-permute-start(f32[8,128]{1,0:T(8,128)S(1)} %add.55), channel_id=1, source_target_pairs={{0,8},{1,9},{2,10},{3,11},{4,12},{5,13},{6,14},{7,15},{8,0},{9,1},... | collective-permute-start | bytes 12296 | tf_op jit(solution)/shard_map/ppermute | solution.py:47
where the time goes:
time: 120 us; the launch traced here: 119 us
  waiting for transfers between devices  36.6 us (30%)
  Pallas kernels  35.7 us (30%)
  starting transfers between devices  21.9 us (18%)
  local copies, waits for them, and re-layouts  15.9 us (13%)
  other arithmetic  6.01 us (5%)
  between operations  3.2 us (3%)
    all_to_all x1, waiting for transfers between devices, body(): lax.all_to_all(pieces, 'tm', 0, 0, axis_index_groups=groups, tiled=False)  21.5 us
    pallas_call x1, Pallas kernels, body(): pl.pallas_call(second_kernel, out_shape=(jax.ShapeDtypeStruct((ATOMS, wid...  18.3 us
    ppermute x9, waiting for transfers between devices, swapped(): return lax.ppermute(value, 'tm', [(i, i ^ bit) for i in range(count)])  15.2 us
    ppermute x9, starting transfers between devices, swapped(): return lax.ppermute(value, 'tm', [(i, i ^ bit) for i in range(count)])  12.9 us
    pallas_call x1, Pallas kernels, correlate(): pl.pallas_call(correlate_kernel, out_shape=jax.ShapeDtypeStruct((COARSE *...  9.82 us
    pallas_call x1, Pallas kernels, body(): pl.pallas_call(first_kernel, out_shape=(jax.ShapeDtypeStruct((rows1, ATOM...  7.62 us
    transpose x1, local copies, waits for them, and re-layouts, body(): jnp.transpose(dictionary, (2, 1, 0)).reshape(ATOM_LEN * CHANNELS, ATOMS)  7.33 us
    all_to_all x1, starting transfers between devices, body(): lax.all_to_all(pieces, 'tm', 0, 0, axis_index_groups=groups, tiled=False)  5.26 us
  transfers between devices with their start and end apart: 12, of which 9 were waited for; matrix products, arithmetic and copies ran while one was open for 8% of the time, Pallas kernels for 0%

commit v1 on v0

v1 whole, which is shorter than its diff:
```python
import math

import jax
import jax.numpy as jnp
from jax import lax
from jax.experimental import pallas as pl
from jax.experimental.pallas import tpu as pltpu
from jax.sharding import PartitionSpec as P

ATOMS = 256
CHANNELS = 64
ATOM_LEN = 128
SPARSITY = 0.05
DICT_RATE = 0.5
EPSILON = 1e-06

SCALE = 1.0 / math.sqrt(CHANNELS * ATOM_LEN)
FINE = 16
COARSE = ATOM_LEN // FINE
WIDE = FINE * CHANNELS
HALO = 2 * ATOM_LEN
F32 = jnp.float32
BF16 = jnp.bfloat16
VMEM_LIMIT = 56 * 1024 * 1024


def vmem():
    return pl.BlockSpec(memory_space=pltpu.VMEM)


def smem():
    return pl.BlockSpec(memory_space=pltpu.SMEM)


def kernel_params():
    return pltpu.CompilerParams(vmem_limit_bytes=VMEM_LIMIT)


def shifted(value, axis, steps):
    count = lax.axis_size(axis)
    leading, last = (max(0, -steps), min(count, count - steps))
    return lax.ppermute(value, axis, [(source, source + steps) for source in range(leading, last)])


def swapped(value, bit):
    count = lax.axis_size("tm")
    return lax.ppermute(value, "tm", [(i, i ^ bit) for i in range(count)])


def fill_windows(pairs, windows, rows):
    for step in range(FINE // 2):
        windows[0:rows, step * 128 : (step + 1) * 128] = pairs[
            2 * step : 2 * step + rows, :
        ].astype(BF16)


def adjoint(windows, lags, total, start, rows):
    for coarse in range(COARSE):
        part = jnp.dot(
            windows[start + coarse * FINE : start + coarse * FINE + rows, :],
            lags[coarse * WIDE : (coarse + 1) * WIDE, :],
            preferred_element_type=F32,
        )
        if coarse == 0:
            total[0:rows, :] = part
        else:
            total[0:rows, :] += part


def first_kernel(left, middle, right, lags, gradient, largest, pairs, windows):
    width = middle.shape[1]
    rows = width + 3 * ATOM_LEN
    whole = jnp.concatenate([left[...], middle[...], right[...]], 1)
    whole = -whole
    both = jnp.concatenate([whole, pltpu.roll(whole, whole.shape[1] - 1, 1)], 0)
    pairs[0 : width + 2 * HALO, :] = both.T
    fill_windows(pairs, windows, width + 2 * HALO - FINE)
    adjoint(windows, lags, gradient, 0, rows)
    own = jnp.abs(gradient[HALO : HALO + width, :]) * SCALE
    folded = jnp.max(own.reshape(width // 8, 8, ATOMS), 0)
    largest[...] = jnp.maximum(folded[:, :128], folded[:, 128:])


def forward(codes, lags, wide, spread, folded, start, rows):
    for coarse in range(COARSE):
        low = start - coarse * FINE
        wide[0:rows, coarse * ATOMS : (coarse + 1) * ATOMS] = codes[low : low + rows, :]
    weights = jnp.concatenate(
        [lags[coarse * WIDE : (coarse + 1) * WIDE, :] for coarse in range(COARSE)], 1
    )
    spread[0:rows, :] = lax.dot_general(
        wide[0:rows, :], weights, (((1,), (1,)), ((), ())), preferred_element_type=F32
    )
    keep = rows - FINE
    total = spread[FINE - 2 : FINE - 2 + keep + 2, 0:128]
    for step in range(1, FINE // 2):
        lanes = slice(step * 128, (step + 1) * 128)
        low = FINE - 2 - 2 * step
        total = total + spread[low : low + keep + 2, lanes]
    folded[0 : keep + 2, :] = total
    return folded[2 : keep + 2, 0:64] + folded[1 : keep + 1, 64:128]


def soft(moved, bound):
    return jnp.where(moved > 0, 1.0, -1.0) * jnp.maximum(jnp.abs(moved) - bound, 0.0)


def second_kernel(
    left, middle, right, lags, gradient, peak, step, valid, *rest
):
    outs, (signal, codes, codes_low, pairs, windows, wide, spread, folded) = rest[:-8], rest[-8:]
    width = middle.shape[1]
    step_size = step[0]
    threshold = SPARSITY * jnp.max(peak[...])
    bound = step_size * threshold
    low, high = valid[0], valid[1]
    whole = jnp.concatenate([left[...], middle[...], right[...]], 1)
    signal[...] = whole.T

    def row(start, count):
        return lax.broadcasted_iota(jnp.int32, (count, 1), 0) + start

    rows1 = width + 3 * ATOM_LEN
    moved = -step_size * (gradient[...] * SCALE)
    updated = jnp.where(row(0, rows1) >= low, soft(moved, bound), 0.0)
    codes[...] = updated
    codes_low[...] = updated.astype(BF16)
    rows2 = width + 2 * ATOM_LEN
    model = forward(codes_low, lags, wide, spread, folded, ATOM_LEN - FINE, rows2 + FINE)
    resid = model * SCALE - signal[ATOM_LEN : ATOM_LEN + rows2, :]
    resid = jnp.where(row(ATOM_LEN, rows2) < high, resid, 0.0)
    pairs[0:rows2, 0:64] = resid
    pairs[0 : rows2 - 1, 64:128] = pairs[1:rows2, 0:64]
    fill_windows(pairs, windows, rows2 - FINE)
    rows3 = width + ATOM_LEN
    adjoint(windows, lags, spread.at[:, 0:ATOMS], 0, rows3)
    before = codes[ATOM_LEN : ATOM_LEN + rows3, :]
    moved = before - step_size * (spread[0:rows3, 0:ATOMS] * SCALE)
    updated = jnp.where(row(ATOM_LEN, rows3) >= low, soft(moved, bound), 0.0)
    codes[0:rows3, :] = updated
    codes_low[0:rows3, :] = updated.astype(BF16)
    turned = updated.T
    outs[0][...] = turned[:, ATOM_LEN:]
    sparse = jnp.sum(jnp.abs(codes[ATOM_LEN:rows3, :]))
    model = forward(codes_low, lags, wide, spread, folded, ATOM_LEN - FINE, width + FINE)
    resid = model * SCALE - signal[HALO : HALO + width, :]
    resid_low = resid.T.astype(BF16)
    ahead = turned.astype(BF16)
    loss = 0.5 * jnp.sum(resid * resid) + threshold * sparse
    if len(outs) == 2:
        peers, rows, _ = outs[1].shape
        atoms = rows - CHANNELS
        whole_loss = jnp.full((CHANNELS, ATOM_LEN), loss, F32)
        high_part = whole_loss.astype(BF16)
        rest_loss = whole_loss - high_part.astype(F32)
        middle_part = rest_loss.astype(BF16)
        low_part = (rest_loss - middle_part.astype(F32)).astype(BF16)
        lane = lax.broadcasted_iota(jnp.int32, (CHANNELS, ATOM_LEN), 1)
        tail = jnp.where(
            lane == 0,
            high_part.astype(F32),
            jnp.where(lane == 1, middle_part.astype(F32), low_part.astype(F32)),
        ).astype(BF16)
        for peer in range(peers):
            outs[1][peer, 0:atoms, :] = ahead[peer * atoms : (peer + 1) * atoms, :]
            outs[1][peer, atoms:rows, 0:width] = resid_low
            outs[1][peer, atoms:rows, width:] = tail
    else:
        outs[1][...] = ahead
        outs[2][...] = resid_low
        outs[3][...] = jnp.full((8, 128), loss, F32)


def correlate(codes_of, resid_of, blocks, atoms, width, stack, pairs, windows):
    main = blocks * width
    length = width + ATOM_LEN
    lane = lax.broadcasted_iota(jnp.int32, (atoms, ATOM_LEN), 1)
    extra = [jnp.zeros((atoms, ATOM_LEN), F32) for _ in range(COARSE)]
    windows[main : main + ATOM_LEN, :] = jnp.zeros((ATOM_LEN, WIDE), BF16)
    for block in range(blocks):
        piece = jnp.concatenate(
            [resid_of(block).astype(F32), jnp.zeros((CHANNELS, ATOM_LEN), F32)], 1
        )
        piece = pltpu.roll(piece, FINE, 1)
        both = jnp.concatenate([piece, pltpu.roll(piece, length - 1, 1)], 0)
        slot = pairs.at[block % 2]
        slot[...] = both.T
        for step in range(FINE // 2):
            lanes = slice(step * 128, (step + 1) * 128)
            low = 2 * step
            windows[main + block * FINE : main + (block + 1) * FINE, lanes] = slot[
                low : low + FINE, :
            ].astype(BF16)
            low += FINE
            windows[block * width : (block + 1) * width, lanes] = slot[
                low : low + width, :
            ].astype(BF16)
        held = codes_of(block).astype(F32)
        for coarse in range(COARSE):
            start = ATOM_LEN - coarse * FINE
            turned = pltpu.roll(held, length - start, 1)
            stack[coarse * atoms : (coarse + 1) * atoms, block * width : (block + 1) * width] = (
                turned[:, :width].astype(BF16)
            )
            turned = pltpu.roll(held, (FINE * block - (start - FINE)) % length, 1)[:, :ATOM_LEN]
            inside = (lane >= FINE * block) & (lane < FINE * (block + 1))
            extra[coarse] = jnp.where(inside, turned, extra[coarse])
    for coarse in range(COARSE):
        stack[coarse * atoms : (coarse + 1) * atoms, main : main + ATOM_LEN] = extra[coarse].astype(
            BF16
        )
    return jnp.dot(stack[...], windows[...], preferred_element_type=F32)


def shared_kernel(core, taken, keep, give, stack, pairs, windows, total):
    blocks, rows, length = taken.shape
    atoms = rows - CHANNELS
    width = length - ATOM_LEN
    half = atoms // 2
    total[...] = correlate(
        lambda b: taken[b, 0:atoms, :],
        lambda b: taken[b, atoms:rows, 0:width],
        blocks, atoms, width, stack, pairs, windows,
    )
    mine = core[0] * half
    other = half - mine
    for coarse in range(COARSE):
        rows_of = slice(coarse * half, (coarse + 1) * half)
        keep[rows_of, :] = total[pl.ds(coarse * atoms + mine, half), :]
        give[rows_of, :] = total[pl.ds(coarse * atoms + other, half), :]
    loss = jnp.zeros((16, ATOM_LEN), F32)
    for block in range(blocks):
        loss += taken[block, atoms : atoms + 16, width:].astype(F32)
    lane = lax.broadcasted_iota(jnp.int32, (16, ATOM_LEN), 1)
    loss = jnp.sum(jnp.where(lane < 3, loss, 0.0), 1, keepdims=True)[0:8]
    ending = jnp.broadcast_to(loss, (8, WIDE))
    keep[COARSE * half :, :] = ending
    give[COARSE * half :, :] = ending


def lone_kernel(codes, resid, out, stack, pairs, windows):
    out[...] = correlate(
        lambda b: codes[...], lambda b: resid[...], 1, ATOMS, resid.shape[1], stack, pairs, windows
    )


def last_kernel(inverse, keep, recv, atoms_ref, out, loss_out, total, turned):
    half = atoms_ref.shape[0]
    loss_out[0] = (keep[COARSE * half, 0] + recv[COARSE * half, 0]) * inverse
    for step in range(FINE // 2):
        lanes = slice(step * 128, (step + 1) * 128)
        total[step] = keep[0 : COARSE * half, lanes] + recv[0 : COARSE * half, lanes]
    for pair in range(half // 2):
        for step in range(FINE // 2):
            one = total.at[step][pl.ds(2 * pair, COARSE, stride=half), :]
            two = total.at[step][pl.ds(2 * pair + 1, COARSE, stride=half), :]
            block = turned.at[pair]
            block[pl.ds(2 * step, COARSE, stride=FINE), :] = jnp.concatenate(
                [one[:, 0:64], two[:, 0:64]], 1
            )
            block[pl.ds(2 * step + 1, COARSE, stride=FINE), :] = jnp.concatenate(
                [one[:, 64:128], two[:, 64:128]], 1
            )
    gradient = jnp.concatenate([turned[pair].T for pair in range(half // 2)], 0)
    gradient = gradient.reshape(half, CHANNELS, ATOM_LEN)
    normed = gradient / jnp.sqrt(
        jnp.mean(gradient * gradient, axis=(1, 2), keepdims=True) + EPSILON
    )
    moved = atoms_ref[...].astype(F32) - DICT_RATE * normed
    out[...] = moved / jnp.sqrt(jnp.mean(moved * moved, axis=(1, 2), keepdims=True) + EPSILON)


def body(signal, dictionary, step):
    width = signal.shape[1]
    count = lax.axis_size("tm")
    me = lax.axis_index("tm")
    left = shifted(signal[:, width - HALO :], "tm", 1)
    right = shifted(signal[:, :HALO], "tm", -1)
    lags = jnp.transpose(dictionary, (2, 1, 0)).reshape(ATOM_LEN * CHANNELS, ATOMS)
    rows1 = width + 3 * ATOM_LEN
    span = width + 2 * HALO

    gradient, peak = pl.pallas_call(
        first_kernel,
        out_shape=(
            jax.ShapeDtypeStruct((rows1, ATOMS), F32),
            jax.ShapeDtypeStruct((8, 128), F32),
        ),
        in_specs=[vmem()] * 4,
        out_specs=(vmem(), vmem()),
        scratch_shapes=[pltpu.VMEM((span, 128), F32), pltpu.VMEM((span, WIDE), BF16)],
        compiler_params=kernel_params(),
    )(left, signal, right, lags)

    bit = 1
    while bit < count:
        peak = jnp.maximum(peak, swapped(peak, bit))
        bit *= 2

    valid = jnp.stack(
        [jnp.where(me == 0, HALO, 0), jnp.where(me == count - 1, HALO + width, span)]
    ).astype(jnp.int32)
    owned = ATOMS // count
    peers = count // 2
    shared = owned == 16
    own_atoms = lax.dynamic_slice_in_dim(dictionary, me * owned, owned, 0)
    if shared:
        outs = (jax.ShapeDtypeStruct((peers, 2 * owned + CHANNELS, width + ATOM_LEN), BF16),)
    else:
        outs = (
            jax.ShapeDtypeStruct((ATOMS, width + ATOM_LEN), BF16),
            jax.ShapeDtypeStruct((CHANNELS, width), BF16),
            jax.ShapeDtypeStruct((8, 128), F32),
        )
    codes, *others = pl.pallas_call(
        second_kernel,
        out_shape=(jax.ShapeDtypeStruct((ATOMS, width), F32),) + outs,
        in_specs=[vmem()] * 6 + [smem()] * 2,
        out_specs=(vmem(),) * (1 + len(outs)),
        scratch_shapes=[
            pltpu.VMEM((span, CHANNELS), F32),
            pltpu.VMEM((rows1, ATOMS), F32),
            pltpu.VMEM((rows1, ATOMS), BF16),
            pltpu.VMEM((rows1, 128), F32),
            pltpu.VMEM((rows1, WIDE), BF16),
            pltpu.VMEM((rows1, COARSE * ATOMS), BF16),
            pltpu.VMEM((rows1, WIDE), F32),
            pltpu.VMEM((rows1, 128), F32),
        ],
        compiler_params=kernel_params(),
    )(left, signal, right, lags, gradient, peak, step, valid)

    def correlate_scratch(blocks, atoms):
        return [
            pltpu.VMEM((COARSE * atoms, blocks * width + ATOM_LEN), BF16),
            pltpu.VMEM((2, width + ATOM_LEN, 128), F32),
            pltpu.VMEM((blocks * width + ATOM_LEN, WIDE), BF16),
        ]

    inverse = 1.0 / (CHANNELS * width * count)
    if shared:
        core = me % 2
        groups = [[2 * i + c for i in range(peers)] for c in range(2)]
        taken = lax.all_to_all(others[0], "tm", 0, 0, axis_index_groups=groups, tiled=False)
        half_rows = jax.ShapeDtypeStruct((COARSE * owned + 8, WIDE), F32)
        keep, give = pl.pallas_call(
            shared_kernel,
            out_shape=(half_rows, half_rows),
            in_specs=[smem(), vmem()],
            out_specs=(vmem(), vmem()),
            scratch_shapes=correlate_scratch(peers, 2 * owned)
            + [pltpu.VMEM((COARSE * 2 * owned, WIDE), F32)],
            compiler_params=kernel_params(),
        )(core.reshape(1).astype(jnp.int32), taken)
        recv = swapped(give, 1)
        new_dictionary, loss = pl.pallas_call(
            lambda *refs: last_kernel(inverse, *refs),
            out_shape=(
                jax.ShapeDtypeStruct((owned, CHANNELS, ATOM_LEN), F32),
                jax.ShapeDtypeStruct((1,), F32),
            ),
            in_specs=[vmem()] * 3,
            out_specs=(vmem(), smem()),
            scratch_shapes=[
                pltpu.VMEM((FINE // 2, COARSE * owned, 128), F32),
                pltpu.VMEM((owned // 2, ATOM_LEN, 2 * CHANNELS), F32),
            ],
            compiler_params=kernel_params(),
        )(keep, recv, own_atoms)
        return (codes, new_dictionary, loss)

    ahead, resid, loss = others
    part = pl.pallas_call(
        lone_kernel,
        out_shape=jax.ShapeDtypeStruct((COARSE * ATOMS, WIDE), F32),
        in_specs=[vmem()] * 2,
        out_specs=vmem(),
        scratch_shapes=correlate_scratch(1, ATOMS),
        compiler_params=kernel_params(),
    )(ahead, resid)
    summed = lax.psum_scatter(
        part.reshape(COARSE, ATOMS, WIDE), "tm", scatter_dimension=1, tiled=True
    )
    atom_gradient = (
        summed.reshape(COARSE, owned, FINE, CHANNELS)
        .transpose(1, 3, 0, 2)
        .reshape(owned, CHANNELS, ATOM_LEN)
    )
    normed = atom_gradient / jnp.sqrt(
        jnp.mean(atom_gradient * atom_gradient, axis=(1, 2), keepdims=True) + EPSILON
    )
    moved = own_atoms.astype(F32) - DICT_RATE * normed
    new_dictionary = moved / jnp.sqrt(
        jnp.mean(moved * moved, axis=(1, 2), keepdims=True) + EPSILON
    )
    bit = 1
    while bit < count:
        loss = loss + swapped(loss, bit)
        bit *= 2
    return (codes, new_dictionary, loss[0, :1] * inverse)


def solution(mesh):
    return jax.shard_map(
        body,
        mesh=mesh,
        in_specs=(P(None, ("groups", "tm")), P(), P()),
        out_specs=(P(None, ("groups", "tm")), P(("groups", "tm"), None, None), P("groups")),
        check_vma=False,
    )
```

time: 120 us -> 98.7 us (0.82)
  waiting for transfers between devices: 36.6 us -> 26.6 us
  other arithmetic: 6.01 us -> 1.88 us
  local copies, waits for them, and re-layouts: 15.9 us -> 12.3 us
  starting transfers between devices: 21.9 us -> 20.1 us
  between operations: 3.2 us -> 1.49 us
    ppermute x9 -> x5, waiting for transfers between devices: 15.2 us -> 5.1 us  [swapped(): return lax.ppermute(value, 'tm', [(i, i ^ bit) for i in range(count)])]
    slice x3 -> x0, local copies, waits for them, and re-layouts: 2.12 us -> none  [the longest x2 1.61 us: body(): part = correlate(taken[:, :2 * owned], taken[:, 2 * owned:, :width])]
    concatenate x1 -> x0, other arithmetic: 2 us -> none  [body(): jnp.concatenate([ahead.reshape(8, 2 * owned, width + ATOM_LEN), jnp.broad...]
    ppermute x9 -> x5, starting transfers between devices: 12.9 us -> 11.2 us  [swapped(): return lax.ppermute(value, 'tm', [(i, i ^ bit) for i in range(count)])]
    pallas_call x1 -> x2, Pallas kernels: 9.82 us -> 9.86 us  [the longest x1 6.98 us: body(): pl.pallas_call(shared_kernel, out_shape=(half_rows, half_rows), in_specs=...]
  transfers between devices with their start and end apart: 12 -> 8, of which waited for: 9 -> 6; matrix products, arithmetic and copies ran while one was open for 8% -> 10% of each run, Pallas kernels for 0% -> 0%
where the time goes in v1:
time: 98.7 us; the launch traced here: 98.1 us
  Pallas kernels  35.8 us (36%)
  waiting for transfers between devices  26.6 us (27%)
  starting transfers between devices  20.1 us (20%)
  local copies, waits for them, and re-layouts  12.3 us (12%)
  other arithmetic  1.88 us (2%)
  between operations  1.49 us (2%)
    all_to_all x1, waiting for transfers between devices, body(): lax.all_to_all(others[0], 'tm', 0, 0, axis_index_groups=groups, tiled=False)  21.5 us
    pallas_call x1, Pallas kernels, body(): pl.pallas_call(second_kernel, out_shape=(jax.ShapeDtypeStruct((ATOMS, wid...  18.3 us
    ppermute x5, starting transfers between devices, swapped(): return lax.ppermute(value, 'tm', [(i, i ^ bit) for i in range(count)])  11.2 us
    pallas_call x1, Pallas kernels, body(): pl.pallas_call(first_kernel, out_shape=(jax.ShapeDtypeStruct((rows1, ATOM...  7.65 us
    transpose x1, local copies, waits for them, and re-layouts, body(): jnp.transpose(dictionary, (2, 1, 0)).reshape(ATOM_LEN * CHANNELS, ATOMS)  7.35 us
    pallas_call x1, Pallas kernels, body(): pl.pallas_call(shared_kernel, out_shape=(half_rows, half_rows), in_specs=...  6.98 us
    all_to_all x1, starting transfers between devices, body(): lax.all_to_all(others[0], 'tm', 0, 0, axis_index_groups=groups, tiled=False)  5.26 us
    ppermute x5, waiting for transfers between devices, swapped(): return lax.ppermute(value, 'tm', [(i, i ^ bit) for i in range(count)])  5.1 us
  transfers between devices with their start and end apart: 8, of which 6 were waited for; matrix products, arithmetic and copies ran while one was open for 10% of the time, Pallas kernels for 0%

profile of v1, /device:TPU:0, one launch (start us, length us, event | category | flops | bytes accessed | tf_op | source)
XLA Modules:
  0.0 98.1 jit_solution(11454853635482669782)
XLA Ops:
  0.6 0.9 fusion
  1.5 2.4 %collective-permute-start = (f32[64,256]{1,0:T(8,128)S(1)}, f32[64,256]{1,0:T(8,128)S(1)}, u32[]{:S(2)}, u32[]{:S(2)}) collective-permute-start(f32[64,256]{1,0:T(8,128)S(1)} %get-tuple-element.20), channel_id=1, source_target_pairs={{0,1},{1,2},{2,3},{3,4},{4,5},{5,6},{6,7},{7,8},{8,9},{9,10},{10,1... | collective-permute-start | bytes 196616 | tf_op jit(solution)/shard_map/ppermute | solution.py:42
  3.9 1.3 %collective-permute-start.1 = (f32[64,256]{1,0:T(8,128)S(1)}, f32[64,256]{1,0:T(8,128)S(1)}, u32[]{:S(2)}, u32[]{:S(2)}) collective-permute-start(f32[64,256]{1,0:T(8,128)S(1)} %get-tuple-element.19), channel_id=1, source_target_pairs={{1,0},{2,1},{3,2},{4,3},{5,4},{6,5},{7,6},{8,7},{9,8},{10,9},{11,1... | collective-permute-start | bytes 196616 | tf_op jit(solution)/shard_map/ppermute | solution.py:42
  5.2 7.3 %copy.6 = bf16[128,64,256]{2,1,0:T(8,128)(2,1)} copy(bf16[128,64,256]{0,1,2:T(8,128)(2,1)} %bitcast.7) | data formatting | bytes 8388608 | tf_op jit(solution)/shard_map/transpose | solution.py:279
  12.5 0.0 collective-permute-done.left
  12.5 0.0 copy-start.2
  12.5 0.0 collective-permute-done.1.right
  12.5 0.0 copy-start.3
  12.6 0.6 copy-done.2
  13.2 0.0 copy-done.3
  13.2 7.7 %shard_map.58 = (f32[896,256]{1,0:T(8,128)}, f32[8,128]{1,0:T(8,128)}) custom-call(f32[64,256]{1,0:T(8,128)} %copy-done.2, f32[64,512]{1,0:T(8,128)} %middle.3, f32[64,256]{1,0:T(8,128)} %copy-done.3, bf16[8192,256]{1,0:T(8,128)(2,1)} %bitcast.5), custom_call_target="tpu_custom_call" | custom-call | tf_op jit(solution)/shard_map/pallas_call | solution.py:283
  20.8 3.3 %collective-permute-start.2 = (f32[8,128]{1,0:T(8,128)}, f32[8,128]{1,0:T(8,128)S(1)}, u32[]{:S(2)}, u32[]{:S(2)}) collective-permute-start(f32[8,128]{1,0:T(8,128)} %get-tuple-element.12), channel_id=1, source_target_pairs={{0,1},{1,0},{2,3},{3,2},{4,5},{5,4},{6,7},{7,6},{8,9},{9,8},{10,11... | collective-permute-start | bytes 12296 | tf_op jit(solution)/shard_map/ppermute | solution.py:47
  24.1 1.0 %collective-permute-done.2 = f32[8,128]{1,0:T(8,128)S(1)} collective-permute-done((f32[8,128]{1,0:T(8,128)}, f32[8,128]{1,0:T(8,128)S(1)}, u32[]{:S(2)}, u32[]{:S(2)}) %collective-permute-start.2) | collective-permute-done | bytes 4128 | tf_op jit(solution)/shard_map/ppermute | solution.py:47
  25.1 0.7 max.12
  25.8 2.0 %collective-permute-start.3 = (f32[8,128]{1,0:T(8,128)S(1)}, f32[8,128]{1,0:T(8,128)S(1)}, u32[]{:S(2)}, u32[]{:S(2)}) collective-permute-start(f32[8,128]{1,0:T(8,128)S(1)} %max.12), channel_id=1, source_target_pairs={{0,2},{1,3},{2,0},{3,1},{4,6},{5,7},{6,4},{7,5},{8,10},{9,11},{10,... | collective-permute-start | bytes 12296 | tf_op jit(solution)/shard_map/ppermute | solution.py:47
  27.8 1.6 %collective-permute-done.3 = f32[8,128]{1,0:T(8,128)S(1)} collective-permute-done((f32[8,128]{1,0:T(8,128)S(1)}, f32[8,128]{1,0:T(8,128)S(1)}, u32[]{:S(2)}, u32[]{:S(2)}) %collective-permute-start.3) | collective-permute-done | bytes 4128 | tf_op jit(solution)/shard_map/ppermute | solution.py:47
  29.4 2.9 %collective-permute-start.4 = (f32[8,128]{1,0:T(8,128)S(1)}, f32[8,128]{1,0:T(8,128)S(1)}, u32[]{:S(2)}, u32[]{:S(2)}) collective-permute-start(f32[8,128]{1,0:T(8,128)S(1)} %max.13), channel_id=1, source_target_pairs={{0,4},{1,5},{2,6},{3,7},{4,0},{5,1},{6,2},{7,3},{8,12},{9,13},{10,... | collective-permute-start | bytes 12296 | tf_op jit(solution)/shard_map/ppermute | solution.py:47
  32.3 1.6 %collective-permute-done.4 = f32[8,128]{1,0:T(8,128)S(1)} collective-permute-done((f32[8,128]{1,0:T(8,128)S(1)}, f32[8,128]{1,0:T(8,128)S(1)}, u32[]{:S(2)}, u32[]{:S(2)}) %collective-permute-start.4) | collective-permute-done | bytes 4128 | tf_op jit(solution)/shard_map/ppermute | solution.py:47
  33.9 3.0 %collective-permute-start.5 = (f32[8,128]{1,0:T(8,128)S(1)}, f32[8,128]{1,0:T(8,128)S(1)}, u32[]{:S(2)}, u32[]{:S(2)}) collective-permute-start(f32[8,128]{1,0:T(8,128)S(1)} %max.14), channel_id=1, source_target_pairs={{0,8},{1,9},{2,10},{3,11},{4,12},{5,13},{6,14},{7,15},{8,0},{9,1},... | collective-permute-start | bytes 12296 | tf_op jit(solution)/shard_map/ppermute | solution.py:47
  37.0 0.6 pad_add_fusion.valid
  38.2 0.3 collective-permute-done.5
  38.6 0.6 max.15.peak
  39.1 18.3 %shard_map.59 = (f32[256,512]{1,0:T(8,128)}, bf16[8,96,640]{2,1,0:T(8,128)(2,1)}) custom-call(f32[64,256]{1,0:T(8,128)} %copy-done.2, f32[64,512]{1,0:T(8,128)} %middle.3, f32[64,256]{1,0:T(8,128)} %copy-done.3, bf16[8192,256]{1,0:T(8,128)(2,1)} %bitcast.6, f32[896,256]{1,0:T(8,128)} %get-tuple-element.11.gradient, f32[8,128]{1,0:T(8,128)} %max.15.peak, ...), custom_call_target="tpu_custom_call" | custom-call | tf_op jit(solution)/shard_map/pallas_call | solution.py:315
  57.4 5.3 %all-to-all-start = ((bf16[8,96,640]{2,1,0:T(8,128)(2,1)}), bf16[8,96,640]{2,1,0:T(8,128)(2,1)S(1)}, u32[]{:S(2)}, u32[]{:S(2)}) async-start(bf16[8,96,640]{2,1,0:T(8,128)(2,1)} %get-tuple-element.14), calls=%async_computation | async-start | bytes 1966080 | tf_op jit(solution)/shard_map/all_to_all | solution.py:344
  62.7 21.5 %all-to-all-done.taken = bf16[8,96,640]{2,1,0:T(8,128)(2,1)S(1)} async-done(((bf16[8,96,640]{2,1,0:T(8,128)(2,1)}), bf16[8,96,640]{2,1,0:T(8,128)(2,1)S(1)}, u32[]{:S(2)}, u32[]{:S(2)}) %all-to-all-start) | async-done | bytes 983072 | tf_op jit(solution)/shard_map/all_to_all | solution.py:344
  84.2 0.9 copy-done
  85.1 7.0 %shard_map.60 = (f32[136,1024]{1,0:T(8,128)}, f32[136,1024]{1,0:T(8,128)}) custom-call(s32[1]{0:T(128)} %bitcast.4.core, bf16[8,96,640]{2,1,0:T(8,128)(2,1)} %copy-done), custom_call_target="tpu_custom_call" | custom-call | tf_op jit(solution)/shard_map/pallas_call | solution.py:346
  92.1 0.0 collective-permute-start.6
  92.1 1.7 %constant_dynamic-slice_fusion.refs_2_ = bf16[16,64,128]{2,1,0:T(8,128)(2,1)} fusion(bf16[256,64,128]{2,1,0:T(8,128)(2,1)} %param.4, s32[]{:T(128)S(6)} %select_n.20), kind=kLoop, calls=%fused_computation.1 | loop fusion | bytes 524292 | tf_op jit(solution)/shard_map/dynamic_slice | solution.py:306
  93.8 0.5 collective-permute-done.6.refs_1_
  94.3 0.8 copy-done.1
  95.1 2.9 %shard_map.61 = (f32[16,64,128]{2,1,0:T(8,128)}, f32[1]{0:T(128)}) custom-call(f32[136,1024]{1,0:T(8,128)} %get-tuple-element.15.refs_0_, f32[136,1024]{1,0:T(8,128)} %copy-done.1, bf16[16,64,128]{2,1,0:T(8,128)(2,1)} %constant_dynamic-slice_fusion.refs_2_), custom_call_target="tpu_custom_call" | custom-call | tf_op jit(solution)/shard_map/pallas_call | solution.py:356
  (4 shorter events, 0.0 us)
Async XLA Ops:
  1.5 11.0 %collective-permute-start = (f32[64,256]{1,0:T(8,128)S(1)}, f32[64,256]{1,0:T(8,128)S(1)}, u32[]{:S(2)}, u32[]{:S(2)}) collective-permute-start(f32[64,256]{1,0:T(8,128)S(1)} %get-tuple-element.20), channel_id=1, source_target_pairs={{0,1},{1,2},{2,3},{3,4},{4,5},{5,6},{6,7},{7,8},{8,9},{9,10},{10,1... | collective-permute-start | bytes 196616 | tf_op jit(solution)/shard_map/ppermute | solution.py:42
  3.9 8.7 %collective-permute-start.1 = (f32[64,256]{1,0:T(8,128)S(1)}, f32[64,256]{1,0:T(8,128)S(1)}, u32[]{:S(2)}, u32[]{:S(2)}) collective-permute-start(f32[64,256]{1,0:T(8,128)S(1)} %get-tuple-element.19), channel_id=1, source_target_pairs={{1,0},{2,1},{3,2},{4,3},{5,4},{6,5},{7,6},{8,7},{9,8},{10,9},{11,1... | collective-permute-start | bytes 196616 | tf_op jit(solution)/shard_map/ppermute | solution.py:42
  12.5 0.6 copy-start.2
  12.5 0.6 copy-start.3
  20.8 4.3 %collective-permute-start.2 = (f32[8,128]{1,0:T(8,128)}, f32[8,128]{1,0:T(8,128)S(1)}, u32[]{:S(2)}, u32[]{:S(2)}) collective-permute-start(f32[8,128]{1,0:T(8,128)} %get-tuple-element.12), channel_id=1, source_target_pairs={{0,1},{1,0},{2,3},{3,2},{4,5},{5,4},{6,7},{7,6},{8,9},{9,8},{10,11... | collective-permute-start | bytes 12296 | tf_op jit(solution)/shard_map/ppermute | solution.py:47
  25.8 3.6 %collective-permute-start.3 = (f32[8,128]{1,0:T(8,128)S(1)}, f32[8,128]{1,0:T(8,128)S(1)}, u32[]{:S(2)}, u32[]{:S(2)}) collective-permute-start(f32[8,128]{1,0:T(8,128)S(1)} %max.12), channel_id=1, source_target_pairs={{0,2},{1,3},{2,0},{3,1},{4,6},{5,7},{6,4},{7,5},{8,10},{9,11},{10,... | collective-permute-start | bytes 12296 | tf_op jit(solution)/shard_map/ppermute | solution.py:47
  29.4 4.5 %collective-permute-start.4 = (f32[8,128]{1,0:T(8,128)S(1)}, f32[8,128]{1,0:T(8,128)S(1)}, u32[]{:S(2)}, u32[]{:S(2)}) collective-permute-start(f32[8,128]{1,0:T(8,128)S(1)} %max.13), channel_id=1, source_target_pairs={{0,4},{1,5},{2,6},{3,7},{4,0},{5,1},{6,2},{7,3},{8,12},{9,13},{10,... | collective-permute-start | bytes 12296 | tf_op jit(solution)/shard_map/ppermute | solution.py:47
  33.9 4.6 %collective-permute-start.5 = (f32[8,128]{1,0:T(8,128)S(1)}, f32[8,128]{1,0:T(8,128)S(1)}, u32[]{:S(2)}, u32[]{:S(2)}) collective-permute-start(f32[8,128]{1,0:T(8,128)S(1)} %max.14), channel_id=1, source_target_pairs={{0,8},{1,9},{2,10},{3,11},{4,12},{5,13},{6,14},{7,15},{8,0},{9,1},... | collective-permute-start | bytes 12296 | tf_op jit(solution)/shard_map/ppermute | solution.py:47
  57.4 26.7 %all-to-all-start = ((bf16[8,96,640]{2,1,0:T(8,128)(2,1)}), bf16[8,96,640]{2,1,0:T(8,128)(2,1)S(1)}, u32[]{:S(2)}, u32[]{:S(2)}) async-start(bf16[8,96,640]{2,1,0:T(8,128)(2,1)} %get-tuple-element.14), calls=%async_computation | async-start | bytes 1966080 | tf_op jit(solution)/shard_map/all_to_all | solution.py:344
  84.2 1.0 copy-start
  92.1 2.2 %collective-permute-start.6 = (f32[136,1024]{1,0:T(8,128)}, f32[136,1024]{1,0:T(8,128)S(1)}, u32[]{:S(2)}, u32[]{:S(2)}) collective-permute-start(f32[136,1024]{1,0:T(8,128)} %get-tuple-element.16), channel_id=1, source_target_pairs={{0,1},{1,0},{2,3},{3,2},{4,5},{5,4},{6,7},{7,6},{8,9},{9,8},{10,11... | collective-permute-start | bytes 1671176 | tf_op jit(solution)/shard_map/ppermute | solution.py:47
  94.3 0.8 copy-start.1

commit v2 on v1

--- a/solution.py
+++ b/solution.py
@@ -21,7 +21,7 @@
 HALO = 2 * ATOM_LEN
 F32 = jnp.float32
 BF16 = jnp.bfloat16
-VMEM_LIMIT = 56 * 1024 * 1024
+VMEM_LIMIT = 36 * 1024 * 1024
 
 
 def vmem():
@@ -32,8 +32,30 @@
     return pl.BlockSpec(memory_space=pltpu.SMEM)
 
 
-def kernel_params():
-    return pltpu.CompilerParams(vmem_limit_bytes=VMEM_LIMIT)
+def anywhere():
+    return pl.BlockSpec(memory_space=pl.ANY)
+
+
+def fetch_lags(source, lags, arrived):
+    copies = [
+        pltpu.make_async_copy(
+            source.at[pl.ds(coarse * WIDE, WIDE), :],
+            lags.at[pl.ds(coarse * WIDE, WIDE), :],
+            arrived.at[coarse],
+        )
+        for coarse in range(COARSE)
+    ]
+    for copy in copies:
+        copy.start()
+    return copies
+
+
+def cost(flops, bytes_accessed):
+    return pl.CostEstimate(flops=flops, bytes_accessed=bytes_accessed, transcendentals=0)
+
+
+def kernel_params(limit=VMEM_LIMIT):
+    return pltpu.CompilerParams(vmem_limit_bytes=limit)
 
 
 def shifted(value, axis, steps):
@@ -54,10 +76,15 @@
         ].astype(BF16)
 
 
-def adjoint(windows, lags, total, start, rows):
+def adjoint(windows, lags, total, spans, copies=None):
+    rows = sum(count for _, count in spans)
     for coarse in range(COARSE):
+        if copies is not None:
+            copies[coarse].wait()
+        shift = coarse * FINE
+        taken = [windows[start + shift : start + shift + count, :] for start, count in spans]
         part = jnp.dot(
-            windows[start + coarse * FINE : start + coarse * FINE + rows, :],
+            taken[0] if len(taken) == 1 else jnp.concatenate(taken, 0),
             lags[coarse * WIDE : (coarse + 1) * WIDE, :],
             preferred_element_type=F32,
         )
@@ -67,18 +94,45 @@
             total[0:rows, :] += part
 
 
-def first_kernel(left, middle, right, lags, gradient, largest, pairs, windows):
+def windows_of(whole, pairs, windows):
+    length = whole.shape[1]
+    both = jnp.concatenate([whole, pltpu.roll(whole, length - 1, 1)], 0)
+    pairs[0:length, :] = both.T
+    fill_windows(pairs, windows, length - FINE)
+
+
+def own_kernel(middle, right_any, lags, gradient, largest, right, pairs, windows, sems):
     width = middle.shape[1]
-    rows = width + 3 * ATOM_LEN
-    whole = jnp.concatenate([left[...], middle[...], right[...]], 1)
-    whole = -whole
-    both = jnp.concatenate([whole, pltpu.roll(whole, whole.shape[1] - 1, 1)], 0)
-    pairs[0 : width + 2 * HALO, :] = both.T
-    fill_windows(pairs, windows, width + 2 * HALO - FINE)
-    adjoint(windows, lags, gradient, 0, rows)
-    own = jnp.abs(gradient[HALO : HALO + width, :]) * SCALE
+    near = pltpu.make_async_copy(right_any, right, sems.at[COARSE])
+    near.start()
+    near.wait()
+    whole = jnp.concatenate([middle[...], right[:, 0:ATOM_LEN]], 1)
+    windows_of(-whole, pairs, windows)
+    adjoint(windows, lags, gradient, [(0, width)])
+    own = jnp.abs(gradient[...]) * SCALE
     folded = jnp.max(own.reshape(width // 8, 8, ATOMS), 0)
-    largest[...] = jnp.maximum(folded[:, :128], folded[:, 128:])
+    folded = jnp.maximum(folded[:, :128], folded[:, 128:])
+    for peer in range(largest.shape[0]):
+        largest[peer] = folded
+
+
+def border_kernel(
+    left_any, middle, right_any, lags, gradient, lags_out, left, right, pairs, windows, sems
+):
+    near = [
+        pltpu.make_async_copy(left_any, left, sems.at[COARSE]),
+        pltpu.make_async_copy(right_any, right, sems.at[COARSE + 1]),
+    ]
+    for copy in near:
+        copy.start()
+    copies = fetch_lags(lags, lags_out, sems)
+    for copy in near:
+        copy.wait()
+    whole = jnp.concatenate([left[...], middle[:, 0:ATOM_LEN], right[...]], 1)
+    windows_of(-whole, pairs, windows)
+    adjoint(windows, lags, gradient, [(0, HALO), (HALO + ATOM_LEN, ATOM_LEN)])
+    for copy in copies:
+        copy.wait()
 
 
 def forward(codes, lags, wide, spread, folded, start, rows):
@@ -106,9 +160,19 @@
 
 
 def second_kernel(
-    left, middle, right, lags, gradient, peak, step, valid, *rest
+    left_any, middle, right_any, lags, own_gradient, border, peak, step, valid, *rest
 ):
-    outs, (signal, codes, codes_low, pairs, windows, wide, spread, folded) = rest[:-8], rest[-8:]
+    outs, scratch = rest[:-11], rest[-11:]
+    signal, codes, codes_low, pairs, windows, wide, spread, folded = scratch[:8]
+    left, right, sems = scratch[8:]
+    near = [
+        pltpu.make_async_copy(left_any, left, sems.at[COARSE]),
+        pltpu.make_async_copy(right_any, right, sems.at[COARSE + 1]),
+    ]
+    for copy in near:
+        copy.start()
+    for copy in near:
+        copy.wait()
     width = middle.shape[1]
     step_size = step[0]
     threshold = SPARSITY * jnp.max(peak[...])
@@ -120,11 +184,18 @@
     def row(start, count):
         return lax.broadcasted_iota(jnp.int32, (count, 1), 0) + start
 
-    rows1 = width + 3 * ATOM_LEN
-    moved = -step_size * (gradient[...] * SCALE)
-    updated = jnp.where(row(0, rows1) >= low, soft(moved, bound), 0.0)
-    codes[...] = updated
-    codes_low[...] = updated.astype(BF16)
+    for start, values in (
+        (0, border[0:HALO, :]),
+        (HALO, own_gradient[...]),
+        (HALO + width, border[HALO:, :]),
+    ):
+        count = values.shape[0]
+        moved = -step_size * (values * SCALE)
+        updated = soft(moved, bound)
+        if start == 0:
+            updated = jnp.where(row(0, count) >= low, updated, 0.0)
+        codes[start : start + count, :] = updated
+        codes_low[start : start + count, :] = updated.astype(BF16)
     rows2 = width + 2 * ATOM_LEN
     model = forward(codes_low, lags, wide, spread, folded, ATOM_LEN - FINE, rows2 + FINE)
     resid = model * SCALE - signal[ATOM_LEN : ATOM_LEN + rows2, :]
@@ -133,7 +204,7 @@
     pairs[0 : rows2 - 1, 64:128] = pairs[1:rows2, 0:64]
     fill_windows(pairs, windows, rows2 - FINE)
     rows3 = width + ATOM_LEN
-    adjoint(windows, lags, spread.at[:, 0:ATOMS], 0, rows3)
+    adjoint(windows, lags, spread.at[:, 0:ATOMS], [(0, rows3)])
     before = codes[ATOM_LEN : ATOM_LEN + rows3, :]
     moved = before - step_size * (spread[0:rows3, 0:ATOMS] * SCALE)
     updated = jnp.where(row(ATOM_LEN, rows3) >= low, soft(moved, bound), 0.0)
@@ -212,8 +283,16 @@
     return jnp.dot(stack[...], windows[...], preferred_element_type=F32)
 
 
-def shared_kernel(core, taken, keep, give, stack, pairs, windows, total):
+def shared_kernel(core, taken_any, keep, give, stack, pairs, windows, total, taken, sems):
     blocks, rows, length = taken.shape
+    copies = [
+        pltpu.make_async_copy(taken_any.at[block], taken.at[block], sems.at[block])
+        for block in range(blocks)
+    ]
+    for copy in copies:
+        copy.start()
+    for copy in copies:
+        copy.wait()
     atoms = rows - CHANNELS
     width = length - ATOM_LEN
     half = atoms // 2
@@ -244,7 +323,10 @@
     )
 
 
-def last_kernel(inverse, keep, recv, atoms_ref, out, loss_out, total, turned):
+def last_kernel(inverse, keep, recv_any, atoms_ref, out, loss_out, total, turned, recv, sem):
+    copy = pltpu.make_async_copy(recv_any, recv, sem.at[0])
+    copy.start()
+    copy.wait()
     half = atoms_ref.shape[0]
     loss_out[0] = (keep[COARSE * half, 0] + recv[COARSE * half, 0]) * inverse
     for step in range(FINE // 2):
@@ -280,22 +362,39 @@
     rows1 = width + 3 * ATOM_LEN
     span = width + 2 * HALO
 
+    near_scratch = [pltpu.VMEM((CHANNELS, HALO), F32)]
+    sems = [pltpu.SemaphoreType.DMA((COARSE + 2,))]
+    bordered = width + ATOM_LEN
     gradient, peak = pl.pallas_call(
-        first_kernel,
+        own_kernel,
         out_shape=(
-            jax.ShapeDtypeStruct((rows1, ATOMS), F32),
-            jax.ShapeDtypeStruct((8, 128), F32),
+            jax.ShapeDtypeStruct((width, ATOMS), F32),
+            jax.ShapeDtypeStruct((count, 8, 128), F32),
         ),
-        in_specs=[vmem()] * 4,
+        in_specs=[vmem(), anywhere(), vmem()],
+        out_specs=(vmem(),) * 2,
+        scratch_shapes=near_scratch
+        + [pltpu.VMEM((bordered, 128), F32), pltpu.VMEM((bordered, WIDE), BF16)]
+        + sems,
+        compiler_params=kernel_params(),
+        cost_estimate=cost(2 * width * ATOMS * WIDE * COARSE, 5 << 20),
+    )(signal, right, lags)
+    peak = lax.all_to_all(peak, "tm", 0, 0, tiled=False)
+    span_border = 2 * HALO + ATOM_LEN
+    border, lags = pl.pallas_call(
+        border_kernel,
+        out_shape=(
+            jax.ShapeDtypeStruct((HALO + ATOM_LEN, ATOMS), F32),
+            jax.ShapeDtypeStruct(lags.shape, BF16),
+        ),
+        in_specs=[anywhere(), vmem(), anywhere(), vmem()],
         out_specs=(vmem(), vmem()),
-        scratch_shapes=[pltpu.VMEM((span, 128), F32), pltpu.VMEM((span, WIDE), BF16)],
+        scratch_shapes=near_scratch * 2
+        + [pltpu.VMEM((span_border, 128), F32), pltpu.VMEM((span_border, WIDE), BF16)]
+        + sems,
         compiler_params=kernel_params(),
+        cost_estimate=cost(2 * (HALO + ATOM_LEN) * ATOMS * WIDE * COARSE, 5 << 20),
     )(left, signal, right, lags)
-
-    bit = 1
-    while bit < count:
-        peak = jnp.maximum(peak, swapped(peak, bit))
-        bit *= 2
 
     valid = jnp.stack(
         [jnp.where(me == 0, HALO, 0), jnp.where(me == count - 1, HALO + width, span)]
@@ -315,7 +414,7 @@
     codes, *others = pl.pallas_call(
         second_kernel,
         out_shape=(jax.ShapeDtypeStruct((ATOMS, width), F32),) + outs,
-        in_specs=[vmem()] * 6 + [smem()] * 2,
+        in_specs=[anywhere(), vmem(), anywhere(), vmem()] + [vmem()] * 3 + [smem()] * 2,
         out_specs=(vmem(),) * (1 + len(outs)),
         scratch_shapes=[
             pltpu.VMEM((span, CHANNELS), F32),
@@ -326,9 +425,11 @@
             pltpu.VMEM((rows1, COARSE * ATOMS), BF16),
             pltpu.VMEM((rows1, WIDE), F32),
             pltpu.VMEM((rows1, 128), F32),
-        ],
+        ]
+        + near_scratch * 2
+        + sems,
         compiler_params=kernel_params(),
-    )(left, signal, right, lags, gradient, peak, step, valid)
+    )(left, signal, right, lags, gradient, border, peak, step, valid)
 
     def correlate_scratch(blocks, atoms):
         return [
@@ -346,10 +447,14 @@
         keep, give = pl.pallas_call(
             shared_kernel,
             out_shape=(half_rows, half_rows),
-            in_specs=[smem(), vmem()],
+            in_specs=[smem(), anywhere()],
             out_specs=(vmem(), vmem()),
             scratch_shapes=correlate_scratch(peers, 2 * owned)
-            + [pltpu.VMEM((COARSE * 2 * owned, WIDE), F32)],
+            + [
+                pltpu.VMEM((COARSE * 2 * owned, WIDE), F32),
+                pltpu.VMEM(taken.shape, BF16),
+                pltpu.SemaphoreType.DMA((peers,)),
+            ],
             compiler_params=kernel_params(),
         )(core.reshape(1).astype(jnp.int32), taken)
         recv = swapped(give, 1)
@@ -359,11 +464,13 @@
                 jax.ShapeDtypeStruct((owned, CHANNELS, ATOM_LEN), F32),
                 jax.ShapeDtypeStruct((1,), F32),
             ),
-            in_specs=[vmem()] * 3,
+            in_specs=[vmem(), anywhere(), vmem()],
             out_specs=(vmem(), smem()),
             scratch_shapes=[
                 pltpu.VMEM((FINE // 2, COARSE * owned, 128), F32),
                 pltpu.VMEM((owned // 2, ATOM_LEN, 2 * CHANNELS), F32),
+                pltpu.VMEM(half_rows.shape, F32),
+                pltpu.SemaphoreType.DMA((1,)),
             ],
             compiler_params=kernel_params(),
         )(keep, recv, own_atoms)

time: 98.7 us -> 94.8 us (0.960)
  Pallas kernels: 35.8 us -> 30.2 us
  local copies, waits for them, and re-layouts: 12.3 us -> 17.8 us
  other arithmetic: 1.88 us -> 0.08 us
  starting transfers between devices: 20.1 us -> 18.8 us
    ppermute x5 -> x1, starting transfers between devices: 11.2 us -> 0.07 us  [swapped(): return lax.ppermute(value, 'tm', [(i, i ^ bit) for i in range(count)])]
    all_to_all x0 -> x1, starting transfers between devices: none -> 9.31 us  [body(): peak = lax.all_to_all(peak, 'tm', 0, 0, tiled=False)]
    unnamed x8 -> x10, local copies, waits for them, and re-layouts: 2.39 us -> 8.52 us
    ppermute x5 -> x1, waiting for transfers between devices: 5.1 us -> 0.96 us  [swapped(): return lax.ppermute(value, 'tm', [(i, i ^ bit) for i in range(count)])]
    all_to_all x1, waiting for transfers between devices: 21.5 us -> 24.7 us  [body(): lax.all_to_all(others[0], 'tm', 0, 0, axis_index_groups=groups, tiled=False)]
    pallas_call x1, Pallas kernels: 18.3 us -> 16.5 us  [body(): pl.pallas_call(second_kernel, out_shape=(jax.ShapeDtypeStruct((ATOMS, wid...]
    pallas_call x1 -> x2, Pallas kernels: 7.65 us -> 5.99 us  [the longest x1 3.39 us: body(): pl.pallas_call(own_kernel, out_shape=(jax.ShapeDtypeStruct((width, ATOMS)...]
    max x4 -> x0, other arithmetic: 1.28 us -> none  [body(): peak = jnp.maximum(peak, swapped(peak, bit))]
  transfers between devices with their start and end apart: 8 -> 5, of which waited for: 6 -> 3; matrix products, arithmetic and copies ran while one was open for 10% -> 9% of each run, Pallas kernels for 0% -> 6%
where the time goes in v2:
time: 94.8 us; the launch traced here: 94.2 us
  Pallas kernels  30.2 us (32%)
  waiting for transfers between devices  25.8 us (27%)
  starting transfers between devices  18.8 us (20%)
  local copies, waits for them, and re-layouts  17.8 us (19%)
  between operations  1.59 us (2%)
    all_to_all x1, waiting for transfers between devices, body(): lax.all_to_all(others[0], 'tm', 0, 0, axis_index_groups=groups, tiled=False)  24.7 us
    pallas_call x1, Pallas kernels, body(): pl.pallas_call(second_kernel, out_shape=(jax.ShapeDtypeStruct((ATOMS, wid...  16.5 us
    all_to_all x1, starting transfers between devices, body(): peak = lax.all_to_all(peak, 'tm', 0, 0, tiled=False)  9.31 us
    unnamed x10, local copies, waits for them, and re-layouts  8.52 us
    transpose x1, local copies, waits for them, and re-layouts, body(): jnp.transpose(dictionary, (2, 1, 0)).reshape(ATOM_LEN * CHANNELS, ATOMS)  7.38 us
    pallas_call x1, Pallas kernels, body(): pl.pallas_call(shared_kernel, out_shape=(half_rows, half_rows), in_specs=...  6.07 us
    all_to_all x1, starting transfers between devices, body(): lax.all_to_all(others[0], 'tm', 0, 0, axis_index_groups=groups, tiled=False)  5.8 us
    ppermute x2, starting transfers between devices, shifted(): lax.ppermute(value, axis, [(source, source + steps) for source in range(l...  3.65 us
  transfers between devices with their start and end apart: 5, of which 3 were waited for; matrix products, arithmetic and copies ran while one was open for 9% of the time, Pallas kernels for 6%

profile of v2, /device:TPU:0, one launch (start us, length us, event | category | flops | bytes accessed | tf_op | source)
XLA Modules:
  0.0 94.2 jit_solution(16020529322033627670)
XLA Ops:
  0.6 0.9 fusion
  1.5 2.4 %collective-permute-start = (f32[64,256]{1,0:T(8,128)S(1)}, f32[64,256]{1,0:T(8,128)S(1)}, u32[]{:S(2)}, u32[]{:S(2)}) collective-permute-start(f32[64,256]{1,0:T(8,128)S(1)} %get-tuple-element.24), channel_id=1, source_target_pairs={{0,1},{1,2},{2,3},{3,4},{4,5},{5,6},{6,7},{7,8},{8,9},{9,10},{10,1... | collective-permute-start | bytes 196616 | tf_op jit(solution)/shard_map/ppermute | solution.py:64
  3.9 1.3 %collective-permute-start.1 = (f32[64,256]{1,0:T(8,128)S(1)}, f32[64,256]{1,0:T(8,128)S(1)}, u32[]{:S(2)}, u32[]{:S(2)}) collective-permute-start(f32[64,256]{1,0:T(8,128)S(1)} %get-tuple-element.23), channel_id=1, source_target_pairs={{1,0},{2,1},{3,2},{4,3},{5,4},{6,5},{7,6},{8,7},{9,8},{10,9},{11,1... | collective-permute-start | bytes 196616 | tf_op jit(solution)/shard_map/ppermute | solution.py:64
  5.2 0.0 copy-start.4
  5.2 7.4 %copy.6 = bf16[128,64,256]{2,1,0:T(8,128)(2,1)} copy(bf16[128,64,256]{0,1,2:T(8,128)(2,1)} %bitcast.7) | data formatting | bytes 8388608 | tf_op jit(solution)/shard_map/transpose | solution.py:361
  13.2 0.1 pad_add_fusion.valid
  13.3 0.0 collective-permute-done.1.right_any
  13.3 0.0 copy-done.4
  13.3 0.0 copy-start
  13.3 2.2 %copy-done = bf16[128,64,256]{2,1,0:T(8,128)(2,1)S(1)} copy-done((bf16[128,64,256]{2,1,0:T(8,128)(2,1)S(1)}, bf16[128,64,256]{2,1,0:T(8,128)(2,1)}, u32[]{:S(2)}) %copy-start) | copy-done | bytes 4194328
  15.5 3.4 %shard_map.59 = (f32[512,256]{1,0:T(8,128)S(1)}, f32[16,8,128]{2,1,0:T(8,128)}) custom-call(f32[64,512]{1,0:T(8,128)S(1)} %copy-done.4, f32[64,256]{1,0:T(8,128)S(1)} %collective-permute-done.1.right_any, bf16[8192,256]{1,0:T(8,128)(2,1)S(1)} %bitcast.5), custom_call_target="tpu_custom_call" | custom-call | flops 2147483648 | bytes 5242880 | tf_op jit(solution)/shard_map/pallas_call | solution.py:368
  18.9 9.3 %all-to-all-start = ((f32[16,8,128]{2,1,0:T(8,128)}), f32[16,8,128]{2,1,0:T(8,128)S(1)}, u32[]{:S(2)}, u32[]{:S(2)}) async-start(f32[16,8,128]{2,1,0:T(8,128)} %get-tuple-element.16), calls=%async_computation | async-start | bytes 131072 | tf_op jit(solution)/shard_map/all_to_all | solution.py:382
  28.2 0.0 collective-permute-done.left_any
  28.2 0.0 copy-start.1
  28.3 2.2 %copy-done.1 = bf16[128,64,256]{2,1,0:T(8,128)(2,1)S(1)} copy-done((bf16[128,64,256]{2,1,0:T(8,128)(2,1)S(1)}, bf16[128,64,256]{2,1,0:T(8,128)(2,1)}, u32[]{:S(2)}) %copy-start.1) | copy-done | bytes 4194328
  30.4 2.6 %shard_map.58 = (f32[384,256]{1,0:T(8,128)S(1)}, bf16[8192,256]{1,0:T(8,128)(2,1)S(1)}) custom-call(f32[64,256]{1,0:T(8,128)S(1)} %collective-permute-done.left_any, f32[64,512]{1,0:T(8,128)S(1)} %copy-done.4, f32[64,256]{1,0:T(8,128)S(1)} %collective-permute-done.1.right_any, bf16[8192,256]{1,0:T(8,128)(2,1)S(1)} %bitcast.6), custom_call_target="tpu_custom_call" | custom-call | flops 1610612736 | bytes 5242880 | tf_op jit(solution)/shard_map/pallas_call | solution.py:384
  33.0 0.0 copy-start.2
  33.0 2.0 %copy-done.2 = bf16[8192,256]{1,0:T(8,128)(2,1)} copy-done((bf16[8192,256]{1,0:T(8,128)(2,1)}, bf16[8192,256]{1,0:T(8,128)(2,1)S(1)}, u32[]{:S(2)}) %copy-start.2) | copy-done | bytes 4194328
  35.0 0.1 all-to-all-done.peak
  35.1 0.0 copy-start.3
  35.1 2.2 %copy-done.3 = bf16[8192,256]{1,0:T(8,128)(2,1)S(1)} copy-done((bf16[8192,256]{1,0:T(8,128)(2,1)S(1)}, bf16[8192,256]{1,0:T(8,128)(2,1)}, u32[]{:S(2)}) %copy-start.3) | copy-done | bytes 4194328
  37.3 16.5 %shard_map.60 = (f32[256,512]{1,0:T(8,128)}, bf16[8,96,640]{2,1,0:T(8,128)(2,1)}) custom-call(f32[64,256]{1,0:T(8,128)S(1)} %collective-permute-done.left_any, f32[64,512]{1,0:T(8,128)S(1)} %copy-done.4, f32[64,256]{1,0:T(8,128)S(1)} %collective-permute-done.1.right_any, bf16[8192,256]{1,0:T(8,128)(2,1)S(1)} %copy-done.3, ...), custom_call_target="tpu_custom_call" | custom-call | tf_op jit(solution)/shard_map/pallas_call | solution.py:414
  53.8 5.8 %all-to-all-start.1 = ((bf16[8,96,640]{2,1,0:T(8,128)(2,1)}), bf16[8,96,640]{2,1,0:T(8,128)(2,1)S(1)}, u32[]{:S(2)}, u32[]{:S(2)}) async-start(bf16[8,96,640]{2,1,0:T(8,128)(2,1)} %get-tuple-element.18), calls=%async_computation.1 | async-start | bytes 1966080 | tf_op jit(solution)/shard_map/all_to_all | solution.py:445
  59.6 24.7 %all-to-all-done.1.taken_any = bf16[8,96,640]{2,1,0:T(8,128)(2,1)S(1)} async-done(((bf16[8,96,640]{2,1,0:T(8,128)(2,1)}), bf16[8,96,640]{2,1,0:T(8,128)(2,1)S(1)}, u32[]{:S(2)}, u32[]{:S(2)}) %all-to-all-start.1) | async-done | bytes 983072 | tf_op jit(solution)/shard_map/all_to_all | solution.py:445
  84.3 6.1 %shard_map.61 = (f32[136,1024]{1,0:T(8,128)S(1)}, f32[136,1024]{1,0:T(8,128)S(1)}) custom-call(s32[1]{0:T(128)} %bitcast.4.core, bf16[8,96,640]{2,1,0:T(8,128)(2,1)S(1)} %all-to-all-done.1.taken_any), custom_call_target="tpu_custom_call" | custom-call | tf_op jit(solution)/shard_map/pallas_call | solution.py:447
  90.3 0.1 collective-permute-start.2
  90.4 1.0 %constant_dynamic-slice_fusion.refs_2_ = bf16[16,64,128]{2,1,0:T(8,128)(2,1)S(1)} fusion(bf16[256,64,128]{2,1,0:T(8,128)(2,1)} %param.4, s32[]{:T(128)S(6)} %select_n.20), kind=kLoop, calls=%fused_computation.1 | loop fusion | bytes 524292 | tf_op jit(solution)/shard_map/dynamic_slice | solution.py:405
  91.4 1.0 %collective-permute-done.2.refs_1_ = f32[136,1024]{1,0:T(8,128)S(1)} collective-permute-done((f32[136,1024]{1,0:T(8,128)S(1)}, f32[136,1024]{1,0:T(8,128)S(1)}, u32[]{:S(2)}, u32[]{:S(2)}) %collective-permute-start.2) | collective-permute-done | bytes 557088 | tf_op jit(solution)/shard_map/ppermute | solution.py:69
  92.4 1.7 %shard_map.62 = (f32[16,64,128]{2,1,0:T(8,128)}, f32[1]{0:T(128)}) custom-call(f32[136,1024]{1,0:T(8,128)S(1)} %get-tuple-element.19.refs_0_, f32[136,1024]{1,0:T(8,128)S(1)} %collective-permute-done.2.refs_1_, bf16[16,64,128]{2,1,0:T(8,128)(2,1)S(1)} %constant_dynamic-slice_fusion.refs_2_), custom_call_target="tpu_custom_call" | custom-call | tf_op jit(solution)/shard_map/pallas_call | solution.py:461
Async XLA Ops:
  1.5 26.7 %collective-permute-start = (f32[64,256]{1,0:T(8,128)S(1)}, f32[64,256]{1,0:T(8,128)S(1)}, u32[]{:S(2)}, u32[]{:S(2)}) collective-permute-start(f32[64,256]{1,0:T(8,128)S(1)} %get-tuple-element.24), channel_id=1, source_target_pairs={{0,1},{1,2},{2,3},{3,4},{4,5},{5,6},{6,7},{7,8},{8,9},{9,10},{10,1... | collective-permute-start | bytes 196616 | tf_op jit(solution)/shard_map/ppermute | solution.py:64
  3.9 9.4 %collective-permute-start.1 = (f32[64,256]{1,0:T(8,128)S(1)}, f32[64,256]{1,0:T(8,128)S(1)}, u32[]{:S(2)}, u32[]{:S(2)}) collective-permute-start(f32[64,256]{1,0:T(8,128)S(1)} %get-tuple-element.23), channel_id=1, source_target_pairs={{1,0},{2,1},{3,2},{4,3},{5,4},{6,5},{7,6},{8,7},{9,8},{10,9},{11,1... | collective-permute-start | bytes 196616 | tf_op jit(solution)/shard_map/ppermute | solution.py:64
  5.2 8.1 %copy-start.4 = (f32[64,512]{1,0:T(8,128)S(1)}, f32[64,512]{1,0:T(8,128)}, u32[]{:S(2)}) copy-start(f32[64,512]{1,0:T(8,128)} %middle.5) | copy-start | bytes 393220
  13.3 2.2 %copy-start = (bf16[128,64,256]{2,1,0:T(8,128)(2,1)S(1)}, bf16[128,64,256]{2,1,0:T(8,128)(2,1)}, u32[]{:S(2)}) copy-start(bf16[128,64,256]{2,1,0:T(8,128)(2,1)} %copy.6) | copy-start | bytes 12582916
  18.9 16.2 %all-to-all-start = ((f32[16,8,128]{2,1,0:T(8,128)}), f32[16,8,128]{2,1,0:T(8,128)S(1)}, u32[]{:S(2)}, u32[]{:S(2)}) async-start(f32[16,8,128]{2,1,0:T(8,128)} %get-tuple-element.16), calls=%async_computation | async-start | bytes 131072 | tf_op jit(solution)/shard_map/all_to_all | solution.py:382
  28.2 2.2 %copy-start.1 = (bf16[128,64,256]{2,1,0:T(8,128)(2,1)S(1)}, bf16[128,64,256]{2,1,0:T(8,128)(2,1)}, u32[]{:S(2)}) copy-start(bf16[128,64,256]{2,1,0:T(8,128)(2,1)} %copy.6) | copy-start | bytes 12582916
  33.0 2.0 %copy-start.2 = (bf16[8192,256]{1,0:T(8,128)(2,1)}, bf16[8192,256]{1,0:T(8,128)(2,1)S(1)}, u32[]{:S(2)}) copy-start(bf16[8192,256]{1,0:T(8,128)(2,1)S(1)} %get-tuple-element.13.lags) | copy-start | bytes 12582916
  35.1 2.2 %copy-start.3 = (bf16[8192,256]{1,0:T(8,128)(2,1)S(1)}, bf16[8192,256]{1,0:T(8,128)(2,1)}, u32[]{:S(2)}) copy-start(bf16[8192,256]{1,0:T(8,128)(2,1)} %copy-done.2) | copy-start | bytes 12582916
  53.8 30.5 %all-to-all-start.1 = ((bf16[8,96,640]{2,1,0:T(8,128)(2,1)}), bf16[8,96,640]{2,1,0:T(8,128)(2,1)S(1)}, u32[]{:S(2)}, u32[]{:S(2)}) async-start(bf16[8,96,640]{2,1,0:T(8,128)(2,1)} %get-tuple-element.18), calls=%async_computation.1 | async-start | bytes 1966080 | tf_op jit(solution)/shard_map/all_to_all | solution.py:445
  90.3 2.0 %collective-permute-start.2 = (f32[136,1024]{1,0:T(8,128)S(1)}, f32[136,1024]{1,0:T(8,128)S(1)}, u32[]{:S(2)}, u32[]{:S(2)}) collective-permute-start(f32[136,1024]{1,0:T(8,128)S(1)} %get-tuple-element.20), channel_id=1, source_target_pairs={{0,1},{1,0},{2,3},{3,2},{4,5},{5,4},{6,7},{7,6},{8,9},{9,8},{10,11... | collective-permute-start | bytes 1671176 | tf_op jit(solution)/shard_map/ppermute | solution.py:69

commit v3 on v2

--- a/solution.py
+++ b/solution.py
@@ -21,6 +21,7 @@
 HALO = 2 * ATOM_LEN
 F32 = jnp.float32
 BF16 = jnp.bfloat16
+PEERS = 8
 VMEM_LIMIT = 36 * 1024 * 1024
 
 
@@ -162,7 +163,7 @@
 def second_kernel(
     left_any, middle, right_any, lags, own_gradient, border, peak, step, valid, *rest
 ):
-    outs, scratch = rest[:-11], rest[-11:]
+    outs, scratch, kept = rest[:-12], rest[-12:-1], rest[-1]
     signal, codes, codes_low, pairs, windows, wide, spread, folded = scratch[:8]
     left, right, sems = scratch[8:]
     near = [
@@ -218,24 +219,33 @@
     resid_low = resid.T.astype(BF16)
     ahead = turned.astype(BF16)
     loss = 0.5 * jnp.sum(resid * resid) + threshold * sparse
-    if len(outs) == 2:
-        peers, rows, _ = outs[1].shape
-        atoms = rows - CHANNELS
-        whole_loss = jnp.full((CHANNELS, ATOM_LEN), loss, F32)
+    if len(outs) == 1 + PEERS:
+        atoms = ATOMS // PEERS
+        whole_loss = jnp.full((16, ATOM_LEN), loss, F32)
         high_part = whole_loss.astype(BF16)
         rest_loss = whole_loss - high_part.astype(F32)
         middle_part = rest_loss.astype(BF16)
         low_part = (rest_loss - middle_part.astype(F32)).astype(BF16)
-        lane = lax.broadcasted_iota(jnp.int32, (CHANNELS, ATOM_LEN), 1)
+        lane = lax.broadcasted_iota(jnp.int32, (16, ATOM_LEN), 1)
         tail = jnp.where(
             lane == 0,
             high_part.astype(F32),
             jnp.where(lane == 1, middle_part.astype(F32), low_part.astype(F32)),
         ).astype(BF16)
-        for peer in range(peers):
-            outs[1][peer, 0:atoms, :] = ahead[peer * atoms : (peer + 1) * atoms, :]
-            outs[1][peer, atoms:rows, 0:width] = resid_low
-            outs[1][peer, atoms:rows, width:] = tail
+        kept[...] = ahead
+        for turn in range(PEERS):
+            first = pl.multiple_of(valid[2 + turn] * atoms, atoms)
+            piece = outs[1 + turn]
+            piece[0:atoms, :] = kept[pl.ds(first, atoms), ATOM_LEN:]
+            piece[atoms : atoms + CHANNELS, :] = resid_low
+            for part in range(atoms // 16):
+                piece[atoms + CHANNELS :, part * ATOM_LEN : (part + 1) * ATOM_LEN] = kept[
+                    pl.ds(pl.multiple_of(first + part * 16, 16), 16), 0:ATOM_LEN
+                ]
+            piece[atoms + CHANNELS :, HALO : HALO + ATOM_LEN] = tail
+            piece[atoms + CHANNELS :, HALO + ATOM_LEN :] = jnp.zeros(
+                (16, width - HALO - ATOM_LEN), BF16
+            )
     else:
         outs[1][...] = ahead
         outs[2][...] = resid_low
@@ -283,36 +293,55 @@
     return jnp.dot(stack[...], windows[...], preferred_element_type=F32)
 
 
-def shared_kernel(core, taken_any, keep, give, stack, pairs, windows, total, taken, sems):
-    blocks, rows, length = taken.shape
-    copies = [
-        pltpu.make_async_copy(taken_any.at[block], taken.at[block], sems.at[block])
-        for block in range(blocks)
-    ]
-    for copy in copies:
-        copy.start()
-    for copy in copies:
-        copy.wait()
-    atoms = rows - CHANNELS
-    width = length - ATOM_LEN
+def shared_part(pieces, stack, pairs, windows):
+    rows, width = pieces[0].shape
+    atoms = rows - CHANNELS - 16
+
+    def codes_of(block):
+        before = [
+            pieces[block][atoms + CHANNELS :, part * ATOM_LEN : (part + 1) * ATOM_LEN]
+            for part in range(atoms // 16)
+        ]
+        return jnp.concatenate(
+            [jnp.concatenate(before, 0).astype(F32), pieces[block][0:atoms, :].astype(F32)], 1
+        )
+
+    def resid_of(block):
+        return pieces[block][atoms : atoms + CHANNELS, :]
+
+    loss = jnp.zeros((16, ATOM_LEN), F32)
+    for piece in pieces:
+        loss += piece[atoms + CHANNELS :, HALO : HALO + ATOM_LEN].astype(F32)
+    lane = lax.broadcasted_iota(jnp.int32, (16, ATOM_LEN), 1)
+    loss = jnp.sum(jnp.where(lane < 3, loss, 0.0), 1, keepdims=True)[0:8]
+    total = correlate(
+        codes_of, resid_of, len(pieces), atoms, width, stack, pairs, windows
+    )
+    return total, jnp.broadcast_to(loss, (8, WIDE))
+
+
+def shared_first(*refs):
+    pieces, (out, stack, pairs, windows) = refs[: PEERS // 2], refs[PEERS // 2 :]
+    total, loss = shared_part(pieces, stack, pairs, windows)
+    rows = total.shape[0]
+    out[0:rows, :] = total
+    out[rows:, :] = loss
+
+
+def shared_second(core, before, *refs):
+    pieces, (keep, give, stack, pairs, windows, total) = refs[: PEERS // 2], refs[PEERS // 2 :]
+    sums, loss = shared_part(pieces, stack, pairs, windows)
+    rows = total.shape[0]
+    atoms = rows // COARSE
+    total[...] = sums + before[0:rows, :]
     half = atoms // 2
-    total[...] = correlate(
-        lambda b: taken[b, 0:atoms, :],
-        lambda b: taken[b, atoms:rows, 0:width],
-        blocks, atoms, width, stack, pairs, windows,
-    )
     mine = core[0] * half
     other = half - mine
     for coarse in range(COARSE):
         rows_of = slice(coarse * half, (coarse + 1) * half)
         keep[rows_of, :] = total[pl.ds(coarse * atoms + mine, half), :]
         give[rows_of, :] = total[pl.ds(coarse * atoms + other, half), :]
-    loss = jnp.zeros((16, ATOM_LEN), F32)
-    for block in range(blocks):
-        loss += taken[block, atoms : atoms + 16, width:].astype(F32)
-    lane = lax.broadcasted_iota(jnp.int32, (16, ATOM_LEN), 1)
-    loss = jnp.sum(jnp.where(lane < 3, loss, 0.0), 1, keepdims=True)[0:8]
-    ending = jnp.broadcast_to(loss, (8, WIDE))
+    ending = loss + before[rows:, :]
     keep[COARSE * half :, :] = ending
     give[COARSE * half :, :] = ending
 
@@ -398,13 +427,14 @@
 
     valid = jnp.stack(
         [jnp.where(me == 0, HALO, 0), jnp.where(me == count - 1, HALO + width, span)]
+        + [(me // 2) ^ turn for turn in range(PEERS)]
     ).astype(jnp.int32)
     owned = ATOMS // count
-    peers = count // 2
-    shared = owned == 16
+    shared = count == 2 * PEERS
     own_atoms = lax.dynamic_slice_in_dim(dictionary, me * owned, owned, 0)
     if shared:
-        outs = (jax.ShapeDtypeStruct((peers, 2 * owned + CHANNELS, width + ATOM_LEN), BF16),)
+        rows = ATOMS // PEERS + CHANNELS + 16
+        outs = (jax.ShapeDtypeStruct((rows, width), BF16),) * PEERS
     else:
         outs = (
             jax.ShapeDtypeStruct((ATOMS, width + ATOM_LEN), BF16),
@@ -427,7 +457,8 @@
             pltpu.VMEM((rows1, 128), F32),
         ]
         + near_scratch * 2
-        + sems,
+        + sems
+        + [pltpu.VMEM((ATOMS, width + ATOM_LEN), BF16)],
         compiler_params=kernel_params(),
     )(left, signal, right, lags, gradient, border, peak, step, valid)
 
@@ -441,22 +472,30 @@
     inverse = 1.0 / (CHANNELS * width * count)
     if shared:
         core = me % 2
-        groups = [[2 * i + c for i in range(peers)] for c in range(2)]
-        taken = lax.all_to_all(others[0], "tm", 0, 0, axis_index_groups=groups, tiled=False)
+        pieces = list(others)
+        for turn in (4, 5, 6, 7, 2, 3, 1):
+            pieces[turn] = swapped(pieces[turn], 2 * turn)
         half_rows = jax.ShapeDtypeStruct((COARSE * owned + 8, WIDE), F32)
+        blocks = PEERS // 2
+        before = pl.pallas_call(
+            shared_first,
+            out_shape=jax.ShapeDtypeStruct((COARSE * 2 * owned + 8, WIDE), F32),
+            in_specs=[vmem()] * blocks,
+            out_specs=vmem(),
+            scratch_shapes=correlate_scratch(blocks, 2 * owned),
+            compiler_params=kernel_params(),
+            cost_estimate=cost(2 * COARSE * 2 * owned * blocks * width * WIDE, 2 << 20),
+        )(*pieces[:blocks])
         keep, give = pl.pallas_call(
-            shared_kernel,
+            shared_second,
             out_shape=(half_rows, half_rows),
-            in_specs=[smem(), anywhere()],
+            in_specs=[smem(), vmem()] + [vmem()] * blocks,
             out_specs=(vmem(), vmem()),
-            scratch_shapes=correlate_scratch(peers, 2 * owned)
-            + [
-                pltpu.VMEM((COARSE * 2 * owned, WIDE), F32),
-                pltpu.VMEM(taken.shape, BF16),
-                pltpu.SemaphoreType.DMA((peers,)),
-            ],
+            scratch_shapes=correlate_scratch(blocks, 2 * owned)
+            + [pltpu.VMEM((COARSE * 2 * owned, WIDE), F32)],
             compiler_params=kernel_params(),
-        )(core.reshape(1).astype(jnp.int32), taken)
+            cost_estimate=cost(2 * COARSE * 2 * owned * blocks * width * WIDE, 2 << 20),
+        )(core.reshape(1).astype(jnp.int32), before, *pieces[blocks:])
         recv = swapped(give, 1)
         new_dictionary, loss = pl.pallas_call(
             lambda *refs: last_kernel(inverse, *refs),

time: 94.8 us -> 86 us (0.907)
  the two profiles are of different devices: /device:TPU:0 before, /device:TPU:19 now
where the time goes in v3:
time: 86 us; the launch traced here: 85.5 us
  Pallas kernels  29.3 us (34%)
  starting transfers between devices  20.5 us (24%)
  local copies, waits for them, and re-layouts  17.9 us (21%)
  waiting for transfers between devices  16.3 us (19%)
  between operations  1.61 us (2%)
    pallas_call x1, Pallas kernels, body(): pl.pallas_call(second_kernel, out_shape=(jax.ShapeDtypeStruct((ATOMS, wid...  16.3 us
    ppermute x8, waiting for transfers between devices, swapped(): return lax.ppermute(value, 'tm', [(i, i ^ bit) for i in range(count)])  16.3 us
    ppermute x8, starting transfers between devices, swapped(): return lax.ppermute(value, 'tm', [(i, i ^ bit) for i in range(count)])  9.07 us
    unnamed x10, local copies, waits for them, and re-layouts  8.49 us
    transpose x1, local copies, waits for them, and re-layouts, body(): jnp.transpose(dictionary, (2, 1, 0)).reshape(ATOM_LEN * CHANNELS, ATOMS)  7.43 us
    all_to_all x1, starting transfers between devices, body(): peak = lax.all_to_all(peak, 'tm', 0, 0, tiled=False)  5.77 us
    ppermute x2, starting transfers between devices, shifted(): lax.ppermute(value, axis, [(source, source + steps) for source in range(l...  5.63 us
    pallas_call x1, Pallas kernels, body(): pl.pallas_call(own_kernel, out_shape=(jax.ShapeDtypeStruct((width, ATOMS)...  3.38 us
  transfers between devices with their start and end apart: 11, of which 5 were waited for; matrix products, arithmetic and copies ran while one was open for 10% of the time, Pallas kernels for 10%

profile of v3, /device:TPU:19, one launch (start us, length us, event | category | flops | bytes accessed | tf_op | source)
XLA Modules:
  0.0 85.5 jit_solution(15368525193762067128)
XLA Ops:
  0.6 0.9 %fusion = (f32[64,256]{1,0:T(8,128)S(1)}, f32[64,256]{1,0:T(8,128)S(1)}) fusion(f32[64,512]{1,0:T(8,128)} %middle.5), kind=kLoop, calls=%fused_computation.1 | loop fusion | bytes 262144 | tf_op jit(solution)/shard_map/slice | solution.py:389
  1.5 2.6 %collective-permute-start.1 = (f32[64,256]{1,0:T(8,128)S(1)}, f32[64,256]{1,0:T(8,128)S(1)}, u32[]{:S(2)}, u32[]{:S(2)}) collective-permute-start(f32[64,256]{1,0:T(8,128)S(1)} %get-tuple-element.37), channel_id=1, source_target_pairs={{1,0},{2,1},{3,2},{4,3},{5,4},{6,5},{7,6},{8,7},{9,8},{10,9},{11,1... | collective-permute-start | bytes 196616 | tf_op jit(solution)/shard_map/ppermute | solution.py:65
  4.1 3.0 %collective-permute-start = (f32[64,256]{1,0:T(8,128)S(1)}, f32[64,256]{1,0:T(8,128)S(1)}, u32[]{:S(2)}, u32[]{:S(2)}) collective-permute-start(f32[64,256]{1,0:T(8,128)S(1)} %get-tuple-element.38), channel_id=1, source_target_pairs={{0,1},{1,2},{2,3},{3,4},{4,5},{5,6},{6,7},{7,8},{8,9},{9,10},{10,1... | collective-permute-start | bytes 196616 | tf_op jit(solution)/shard_map/ppermute | solution.py:65
  7.2 0.0 copy-start.4
  7.2 7.4 %copy.6 = bf16[128,64,256]{2,1,0:T(8,128)(2,1)} copy(bf16[128,64,256]{0,1,2:T(8,128)(2,1)} %bitcast.15) | data formatting | bytes 8388608 | tf_op jit(solution)/shard_map/transpose | solution.py:390
  15.3 0.1 stack.43.valid
  15.4 0.0 collective-permute-done.1.right_any
  15.4 2.2 %copy-done = bf16[128,64,256]{2,1,0:T(8,128)(2,1)S(1)} copy-done((bf16[128,64,256]{2,1,0:T(8,128)(2,1)S(1)}, bf16[128,64,256]{2,1,0:T(8,128)(2,1)}, u32[]{:S(2)}) %copy-start) | copy-done | bytes 4194328
  17.6 3.4 %shard_map.59 = (f32[512,256]{1,0:T(8,128)S(1)}, f32[16,8,128]{2,1,0:T(8,128)}) custom-call(f32[64,512]{1,0:T(8,128)S(1)} %copy-done.4, f32[64,256]{1,0:T(8,128)S(1)} %collective-permute-done.1.right_any, bf16[8192,256]{1,0:T(8,128)(2,1)S(1)} %bitcast.13), custom_call_target="tpu_custom_call" | custom-call | flops 2147483648 | bytes 5242880 | tf_op jit(solution)/shard_map/pallas_call | solution.py:397
  21.0 5.8 %all-to-all-start = ((f32[16,8,128]{2,1,0:T(8,128)}), f32[16,8,128]{2,1,0:T(8,128)S(1)}, u32[]{:S(2)}, u32[]{:S(2)}) async-start(f32[16,8,128]{2,1,0:T(8,128)} %get-tuple-element.23), calls=%async_computation | async-start | bytes 131072 | tf_op jit(solution)/shard_map/all_to_all | solution.py:411
  26.8 2.2 %copy-done.1 = bf16[128,64,256]{2,1,0:T(8,128)(2,1)S(1)} copy-done((bf16[128,64,256]{2,1,0:T(8,128)(2,1)S(1)}, bf16[128,64,256]{2,1,0:T(8,128)(2,1)}, u32[]{:S(2)}) %copy-start.1) | copy-done | bytes 4194328
  28.9 2.6 %shard_map.58 = (f32[384,256]{1,0:T(8,128)S(1)}, bf16[8192,256]{1,0:T(8,128)(2,1)S(1)}) custom-call(f32[64,256]{1,0:T(8,128)S(1)} %collective-permute-done.left_any, f32[64,512]{1,0:T(8,128)S(1)} %copy-done.4, f32[64,256]{1,0:T(8,128)S(1)} %collective-permute-done.1.right_any, bf16[8192,256]{1,0:T(8,128)(2,1)S(1)} %bitcast.14), custom_call_target="tpu_custom_call" | custom-call | flops 1610612736 | bytes 5242880 | tf_op jit(solution)/shard_map/pallas_call | solution.py:413
  31.6 1.9 %copy-done.2 = bf16[8192,256]{1,0:T(8,128)(2,1)} copy-done((bf16[8192,256]{1,0:T(8,128)(2,1)}, bf16[8192,256]{1,0:T(8,128)(2,1)S(1)}, u32[]{:S(2)}) %copy-start.2) | copy-done | bytes 4194328
  33.5 2.2 %copy-done.3 = bf16[8192,256]{1,0:T(8,128)(2,1)S(1)} copy-done((bf16[8192,256]{1,0:T(8,128)(2,1)S(1)}, bf16[8192,256]{1,0:T(8,128)(2,1)}, u32[]{:S(2)}) %copy-start.3) | copy-done | bytes 4194328
  35.7 16.3 %shard_map.60 = (f32[256,512]{1,0:T(8,128)}, bf16[112,512]{1,0:T(8,128)(2,1)S(1)}, bf16[112,512]{1,0:T(8,128)(2,1)S(1)}, bf16[112,512]{1,0:T(8,128)(2,1)S(1)}, b...) custom-call(f32[64,256]{1,0:T(8,128)S(1)} %collective-permute-done.l, ...), custom_call_target="tpu_custom_call" | custom-call | tf_op jit(solution)/shard_map/pallas_call | solution.py:444
  52.0 1.2 %collective-permute-start.2 = (bf16[112,512]{1,0:T(8,128)(2,1)S(1)}, bf16[112,512]{1,0:T(8,128)(2,1)S(1)}, u32[]{:S(2)}, u32[]{:S(2)}) collective-permute-start(bf16[112,512]{1,0:T(8,128)(2,1)S(1)} %get-tuple-element.26), channel_id=1, source_target_pairs={{0,2},{1,3},{2,0},{3,1},{4,6},{5,7},{6,4},{7,5},{8,10},{9,11},{10,... | collective-permute-start | bytes 344072 | tf_op jit(solution)/shard_map/ppermute | solution.py:70
  53.3 1.2 %collective-permute-start.3 = (bf16[112,512]{1,0:T(8,128)(2,1)S(1)}, bf16[112,512]{1,0:T(8,128)(2,1)S(1)}, u32[]{:S(2)}, u32[]{:S(2)}) collective-permute-start(bf16[112,512]{1,0:T(8,128)(2,1)S(1)} %get-tuple-element.27), channel_id=1, source_target_pairs={{0,4},{1,5},{2,6},{3,7},{4,0},{5,1},{6,2},{7,3},{8,12},{9,13},{10,... | collective-permute-start | bytes 344072 | tf_op jit(solution)/shard_map/ppermute | solution.py:70
  54.5 0.3 collective-permute-start.4
  54.7 0.1 collective-permute-start.5
  54.8 3.2 %collective-permute-start.6 = (bf16[112,512]{1,0:T(8,128)(2,1)S(1)}, bf16[112,512]{1,0:T(8,128)(2,1)S(1)}, u32[]{:S(2)}, u32[]{:S(2)}) collective-permute-start(bf16[112,512]{1,0:T(8,128)(2,1)S(1)} %get-tuple-element.30), channel_id=1, source_target_pairs={{0,10},{1,11},{2,8},{3,9},{4,14},{5,15},{6,12},{7,13},{8,2},{9,3},... | collective-permute-start | bytes 344072 | tf_op jit(solution)/shard_map/ppermute | solution.py:70
  58.0 0.3 collective-permute-start.7
  58.3 1.2 %collective-permute-start.8 = (bf16[112,512]{1,0:T(8,128)(2,1)S(1)}, bf16[112,512]{1,0:T(8,128)(2,1)S(1)}, u32[]{:S(2)}, u32[]{:S(2)}) collective-permute-start(bf16[112,512]{1,0:T(8,128)(2,1)S(1)} %get-tuple-element.32), channel_id=1, source_target_pairs={{0,14},{1,15},{2,12},{3,13},{4,10},{5,11},{6,8},{7,9},{8,6},{9,7},... | collective-permute-start | bytes 344072 | tf_op jit(solution)/shard_map/ppermute | solution.py:70
  59.5 1.6 %collective-permute-done.4.refs_3_ = bf16[112,512]{1,0:T(8,128)(2,1)S(1)} collective-permute-done((bf16[112,512]{1,0:T(8,128)(2,1)S(1)}, bf16[112,512]{1,0:T(8,128)(2,1)S(1)}, u32[]{:S(2)}, u32[]{:S(2)}) %collective-permute-start.4) | collective-permute-done | bytes 114720 | tf_op jit(solution)/shard_map/ppermute | solution.py:70
  61.1 2.6 %shard_map.61.before = f32[264,1024]{1,0:T(8,128)S(1)} custom-call(bf16[112,512]{1,0:T(8,128)(2,1)S(1)} %get-tuple-element.25.refs_0_, bf16[112,512]{1,0:T(8,128)(2,1)S(1)} %collective-permute-done.2.refs_1_, bf16[112,512]{1,0:T(8,128)(2,1)S(1)} %collective-permute-done.3.refs_2_, bf16[112,512]{1,0:T(8,128)(2,1)S(1)} %collective-permute-done.4.refs_3_), custom_call_target="tpu_custom_call" | custom-call | flops 1073741824 | bytes 2097152 | tf_op jit(solution)/shard_map/pallas_call | solution.py:480
  63.7 1.1 %collective-permute-done.6.refs_1_ = bf16[112,512]{1,0:T(8,128)(2,1)S(1)} collective-permute-done((bf16[112,512]{1,0:T(8,128)(2,1)S(1)}, bf16[112,512]{1,0:T(8,128)(2,1)S(1)}, u32[]{:S(2)}, u32[]{:S(2)}) %collective-permute-start.6) | collective-permute-done | bytes 114720 | tf_op jit(solution)/shard_map/ppermute | solution.py:70
  64.7 9.0 %collective-permute-done.7.refs_2_ = bf16[112,512]{1,0:T(8,128)(2,1)S(1)} collective-permute-done((bf16[112,512]{1,0:T(8,128)(2,1)S(1)}, bf16[112,512]{1,0:T(8,128)(2,1)S(1)}, u32[]{:S(2)}, u32[]{:S(2)}) %collective-permute-start.7) | collective-permute-done | bytes 114720 | tf_op jit(solution)/shard_map/ppermute | solution.py:70
  73.7 4.0 %collective-permute-done.8.refs_3_ = bf16[112,512]{1,0:T(8,128)(2,1)S(1)} collective-permute-done((bf16[112,512]{1,0:T(8,128)(2,1)S(1)}, bf16[112,512]{1,0:T(8,128)(2,1)S(1)}, u32[]{:S(2)}, u32[]{:S(2)}) %collective-permute-start.8) | collective-permute-done | bytes 114720 | tf_op jit(solution)/shard_map/ppermute | solution.py:70
  77.8 2.7 %shard_map.62 = (f32[136,1024]{1,0:T(8,128)S(1)}, f32[136,1024]{1,0:T(8,128)S(1)}) custom-call(s32[1]{0:T(128)} %bitcast.12.core, f32[264,1024]{1,0:T(8,128)S(1)} %shard_map.61.before, bf16[112,512]{1,0:T(8,128)(2,1)S(1)} %collective-permute-done.5.refs_0_, bf16[112,512]{1,0:T(8,128)(2,1)S(1)} %collective-permute-done.6.refs_1_, ...), custom_call_target="tpu_custom_call" | custom-call | flops 1073741824 | bytes 2097152 | tf_op jit(solution)/shard_map/pallas_call | solution.py:489
  80.4 1.6 %collective-permute-start.9 = (f32[136,1024]{1,0:T(8,128)S(1)}, f32[136,1024]{1,0:T(8,128)S(1)}, u32[]{:S(2)}, u32[]{:S(2)}) collective-permute-start(f32[136,1024]{1,0:T(8,128)S(1)} %get-tuple-element.34), channel_id=1, source_target_pairs={{0,1},{1,0},{2,3},{3,2},{4,5},{5,4},{6,7},{7,6},{8,9},{9,8},{10,11... | collective-permute-start | bytes 1671176 | tf_op jit(solution)/shard_map/ppermute | solution.py:70
  82.1 1.0 %constant_dynamic-slice_fusion.refs_2_ = bf16[16,64,128]{2,1,0:T(8,128)(2,1)S(1)} fusion(bf16[256,64,128]{2,1,0:T(8,128)(2,1)} %param.4, s32[]{:T(128)S(6)} %select_n.32), kind=kLoop, calls=%fused_computation | loop fusion | bytes 524292 | tf_op jit(solution)/shard_map/dynamic_slice | solution.py:434
  83.0 0.6 collective-permute-done.9.refs_1_
  83.7 1.7 %shard_map.63 = (f32[16,64,128]{2,1,0:T(8,128)}, f32[1]{0:T(128)}) custom-call(f32[136,1024]{1,0:T(8,128)S(1)} %get-tuple-element.33.refs_0_, f32[136,1024]{1,0:T(8,128)S(1)} %collective-permute-done.9.refs_1_, bf16[16,64,128]{2,1,0:T(8,128)(2,1)S(1)} %constant_dynamic-slice_fusion.refs_2_), custom_call_target="tpu_custom_call" | custom-call | tf_op jit(solution)/shard_map/pallas_call | solution.py:500
  (10 shorter events, 0.0 us)
Async XLA Ops:
  1.5 13.9 %collective-permute-start.1 = (f32[64,256]{1,0:T(8,128)S(1)}, f32[64,256]{1,0:T(8,128)S(1)}, u32[]{:S(2)}, u32[]{:S(2)}) collective-permute-start(f32[64,256]{1,0:T(8,128)S(1)} %get-tuple-element.37), channel_id=1, source_target_pairs={{1,0},{2,1},{3,2},{4,3},{5,4},{6,5},{7,6},{8,7},{9,8},{10,9},{11,1... | collective-permute-start | bytes 196616 | tf_op jit(solution)/shard_map/ppermute | solution.py:65
  4.1 22.6 %collective-permute-start = (f32[64,256]{1,0:T(8,128)S(1)}, f32[64,256]{1,0:T(8,128)S(1)}, u32[]{:S(2)}, u32[]{:S(2)}) collective-permute-start(f32[64,256]{1,0:T(8,128)S(1)} %get-tuple-element.38), channel_id=1, source_target_pairs={{0,1},{1,2},{2,3},{3,4},{4,5},{5,6},{6,7},{7,8},{8,9},{9,10},{10,1... | collective-permute-start | bytes 196616 | tf_op jit(solution)/shard_map/ppermute | solution.py:65
  7.2 8.2 %copy-start.4 = (f32[64,512]{1,0:T(8,128)S(1)}, f32[64,512]{1,0:T(8,128)}, u32[]{:S(2)}) copy-start(f32[64,512]{1,0:T(8,128)} %middle.5) | copy-start | bytes 393220
  15.4 2.2 %copy-start = (bf16[128,64,256]{2,1,0:T(8,128)(2,1)S(1)}, bf16[128,64,256]{2,1,0:T(8,128)(2,1)}, u32[]{:S(2)}) copy-start(bf16[128,64,256]{2,1,0:T(8,128)(2,1)} %copy.6) | copy-start | bytes 12582916
  21.0 12.5 %all-to-all-start = ((f32[16,8,128]{2,1,0:T(8,128)}), f32[16,8,128]{2,1,0:T(8,128)S(1)}, u32[]{:S(2)}, u32[]{:S(2)}) async-start(f32[16,8,128]{2,1,0:T(8,128)} %get-tuple-element.23), calls=%async_computation | async-start | bytes 131072 | tf_op jit(solution)/shard_map/all_to_all | solution.py:411
  26.8 2.2 %copy-start.1 = (bf16[128,64,256]{2,1,0:T(8,128)(2,1)S(1)}, bf16[128,64,256]{2,1,0:T(8,128)(2,1)}, u32[]{:S(2)}) copy-start(bf16[128,64,256]{2,1,0:T(8,128)(2,1)} %copy.6) | copy-start | bytes 12582916
  31.6 1.9 %copy-start.2 = (bf16[8192,256]{1,0:T(8,128)(2,1)}, bf16[8192,256]{1,0:T(8,128)(2,1)S(1)}, u32[]{:S(2)}) copy-start(bf16[8192,256]{1,0:T(8,128)(2,1)S(1)} %get-tuple-element.20.lags) | copy-start | bytes 12582916
  33.5 2.2 %copy-start.3 = (bf16[8192,256]{1,0:T(8,128)(2,1)S(1)}, bf16[8192,256]{1,0:T(8,128)(2,1)}, u32[]{:S(2)}) copy-start(bf16[8192,256]{1,0:T(8,128)(2,1)} %copy-done.2) | copy-start | bytes 12582916
  52.0 6.0 %collective-permute-start.2 = (bf16[112,512]{1,0:T(8,128)(2,1)S(1)}, bf16[112,512]{1,0:T(8,128)(2,1)S(1)}, u32[]{:S(2)}, u32[]{:S(2)}) collective-permute-start(bf16[112,512]{1,0:T(8,128)(2,1)S(1)} %get-tuple-element.26), channel_id=1, source_target_pairs={{0,2},{1,3},{2,0},{3,1},{4,6},{5,7},{6,4},{7,5},{8,10},{9,11},{10,... | collective-permute-start | bytes 344072 | tf_op jit(solution)/shard_map/ppermute | solution.py:70
  53.3 5.0 %collective-permute-start.3 = (bf16[112,512]{1,0:T(8,128)(2,1)S(1)}, bf16[112,512]{1,0:T(8,128)(2,1)S(1)}, u32[]{:S(2)}, u32[]{:S(2)}) collective-permute-start(bf16[112,512]{1,0:T(8,128)(2,1)S(1)} %get-tuple-element.27), channel_id=1, source_target_pairs={{0,4},{1,5},{2,6},{3,7},{4,0},{5,1},{6,2},{7,3},{8,12},{9,13},{10,... | collective-permute-start | bytes 344072 | tf_op jit(solution)/shard_map/ppermute | solution.py:70
  54.5 6.6 %collective-permute-start.4 = (bf16[112,512]{1,0:T(8,128)(2,1)S(1)}, bf16[112,512]{1,0:T(8,128)(2,1)S(1)}, u32[]{:S(2)}, u32[]{:S(2)}) collective-permute-start(bf16[112,512]{1,0:T(8,128)(2,1)S(1)} %get-tuple-element.28), channel_id=1, source_target_pairs={{0,6},{1,7},{2,4},{3,5},{4,2},{5,3},{6,0},{7,1},{8,14},{9,15},{10,... | collective-permute-start | bytes 344072 | tf_op jit(solution)/shard_map/ppermute | solution.py:70
  54.7 8.9 %collective-permute-start.5 = (bf16[112,512]{1,0:T(8,128)(2,1)S(1)}, bf16[112,512]{1,0:T(8,128)(2,1)S(1)}, u32[]{:S(2)}, u32[]{:S(2)}) collective-permute-start(bf16[112,512]{1,0:T(8,128)(2,1)S(1)} %get-tuple-element.29), channel_id=1, source_target_pairs={{0,8},{1,9},{2,10},{3,11},{4,12},{5,13},{6,14},{7,15},{8,0},{9,1},... | collective-permute-start | bytes 344072 | tf_op jit(solution)/shard_map/ppermute | solution.py:70
  54.8 9.9 %collective-permute-start.6 = (bf16[112,512]{1,0:T(8,128)(2,1)S(1)}, bf16[112,512]{1,0:T(8,128)(2,1)S(1)}, u32[]{:S(2)}, u32[]{:S(2)}) collective-permute-start(bf16[112,512]{1,0:T(8,128)(2,1)S(1)} %get-tuple-element.30), channel_id=1, source_target_pairs={{0,10},{1,11},{2,8},{3,9},{4,14},{5,15},{6,12},{7,13},{8,2},{9,3},... | collective-permute-start | bytes 344072 | tf_op jit(solution)/shard_map/ppermute | solution.py:70
  58.0 15.7 %collective-permute-start.7 = (bf16[112,512]{1,0:T(8,128)(2,1)S(1)}, bf16[112,512]{1,0:T(8,128)(2,1)S(1)}, u32[]{:S(2)}, u32[]{:S(2)}) collective-permute-start(bf16[112,512]{1,0:T(8,128)(2,1)S(1)} %get-tuple-element.31), channel_id=1, source_target_pairs={{0,12},{1,13},{2,14},{3,15},{4,8},{5,9},{6,10},{7,11},{8,4},{9,5},... | collective-permute-start | bytes 344072 | tf_op jit(solution)/shard_map/ppermute | solution.py:70
  58.3 19.5 %collective-permute-start.8 = (bf16[112,512]{1,0:T(8,128)(2,1)S(1)}, bf16[112,512]{1,0:T(8,128)(2,1)S(1)}, u32[]{:S(2)}, u32[]{:S(2)}) collective-permute-start(bf16[112,512]{1,0:T(8,128)(2,1)S(1)} %get-tuple-element.32), channel_id=1, source_target_pairs={{0,14},{1,15},{2,12},{3,13},{4,10},{5,11},{6,8},{7,9},{8,6},{9,7},... | collective-permute-start | bytes 344072 | tf_op jit(solution)/shard_map/ppermute | solution.py:70
  80.4 3.2 %collective-permute-start.9 = (f32[136,1024]{1,0:T(8,128)S(1)}, f32[136,1024]{1,0:T(8,128)S(1)}, u32[]{:S(2)}, u32[]{:S(2)}) collective-permute-start(f32[136,1024]{1,0:T(8,128)S(1)} %get-tuple-element.34), channel_id=1, source_target_pairs={{0,1},{1,0},{2,3},{3,2},{4,5},{5,4},{6,7},{7,6},{8,9},{9,8},{10,11... | collective-permute-start | bytes 1671176 | tf_op jit(solution)/shard_map/ppermute | solution.py:70

commit v4 on v3

--- a/solution.py
+++ b/solution.py
@@ -21,7 +21,9 @@
 HALO = 2 * ATOM_LEN
 F32 = jnp.float32
 BF16 = jnp.bfloat16
+PITCH = CHANNELS + 8
 PEERS = 8
+OWN_LIMIT = 60 * 1024 * 1024
 VMEM_LIMIT = 36 * 1024 * 1024
 
 
@@ -102,38 +104,71 @@
     fill_windows(pairs, windows, length - FINE)
 
 
-def own_kernel(middle, right_any, lags, gradient, largest, right, pairs, windows, sems):
+def turn_dictionary(atoms, lags, by_atom, by_lag, copies):
+    half = ATOMS // 2
+    for part in range(2):
+        copies[part].wait()
+        for atom in range(half):
+            by_atom[atom * PITCH : atom * PITCH + CHANNELS, :] = atoms[part * half + atom].astype(
+                F32
+            )
+        for channel in range(CHANNELS):
+            turned = by_atom[pl.ds(channel, half, stride=PITCH), :].T
+            by_lag[pl.ds(channel, ATOM_LEN, stride=PITCH), :] = turned
+        for lag in range(ATOM_LEN):
+            lags[lag * CHANNELS : (lag + 1) * CHANNELS, part * half : (part + 1) * half] = by_lag[
+                lag * PITCH : lag * PITCH + CHANNELS, :
+            ].astype(BF16)
+
+
+def own_kernel(
+    middle, right_any, atoms_any, gradient, largest, lags_out,
+    right, atoms, lags, by_atom, by_lag, pairs, windows, sems, atom_sems,
+):
     width = middle.shape[1]
-    near = pltpu.make_async_copy(right_any, right, sems.at[COARSE])
+    half = ATOMS // 2
+    loads = [
+        pltpu.make_async_copy(
+            atoms_any.at[pl.ds(part * half, half)],
+            atoms.at[pl.ds(part * half, half)],
+            atom_sems.at[part],
+        )
+        for part in range(2)
+    ]
+    loads[0].start()
+    near = pltpu.make_async_copy(right_any.at[:, pl.ds(0, HALO)], right, sems.at[COARSE])
     near.start()
+    loads[1].start()
     near.wait()
     whole = jnp.concatenate([middle[...], right[:, 0:ATOM_LEN]], 1)
     windows_of(-whole, pairs, windows)
+    turn_dictionary(atoms, lags, by_atom, by_lag, loads)
+    copies = fetch_lags(lags, lags_out, sems)
     adjoint(windows, lags, gradient, [(0, width)])
     own = jnp.abs(gradient[...]) * SCALE
     folded = jnp.max(own.reshape(width // 8, 8, ATOMS), 0)
     folded = jnp.maximum(folded[:, :128], folded[:, 128:])
     for peer in range(largest.shape[0]):
         largest[peer] = folded
+    for copy in copies:
+        copy.wait()
 
 
 def border_kernel(
-    left_any, middle, right_any, lags, gradient, lags_out, left, right, pairs, windows, sems
+    left_any, middle, right_any, lags, gradient, left, right, pairs, windows, sems
 ):
     near = [
-        pltpu.make_async_copy(left_any, left, sems.at[COARSE]),
-        pltpu.make_async_copy(right_any, right, sems.at[COARSE + 1]),
+        pltpu.make_async_copy(
+            left_any.at[:, pl.ds(left_any.shape[1] - HALO, HALO)], left, sems.at[COARSE]),
+        pltpu.make_async_copy(right_any.at[:, pl.ds(0, HALO)], right, sems.at[COARSE + 1]),
     ]
     for copy in near:
         copy.start()
-    copies = fetch_lags(lags, lags_out, sems)
     for copy in near:
         copy.wait()
     whole = jnp.concatenate([left[...], middle[:, 0:ATOM_LEN], right[...]], 1)
     windows_of(-whole, pairs, windows)
     adjoint(windows, lags, gradient, [(0, HALO), (HALO + ATOM_LEN, ATOM_LEN)])
-    for copy in copies:
-        copy.wait()
 
 
 def forward(codes, lags, wide, spread, folded, start, rows):
@@ -167,8 +202,9 @@
     signal, codes, codes_low, pairs, windows, wide, spread, folded = scratch[:8]
     left, right, sems = scratch[8:]
     near = [
-        pltpu.make_async_copy(left_any, left, sems.at[COARSE]),
-        pltpu.make_async_copy(right_any, right, sems.at[COARSE + 1]),
+        pltpu.make_async_copy(
+            left_any.at[:, pl.ds(left_any.shape[1] - HALO, HALO)], left, sems.at[COARSE]),
+        pltpu.make_async_copy(right_any.at[:, pl.ds(0, HALO)], right, sems.at[COARSE + 1]),
     ]
     for copy in near:
         copy.start()
@@ -385,39 +421,40 @@
     width = signal.shape[1]
     count = lax.axis_size("tm")
     me = lax.axis_index("tm")
-    left = shifted(signal[:, width - HALO :], "tm", 1)
-    right = shifted(signal[:, :HALO], "tm", -1)
-    lags = jnp.transpose(dictionary, (2, 1, 0)).reshape(ATOM_LEN * CHANNELS, ATOMS)
+    left = shifted(signal, "tm", 1)
+    right = shifted(signal, "tm", -1)
     rows1 = width + 3 * ATOM_LEN
     span = width + 2 * HALO
 
     near_scratch = [pltpu.VMEM((CHANNELS, HALO), F32)]
     sems = [pltpu.SemaphoreType.DMA((COARSE + 2,))]
     bordered = width + ATOM_LEN
-    gradient, peak = pl.pallas_call(
+    gradient, peak, lags = pl.pallas_call(
         own_kernel,
         out_shape=(
             jax.ShapeDtypeStruct((width, ATOMS), F32),
             jax.ShapeDtypeStruct((count, 8, 128), F32),
+            jax.ShapeDtypeStruct((ATOM_LEN * CHANNELS, ATOMS), BF16),
         ),
-        in_specs=[vmem(), anywhere(), vmem()],
-        out_specs=(vmem(),) * 2,
+        in_specs=[vmem(), anywhere(), pl.BlockSpec(memory_space=pltpu.HBM)],
+        out_specs=(vmem(), vmem(), pl.BlockSpec(memory_space=pltpu.HBM)),
         scratch_shapes=near_scratch
+        + [pltpu.VMEM(dictionary.shape, BF16)]
+        + [pltpu.VMEM((ATOM_LEN * CHANNELS, ATOMS), BF16)]
+        + [pltpu.VMEM((ATOM_LEN * PITCH, 128), F32)] * 2
         + [pltpu.VMEM((bordered, 128), F32), pltpu.VMEM((bordered, WIDE), BF16)]
-        + sems,
-        compiler_params=kernel_params(),
+        + sems
+        + [pltpu.SemaphoreType.DMA((2,))],
+        compiler_params=kernel_params(OWN_LIMIT),
         cost_estimate=cost(2 * width * ATOMS * WIDE * COARSE, 5 << 20),
-    )(signal, right, lags)
+    )(signal, right, dictionary)
     peak = lax.all_to_all(peak, "tm", 0, 0, tiled=False)
     span_border = 2 * HALO + ATOM_LEN
-    border, lags = pl.pallas_call(
+    border = pl.pallas_call(
         border_kernel,
-        out_shape=(
-            jax.ShapeDtypeStruct((HALO + ATOM_LEN, ATOMS), F32),
-            jax.ShapeDtypeStruct(lags.shape, BF16),
-        ),
+        out_shape=jax.ShapeDtypeStruct((HALO + ATOM_LEN, ATOMS), F32),
         in_specs=[anywhere(), vmem(), anywhere(), vmem()],
-        out_specs=(vmem(), vmem()),
+        out_specs=vmem(),
         scratch_shapes=near_scratch * 2
         + [pltpu.VMEM((span_border, 128), F32), pltpu.VMEM((span_border, WIDE), BF16)]
         + sems,
@@ -473,7 +510,7 @@
     if shared:
         core = me % 2
         pieces = list(others)
-        for turn in (4, 5, 6, 7, 2, 3, 1):
+        for turn in range(1, PEERS):
             pieces[turn] = swapped(pieces[turn], 2 * turn)
         half_rows = jax.ShapeDtypeStruct((COARSE * owned + 8, WIDE), F32)
         blocks = PEERS // 2
@@ -485,7 +522,7 @@
             scratch_shapes=correlate_scratch(blocks, 2 * owned),
             compiler_params=kernel_params(),
             cost_estimate=cost(2 * COARSE * 2 * owned * blocks * width * WIDE, 2 << 20),
-        )(*pieces[:blocks])
+        )(*[pieces[turn] for turn in (0, 4, 5, 6)])
         keep, give = pl.pallas_call(
             shared_second,
             out_shape=(half_rows, half_rows),
@@ -495,7 +532,7 @@
             + [pltpu.VMEM((COARSE * 2 * owned, WIDE), F32)],
             compiler_params=kernel_params(),
             cost_estimate=cost(2 * COARSE * 2 * owned * blocks * width * WIDE, 2 << 20),
-        )(core.reshape(1).astype(jnp.int32), before, *pieces[blocks:])
+        )(core.reshape(1).astype(jnp.int32), before, *[pieces[turn] for turn in (7, 3, 2, 1)])
         recv = swapped(give, 1)
         new_dictionary, loss = pl.pallas_call(
             lambda *refs: last_kernel(inverse, *refs),

time: 86 us -> 80.9 us (0.941)
  the two profiles are of different devices: /device:TPU:19 before, /device:TPU:0 now
where the time goes in v4:
time: 80.9 us; the launch traced here: 80.5 us
  Pallas kernels  35.3 us (44%)
  starting transfers between devices  21.4 us (26%)
  waiting for transfers between devices  15.2 us (19%)
  local copies, waits for them, and re-layouts  7 us (9%)
  between operations  1.62 us (2%)
    pallas_call x1, Pallas kernels, body(): pl.pallas_call(second_kernel, out_shape=(jax.ShapeDtypeStruct((ATOMS, wid...  16.2 us
    ppermute x8, waiting for transfers between devices, swapped(): return lax.ppermute(value, 'tm', [(i, i ^ bit) for i in range(count)])  13.6 us
    pallas_call x1, Pallas kernels, body(): pl.pallas_call(own_kernel, out_shape=(jax.ShapeDtypeStruct((width, ATOMS)...  9.91 us
    ppermute x8, starting transfers between devices, swapped(): return lax.ppermute(value, 'tm', [(i, i ^ bit) for i in range(count)])  8.61 us
    all_to_all x1, starting transfers between devices, body(): peak = lax.all_to_all(peak, 'tm', 0, 0, tiled=False)  8.28 us
    unnamed x14, local copies, waits for them, and re-layouts  5.94 us
    ppermute x2, starting transfers between devices, shifted(): lax.ppermute(value, axis, [(source, source + steps) for source in range(l...  4.47 us
    pallas_call x1, Pallas kernels, body(): pl.pallas_call(shared_second, out_shape=(half_rows, half_rows), in_specs=...  2.68 us
  transfers between devices with their start and end apart: 11, of which 5 were waited for; matrix products, arithmetic and copies ran while one was open for 1% of the time, Pallas kernels for 18%

profile of v4, /device:TPU:0, one launch (start us, length us, event | category | flops | bytes accessed | tf_op | source)
XLA Modules:
  0.0 80.5 jit_solution(8404584086830430778)
XLA Ops:
  0.6 0.0 copy-start.3
  0.6 1.4 %collective-permute-start.1 = (f32[64,512]{1,0:T(8,128)}, f32[64,512]{1,0:T(8,128)S(1)}, u32[]{:S(2)}, u32[]{:S(2)}) collective-permute-start(f32[64,512]{1,0:T(8,128)} %middle.5), channel_id=1, source_target_pairs={{1,0},{2,1},{3,2},{4,3},{5,4},{6,5},{7,6},{8,7},{9,8},{10,9},{11,1... | collective-permute-start | bytes 393224 | tf_op jit(solution)/shard_map/ppermute | solution.py:67
  2.1 3.0 %collective-permute-start = (f32[64,512]{1,0:T(8,128)}, f32[64,512]{1,0:T(8,128)S(1)}, u32[]{:S(2)}, u32[]{:S(2)}) collective-permute-start(f32[64,512]{1,0:T(8,128)} %middle.5), channel_id=1, source_target_pairs={{0,1},{1,2},{2,3},{3,4},{4,5},{5,6},{6,7},{7,8},{8,9},{9,10},{10,1... | collective-permute-start | bytes 393224 | tf_op jit(solution)/shard_map/ppermute | solution.py:67
  5.8 0.1 stack.43.valid
  5.9 0.0 collective-permute-done.1.right_any
  5.9 0.0 copy-start.4
  5.9 0.6 copy-done.4
  6.5 9.9 %shard_map.58 = (f32[512,256]{1,0:T(8,128)}, f32[16,8,128]{2,1,0:T(8,128)}, bf16[8192,256]{1,0:T(8,128)(2,1)}) custom-call(f32[64,512]{1,0:T(8,128)} %middle.5, f32[64,512]{1,0:T(8,128)} %copy-done.4, bf16[256,64,128]{2,1,0:T(8,128)(2,1)} %atoms_any.1), custom_call_target="tpu_custom_call" | custom-call | flops 2147483648 | bytes 5242880 | tf_op jit(solution)/shard_map/pallas_call | solution.py:432
  16.5 0.0 copy-start.6
  16.5 8.3 %all-to-all-start = ((f32[16,8,128]{2,1,0:T(8,128)}), f32[16,8,128]{2,1,0:T(8,128)S(1)}, u32[]{:S(2)}, u32[]{:S(2)}) async-start(f32[16,8,128]{2,1,0:T(8,128)} %get-tuple-element.21), calls=%async_computation | async-start | bytes 131072 | tf_op jit(solution)/shard_map/all_to_all | solution.py:451
  24.8 2.2 %copy-done = bf16[8192,256]{1,0:T(8,128)(2,1)S(1)} copy-done((bf16[8192,256]{1,0:T(8,128)(2,1)S(1)}, bf16[8192,256]{1,0:T(8,128)(2,1)}, u32[]{:S(2)}) %copy-start) | copy-done | bytes 4194328
  27.0 0.9 %copy-done.5 = f32[64,512]{1,0:T(8,128)S(1)} copy-done((f32[64,512]{1,0:T(8,128)S(1)}, f32[64,512]{1,0:T(8,128)}, u32[]{:S(2)}) %copy-start.5) | copy-done | bytes 131096
  27.9 2.2 %shard_map.59.border = f32[384,256]{1,0:T(8,128)S(1)} custom-call(f32[64,512]{1,0:T(8,128)S(1)} %collective-permute-done.left_any, f32[64,512]{1,0:T(8,128)S(1)} %copy-done.3, f32[64,512]{1,0:T(8,128)S(1)} %copy-done.5, bf16[8192,256]{1,0:T(8,128)(2,1)S(1)} %copy-done), custom_call_target="tpu_custom_call" | custom-call | flops 1610612736 | bytes 5242880 | tf_op jit(solution)/shard_map/pallas_call | solution.py:453
  30.1 1.6 %all-to-all-done.peak = f32[16,8,128]{2,1,0:T(8,128)S(1)} async-done(((f32[16,8,128]{2,1,0:T(8,128)}), f32[16,8,128]{2,1,0:T(8,128)S(1)}, u32[]{:S(2)}, u32[]{:S(2)}) %all-to-all-start) | async-done | bytes 65568 | tf_op jit(solution)/shard_map/all_to_all | solution.py:451
  31.7 2.2 %copy-done.1 = bf16[8192,256]{1,0:T(8,128)(2,1)S(1)} copy-done((bf16[8192,256]{1,0:T(8,128)(2,1)S(1)}, bf16[8192,256]{1,0:T(8,128)(2,1)}, u32[]{:S(2)}) %copy-start.1) | copy-done | bytes 4194328
  33.9 16.2 %shard_map.60 = (f32[256,512]{1,0:T(8,128)}, bf16[112,512]{1,0:T(8,128)(2,1)S(1)}, bf16[112,512]{1,0:T(8,128)(2,1)S(1)}, bf16[112,512]{1,0:T(8,128)(2,1)S(1)}, b...) custom-call(f32[64,512]{1,0:T(8,128)S(1)} %collective-permute-done.l, ...), custom_call_target="tpu_custom_call" | custom-call | tf_op jit(solution)/shard_map/pallas_call | solution.py:481
  50.0 1.3 %collective-permute-start.2 = (bf16[112,512]{1,0:T(8,128)(2,1)S(1)}, bf16[112,512]{1,0:T(8,128)(2,1)S(1)}, u32[]{:S(2)}, u32[]{:S(2)}) collective-permute-start(bf16[112,512]{1,0:T(8,128)(2,1)S(1)} %get-tuple-element.24), channel_id=1, source_target_pairs={{0,8},{1,9},{2,10},{3,11},{4,12},{5,13},{6,14},{7,15},{8,0},{9,1},... | collective-permute-start | bytes 344072 | tf_op jit(solution)/shard_map/ppermute | solution.py:72
  51.4 1.5 %collective-permute-start.3 = (bf16[112,512]{1,0:T(8,128)(2,1)S(1)}, bf16[112,512]{1,0:T(8,128)(2,1)S(1)}, u32[]{:S(2)}, u32[]{:S(2)}) collective-permute-start(bf16[112,512]{1,0:T(8,128)(2,1)S(1)} %get-tuple-element.25), channel_id=1, source_target_pairs={{0,10},{1,11},{2,8},{3,9},{4,14},{5,15},{6,12},{7,13},{8,2},{9,3},... | collective-permute-start | bytes 344072 | tf_op jit(solution)/shard_map/ppermute | solution.py:72
  52.8 3.3 %collective-permute-start.4 = (bf16[112,512]{1,0:T(8,128)(2,1)S(1)}, bf16[112,512]{1,0:T(8,128)(2,1)S(1)}, u32[]{:S(2)}, u32[]{:S(2)}) collective-permute-start(bf16[112,512]{1,0:T(8,128)(2,1)S(1)} %get-tuple-element.26), channel_id=1, source_target_pairs={{0,12},{1,13},{2,14},{3,15},{4,8},{5,9},{6,10},{7,11},{8,4},{9,5},... | collective-permute-start | bytes 344072 | tf_op jit(solution)/shard_map/ppermute | solution.py:72
  56.1 1.7 %collective-permute-start.5 = (bf16[112,512]{1,0:T(8,128)(2,1)S(1)}, bf16[112,512]{1,0:T(8,128)(2,1)S(1)}, u32[]{:S(2)}, u32[]{:S(2)}) collective-permute-start(bf16[112,512]{1,0:T(8,128)(2,1)S(1)} %get-tuple-element.27), channel_id=1, source_target_pairs={{0,14},{1,15},{2,12},{3,13},{4,10},{5,11},{6,8},{7,9},{8,6},{9,7},... | collective-permute-start | bytes 344072 | tf_op jit(solution)/shard_map/ppermute | solution.py:72
  57.8 8.3 %collective-permute-done.2.refs_1_ = bf16[112,512]{1,0:T(8,128)(2,1)S(1)} collective-permute-done((bf16[112,512]{1,0:T(8,128)(2,1)S(1)}, bf16[112,512]{1,0:T(8,128)(2,1)S(1)}, u32[]{:S(2)}, u32[]{:S(2)}) %collective-permute-start.2) | collective-permute-done | bytes 114720 | tf_op jit(solution)/shard_map/ppermute | solution.py:72
  66.1 3.0 %collective-permute-done.3.refs_2_ = bf16[112,512]{1,0:T(8,128)(2,1)S(1)} collective-permute-done((bf16[112,512]{1,0:T(8,128)(2,1)S(1)}, bf16[112,512]{1,0:T(8,128)(2,1)S(1)}, u32[]{:S(2)}, u32[]{:S(2)}) %collective-permute-start.3) | collective-permute-done | bytes 114720 | tf_op jit(solution)/shard_map/ppermute | solution.py:72
  69.1 0.8 %collective-permute-start.8 = (bf16[112,512]{1,0:T(8,128)(2,1)S(1)}, bf16[112,512]{1,0:T(8,128)(2,1)S(1)}, u32[]{:S(2)}, u32[]{:S(2)}) collective-permute-start(bf16[112,512]{1,0:T(8,128)(2,1)S(1)} %get-tuple-element.30), channel_id=1, source_target_pairs={{0,2},{1,3},{2,0},{3,1},{4,6},{5,7},{6,4},{7,5},{8,10},{9,11},{10,... | collective-permute-start | bytes 344072 | tf_op jit(solution)/shard_map/ppermute | solution.py:72
  70.0 0.0 collective-permute-done.4.refs_3_
  70.0 2.6 %shard_map.61.before = f32[264,1024]{1,0:T(8,128)S(1)} custom-call(bf16[112,512]{1,0:T(8,128)(2,1)S(1)} %get-tuple-element.23.refs_0_, bf16[112,512]{1,0:T(8,128)(2,1)S(1)} %collective-permute-done.2.refs_1_, bf16[112,512]{1,0:T(8,128)(2,1)S(1)} %collective-permute-done.3.refs_2_, bf16[112,512]{1,0:T(8,128)(2,1)S(1)} %collective-permute-done.4.refs_3_), custom_call_target="tpu_custom_call" | custom-call | flops 1073741824 | bytes 2097152 | tf_op jit(solution)/shard_map/pallas_call | solution.py:517
  72.6 0.0 collective-permute-done.5.refs_0_
  72.6 1.3 %collective-permute-done.8.refs_3_ = bf16[112,512]{1,0:T(8,128)(2,1)S(1)} collective-permute-done((bf16[112,512]{1,0:T(8,128)(2,1)S(1)}, bf16[112,512]{1,0:T(8,128)(2,1)S(1)}, u32[]{:S(2)}, u32[]{:S(2)}) %collective-permute-start.8) | collective-permute-done | bytes 114720 | tf_op jit(solution)/shard_map/ppermute | solution.py:72
  73.9 2.7 %shard_map.62 = (f32[136,1024]{1,0:T(8,128)S(1)}, f32[136,1024]{1,0:T(8,128)S(1)}) custom-call(s32[1]{0:T(128)} %bitcast.10.core, f32[264,1024]{1,0:T(8,128)S(1)} %shard_map.61.before, bf16[112,512]{1,0:T(8,128)(2,1)S(1)} %collective-permute-done.5.refs_0_, bf16[112,512]{1,0:T(8,128)(2,1)S(1)} %collective-permute-done.6.refs_1_, ...), custom_call_target="tpu_custom_call" | custom-call | flops 1073741824 | bytes 2097152 | tf_op jit(solution)/shard_map/pallas_call | solution.py:526
  76.6 0.1 collective-permute-start.9
  76.7 1.0 %constant_dynamic-slice_fusion.refs_2_ = bf16[16,64,128]{2,1,0:T(8,128)(2,1)S(1)} fusion(bf16[256,64,128]{2,1,0:T(8,128)(2,1)} %atoms_any.1, s32[]{:T(128)S(6)} %select_n.32), kind=kLoop, calls=%fused_computation | loop fusion | bytes 524292 | tf_op jit(solution)/shard_map/dynamic_slice | solution.py:471
  77.7 1.0 %collective-permute-done.9.refs_1_ = f32[136,1024]{1,0:T(8,128)S(1)} collective-permute-done((f32[136,1024]{1,0:T(8,128)S(1)}, f32[136,1024]{1,0:T(8,128)S(1)}, u32[]{:S(2)}, u32[]{:S(2)}) %collective-permute-start.9) | collective-permute-done | bytes 557088 | tf_op jit(solution)/shard_map/ppermute | solution.py:72
  78.6 1.7 %shard_map.63 = (f32[16,64,128]{2,1,0:T(8,128)}, f32[1]{0:T(128)}) custom-call(f32[136,1024]{1,0:T(8,128)S(1)} %get-tuple-element.31.refs_0_, f32[136,1024]{1,0:T(8,128)S(1)} %collective-permute-done.9.refs_1_, bf16[16,64,128]{2,1,0:T(8,128)(2,1)S(1)} %constant_dynamic-slice_fusion.refs_2_), custom_call_target="tpu_custom_call" | custom-call | tf_op jit(solution)/shard_map/pallas_call | solution.py:537
  (12 shorter events, 0.0 us)
Async XLA Ops:
  0.6 24.1 %copy-start.3 = (f32[64,512]{1,0:T(8,128)S(1)}, f32[64,512]{1,0:T(8,128)}, u32[]{:S(2)}) copy-start(f32[64,512]{1,0:T(8,128)} %middle.5) | copy-start | bytes 393220
  0.6 5.2 %collective-permute-start.1 = (f32[64,512]{1,0:T(8,128)}, f32[64,512]{1,0:T(8,128)S(1)}, u32[]{:S(2)}, u32[]{:S(2)}) collective-permute-start(f32[64,512]{1,0:T(8,128)} %middle.5), channel_id=1, source_target_pairs={{1,0},{2,1},{3,2},{4,3},{5,4},{6,5},{7,6},{8,7},{9,8},{10,9},{11,1... | collective-permute-start | bytes 393224 | tf_op jit(solution)/shard_map/ppermute | solution.py:67
  2.1 22.7 %collective-permute-start = (f32[64,512]{1,0:T(8,128)}, f32[64,512]{1,0:T(8,128)S(1)}, u32[]{:S(2)}, u32[]{:S(2)}) collective-permute-start(f32[64,512]{1,0:T(8,128)} %middle.5), channel_id=1, source_target_pairs={{0,1},{1,2},{2,3},{3,4},{4,5},{5,6},{6,7},{7,8},{8,9},{9,10},{10,1... | collective-permute-start | bytes 393224 | tf_op jit(solution)/shard_map/ppermute | solution.py:67
  5.9 0.7 copy-start.4
  16.5 15.2 %copy-start.6 = (f32[64,512]{1,0:T(8,128)S(1)}, f32[64,512]{1,0:T(8,128)}, u32[]{:S(2)}) copy-start(f32[64,512]{1,0:T(8,128)} %copy-done.4) | copy-start | bytes 393220
  16.5 15.2 %all-to-all-start = ((f32[16,8,128]{2,1,0:T(8,128)}), f32[16,8,128]{2,1,0:T(8,128)S(1)}, u32[]{:S(2)}, u32[]{:S(2)}) async-start(f32[16,8,128]{2,1,0:T(8,128)} %get-tuple-element.21), calls=%async_computation | async-start | bytes 131072 | tf_op jit(solution)/shard_map/all_to_all | solution.py:451
  24.8 2.2 %copy-start = (bf16[8192,256]{1,0:T(8,128)(2,1)S(1)}, bf16[8192,256]{1,0:T(8,128)(2,1)}, u32[]{:S(2)}) copy-start(bf16[8192,256]{1,0:T(8,128)(2,1)} %get-tuple-element.19.lags) | copy-start | bytes 12582916
  27.0 0.9 %copy-start.5 = (f32[64,512]{1,0:T(8,128)S(1)}, f32[64,512]{1,0:T(8,128)}, u32[]{:S(2)}) copy-start(f32[64,512]{1,0:T(8,128)} %copy-done.4) | copy-start | bytes 393220
  27.9 3.8 %copy-start.2 = (f32[512,256]{1,0:T(8,128)S(1)}, f32[512,256]{1,0:T(8,128)}, u32[]{:S(2)}) copy-start(f32[512,256]{1,0:T(8,128)} %get-tuple-element.20.own_gradient) | copy-start | bytes 1572868
  31.7 2.2 %copy-start.1 = (bf16[8192,256]{1,0:T(8,128)(2,1)S(1)}, bf16[8192,256]{1,0:T(8,128)(2,1)}, u32[]{:S(2)}) copy-start(bf16[8192,256]{1,0:T(8,128)(2,1)} %get-tuple-element.19.lags) | copy-start | bytes 12582916
  50.0 16.0 %collective-permute-start.2 = (bf16[112,512]{1,0:T(8,128)(2,1)S(1)}, bf16[112,512]{1,0:T(8,128)(2,1)S(1)}, u32[]{:S(2)}, u32[]{:S(2)}) collective-permute-start(bf16[112,512]{1,0:T(8,128)(2,1)S(1)} %get-tuple-element.24), channel_id=1, source_target_pairs={{0,8},{1,9},{2,10},{3,11},{4,12},{5,13},{6,14},{7,15},{8,0},{9,1},... | collective-permute-start | bytes 344072 | tf_op jit(solution)/shard_map/ppermute | solution.py:72
  51.4 17.8 %collective-permute-start.3 = (bf16[112,512]{1,0:T(8,128)(2,1)S(1)}, bf16[112,512]{1,0:T(8,128)(2,1)S(1)}, u32[]{:S(2)}, u32[]{:S(2)}) collective-permute-start(bf16[112,512]{1,0:T(8,128)(2,1)S(1)} %get-tuple-element.25), channel_id=1, source_target_pairs={{0,10},{1,11},{2,8},{3,9},{4,14},{5,15},{6,12},{7,13},{8,2},{9,3},... | collective-permute-start | bytes 344072 | tf_op jit(solution)/shard_map/ppermute | solution.py:72
  52.8 17.1 %collective-permute-start.4 = (bf16[112,512]{1,0:T(8,128)(2,1)S(1)}, bf16[112,512]{1,0:T(8,128)(2,1)S(1)}, u32[]{:S(2)}, u32[]{:S(2)}) collective-permute-start(bf16[112,512]{1,0:T(8,128)(2,1)S(1)} %get-tuple-element.26), channel_id=1, source_target_pairs={{0,12},{1,13},{2,14},{3,15},{4,8},{5,9},{6,10},{7,11},{8,4},{9,5},... | collective-permute-start | bytes 344072 | tf_op jit(solution)/shard_map/ppermute | solution.py:72
  56.1 16.5 %collective-permute-start.5 = (bf16[112,512]{1,0:T(8,128)(2,1)S(1)}, bf16[112,512]{1,0:T(8,128)(2,1)S(1)}, u32[]{:S(2)}, u32[]{:S(2)}) collective-permute-start(bf16[112,512]{1,0:T(8,128)(2,1)S(1)} %get-tuple-element.27), channel_id=1, source_target_pairs={{0,14},{1,15},{2,12},{3,13},{4,10},{5,11},{6,8},{7,9},{8,6},{9,7},... | collective-permute-start | bytes 344072 | tf_op jit(solution)/shard_map/ppermute | solution.py:72
  57.8 14.8 %collective-permute-start.6 = (bf16[112,512]{1,0:T(8,128)(2,1)S(1)}, bf16[112,512]{1,0:T(8,128)(2,1)S(1)}, u32[]{:S(2)}, u32[]{:S(2)}) collective-permute-start(bf16[112,512]{1,0:T(8,128)(2,1)S(1)} %get-tuple-element.28), channel_id=1, source_target_pairs={{0,6},{1,7},{2,4},{3,5},{4,2},{5,3},{6,0},{7,1},{8,14},{9,15},{10,... | collective-permute-start | bytes 344072 | tf_op jit(solution)/shard_map/ppermute | solution.py:72
  66.1 6.5 %collective-permute-start.7 = (bf16[112,512]{1,0:T(8,128)(2,1)S(1)}, bf16[112,512]{1,0:T(8,128)(2,1)S(1)}, u32[]{:S(2)}, u32[]{:S(2)}) collective-permute-start(bf16[112,512]{1,0:T(8,128)(2,1)S(1)} %get-tuple-element.29), channel_id=1, source_target_pairs={{0,4},{1,5},{2,6},{3,7},{4,0},{5,1},{6,2},{7,3},{8,12},{9,13},{10,... | collective-permute-start | bytes 344072 | tf_op jit(solution)/shard_map/ppermute | solution.py:72
  69.1 4.8 %collective-permute-start.8 = (bf16[112,512]{1,0:T(8,128)(2,1)S(1)}, bf16[112,512]{1,0:T(8,128)(2,1)S(1)}, u32[]{:S(2)}, u32[]{:S(2)}) collective-permute-start(bf16[112,512]{1,0:T(8,128)(2,1)S(1)} %get-tuple-element.30), channel_id=1, source_target_pairs={{0,2},{1,3},{2,0},{3,1},{4,6},{5,7},{6,4},{7,5},{8,10},{9,11},{10,... | collective-permute-start | bytes 344072 | tf_op jit(solution)/shard_map/ppermute | solution.py:72
  76.6 2.0 %collective-permute-start.9 = (f32[136,1024]{1,0:T(8,128)S(1)}, f32[136,1024]{1,0:T(8,128)S(1)}, u32[]{:S(2)}, u32[]{:S(2)}) collective-permute-start(f32[136,1024]{1,0:T(8,128)S(1)} %get-tuple-element.32), channel_id=1, source_target_pairs={{0,1},{1,0},{2,3},{3,2},{4,5},{5,4},{6,7},{7,6},{8,9},{9,8},{10,11... | collective-permute-start | bytes 1671176 | tf_op jit(solution)/shard_map/ppermute | solution.py:72

commit v5 on v4

--- a/solution.py
+++ b/solution.py
@@ -22,6 +22,7 @@
 F32 = jnp.float32
 BF16 = jnp.bfloat16
 PITCH = CHANNELS + 8
+CHUNKS = 2
 PEERS = 8
 OWN_LIMIT = 60 * 1024 * 1024
 VMEM_LIMIT = 36 * 1024 * 1024
@@ -144,7 +145,8 @@
     windows_of(-whole, pairs, windows)
     turn_dictionary(atoms, lags, by_atom, by_lag, loads)
     copies = fetch_lags(lags, lags_out, sems)
-    adjoint(windows, lags, gradient, [(0, width)])
+    for begin, end in row_chunks(width):
+        adjoint(windows, lags, gradient.at[pl.ds(begin, end - begin), :], [(begin, end - begin)])
     own = jnp.abs(gradient[...]) * SCALE
     folded = jnp.max(own.reshape(width // 8, 8, ATOMS), 0)
     folded = jnp.maximum(folded[:, :128], folded[:, 128:])
@@ -168,26 +170,37 @@
         copy.wait()
     whole = jnp.concatenate([left[...], middle[:, 0:ATOM_LEN], right[...]], 1)
     windows_of(-whole, pairs, windows)
-    adjoint(windows, lags, gradient, [(0, HALO), (HALO + ATOM_LEN, ATOM_LEN)])
+    adjoint(windows, lags, gradient.at[pl.ds(0, HALO), :], [(0, HALO)])
+    adjoint(windows, lags, gradient.at[pl.ds(HALO, ATOM_LEN), :], [(HALO + ATOM_LEN, ATOM_LEN)])
+
+
+def row_chunks(rows):
+    size = -(-rows // (CHUNKS * FINE)) * FINE
+    return [(low, min(low + size, rows)) for low in range(0, rows, size)]
 
 
 def forward(codes, lags, wide, spread, folded, start, rows):
-    for coarse in range(COARSE):
-        low = start - coarse * FINE
-        wide[0:rows, coarse * ATOMS : (coarse + 1) * ATOMS] = codes[low : low + rows, :]
+    keep = rows - FINE
     weights = jnp.concatenate(
         [lags[coarse * WIDE : (coarse + 1) * WIDE, :] for coarse in range(COARSE)], 1
     )
-    spread[0:rows, :] = lax.dot_general(
-        wide[0:rows, :], weights, (((1,), (1,)), ((), ())), preferred_element_type=F32
-    )
-    keep = rows - FINE
-    total = spread[FINE - 2 : FINE - 2 + keep + 2, 0:128]
-    for step in range(1, FINE // 2):
-        lanes = slice(step * 128, (step + 1) * 128)
-        low = FINE - 2 - 2 * step
-        total = total + spread[low : low + keep + 2, lanes]
-    folded[0 : keep + 2, :] = total
+    done = 0
+    for begin, end in row_chunks(rows):
+        for coarse in range(COARSE):
+            low = start + begin - coarse * FINE
+            wide[begin:end, coarse * ATOMS : (coarse + 1) * ATOMS] = codes[
+                low : low + end - begin, :
+            ]
+        spread[begin:end, :] = lax.dot_general(
+            wide[begin:end, :], weights, (((1,), (1,)), ((), ())), preferred_element_type=F32
+        )
+        until = keep + 2 if end == rows else end - FINE
+        total = spread[FINE - 2 + done : FINE - 2 + until, 0:128]
+        for step in range(1, FINE // 2):
+            low = FINE - 2 - 2 * step
+            total = total + spread[low + done : low + until, step * 128 : (step + 1) * 128]
+        folded[done:until, :] = total
+        done = until
     return folded[2 : keep + 2, 0:64] + folded[1 : keep + 1, 64:128]
 
 
@@ -241,7 +254,9 @@
     pairs[0 : rows2 - 1, 64:128] = pairs[1:rows2, 0:64]
     fill_windows(pairs, windows, rows2 - FINE)
     rows3 = width + ATOM_LEN
-    adjoint(windows, lags, spread.at[:, 0:ATOMS], [(0, rows3)])
+    for begin, end in row_chunks(rows3):
+        target = spread.at[pl.ds(begin, end - begin), 0:ATOMS]
+        adjoint(windows, lags, target, [(begin, end - begin)])
     before = codes[ATOM_LEN : ATOM_LEN + rows3, :]
     moved = before - step_size * (spread[0:rows3, 0:ATOMS] * SCALE)
     updated = jnp.where(row(ATOM_LEN, rows3) >= low, soft(moved, bound), 0.0)
@@ -326,7 +341,14 @@
         stack[coarse * atoms : (coarse + 1) * atoms, main : main + ATOM_LEN] = extra[coarse].astype(
             BF16
         )
-    return jnp.dot(stack[...], windows[...], preferred_element_type=F32)
+    half = WIDE // 2
+    return jnp.concatenate(
+        [
+            jnp.dot(stack[...], windows[:, low : low + half], preferred_element_type=F32)
+            for low in (0, half)
+        ],
+        1,
+    )
 
 
 def shared_part(pieces, stack, pairs, windows):

time: 80.9 us -> 75.5 us (0.933)
  Pallas kernels: 35.3 us -> 29.9 us
    pallas_call x1, Pallas kernels: 16.2 us -> 10.9 us  [body(): pl.pallas_call(second_kernel, out_shape=(jax.ShapeDtypeStruct((ATOMS, wid...]
  transfers between devices with their start and end apart: 11 -> 11, of which waited for: 5 -> 5; matrix products, arithmetic and copies ran while one was open for 1% -> 1% of each run, Pallas kernels for 18% -> 20%
where the time goes in v5:
time: 75.5 us; the launch traced here: 75.1 us
  Pallas kernels  29.9 us (40%)
  starting transfers between devices  21.3 us (28%)
  waiting for transfers between devices  15.3 us (20%)
  local copies, waits for them, and re-layouts  7 us (9%)
  between operations  1.62 us (2%)
    ppermute x8, waiting for transfers between devices, swapped(): return lax.ppermute(value, 'tm', [(i, i ^ bit) for i in range(count)])  13.6 us
    pallas_call x1, Pallas kernels, body(): pl.pallas_call(second_kernel, out_shape=(jax.ShapeDtypeStruct((ATOMS, wid...  10.9 us
    pallas_call x1, Pallas kernels, body(): pl.pallas_call(own_kernel, out_shape=(jax.ShapeDtypeStruct((width, ATOMS)...  9.97 us
    ppermute x8, starting transfers between devices, swapped(): return lax.ppermute(value, 'tm', [(i, i ^ bit) for i in range(count)])  8.6 us
    all_to_all x1, starting transfers between devices, body(): peak = lax.all_to_all(peak, 'tm', 0, 0, tiled=False)  8.28 us
    unnamed x14, local copies, waits for them, and re-layouts  5.94 us
    ppermute x2, starting transfers between devices, shifted(): lax.ppermute(value, axis, [(source, source + steps) for source in range(l...  4.47 us
    pallas_call x1, Pallas kernels, body(): pl.pallas_call(shared_second, out_shape=(half_rows, half_rows), in_specs=...  2.68 us
  transfers between devices with their start and end apart: 11, of which 5 were waited for; matrix products, arithmetic and copies ran while one was open for 1% of the time, Pallas kernels for 20%

profile of v5, /device:TPU:0, one launch (start us, length us, event | category | flops | bytes accessed | tf_op | source)
XLA Modules:
  0.0 75.1 jit_solution(1897163936430766772)
XLA Ops:
  0.6 0.0 copy-start.3
  0.6 1.4 %collective-permute-start.1 = (f32[64,512]{1,0:T(8,128)}, f32[64,512]{1,0:T(8,128)S(1)}, u32[]{:S(2)}, u32[]{:S(2)}) collective-permute-start(f32[64,512]{1,0:T(8,128)} %middle.5), channel_id=1, source_target_pairs={{1,0},{2,1},{3,2},{4,3},{5,4},{6,5},{7,6},{8,7},{9,8},{10,9},{11,1... | collective-permute-start | bytes 393224 | tf_op jit(solution)/shard_map/ppermute | solution.py:68
  2.1 3.0 %collective-permute-start = (f32[64,512]{1,0:T(8,128)}, f32[64,512]{1,0:T(8,128)S(1)}, u32[]{:S(2)}, u32[]{:S(2)}) collective-permute-start(f32[64,512]{1,0:T(8,128)} %middle.5), channel_id=1, source_target_pairs={{0,1},{1,2},{2,3},{3,4},{4,5},{5,6},{6,7},{7,8},{8,9},{9,10},{10,1... | collective-permute-start | bytes 393224 | tf_op jit(solution)/shard_map/ppermute | solution.py:68
  5.8 0.1 stack.43.valid
  5.9 0.0 copy-start.4
  5.9 0.6 copy-done.4
  6.5 10.0 %shard_map.58 = (f32[512,256]{1,0:T(8,128)}, f32[16,8,128]{2,1,0:T(8,128)}, bf16[8192,256]{1,0:T(8,128)(2,1)}) custom-call(f32[64,512]{1,0:T(8,128)} %middle.5, f32[64,512]{1,0:T(8,128)} %copy-done.4, bf16[256,64,128]{2,1,0:T(8,128)(2,1)} %atoms_any.1), custom_call_target="tpu_custom_call" | custom-call | flops 2147483648 | bytes 5242880 | tf_op jit(solution)/shard_map/pallas_call | solution.py:454
  16.5 0.0 copy-start.6
  16.5 8.3 %all-to-all-start = ((f32[16,8,128]{2,1,0:T(8,128)}), f32[16,8,128]{2,1,0:T(8,128)S(1)}, u32[]{:S(2)}, u32[]{:S(2)}) async-start(f32[16,8,128]{2,1,0:T(8,128)} %get-tuple-element.21), calls=%async_computation | async-start | bytes 131072 | tf_op jit(solution)/shard_map/all_to_all | solution.py:473
  24.8 0.0 collective-permute-done.left_any
  24.8 2.2 %copy-done = bf16[8192,256]{1,0:T(8,128)(2,1)S(1)} copy-done((bf16[8192,256]{1,0:T(8,128)(2,1)S(1)}, bf16[8192,256]{1,0:T(8,128)(2,1)}, u32[]{:S(2)}) %copy-start) | copy-done | bytes 4194328
  27.0 0.9 %copy-done.5 = f32[64,512]{1,0:T(8,128)S(1)} copy-done((f32[64,512]{1,0:T(8,128)S(1)}, f32[64,512]{1,0:T(8,128)}, u32[]{:S(2)}) %copy-start.5) | copy-done | bytes 131096
  27.9 2.1 %shard_map.59.border = f32[384,256]{1,0:T(8,128)S(1)} custom-call(f32[64,512]{1,0:T(8,128)S(1)} %collective-permute-done.left_any, f32[64,512]{1,0:T(8,128)S(1)} %copy-done.3, f32[64,512]{1,0:T(8,128)S(1)} %copy-done.5, bf16[8192,256]{1,0:T(8,128)(2,1)S(1)} %copy-done), custom_call_target="tpu_custom_call" | custom-call | flops 1610612736 | bytes 5242880 | tf_op jit(solution)/shard_map/pallas_call | solution.py:475
  30.0 1.7 %all-to-all-done.peak = f32[16,8,128]{2,1,0:T(8,128)S(1)} async-done(((f32[16,8,128]{2,1,0:T(8,128)}), f32[16,8,128]{2,1,0:T(8,128)S(1)}, u32[]{:S(2)}, u32[]{:S(2)}) %all-to-all-start) | async-done | bytes 65568 | tf_op jit(solution)/shard_map/all_to_all | solution.py:473
  31.7 2.2 %copy-done.1 = bf16[8192,256]{1,0:T(8,128)(2,1)S(1)} copy-done((bf16[8192,256]{1,0:T(8,128)(2,1)S(1)}, bf16[8192,256]{1,0:T(8,128)(2,1)}, u32[]{:S(2)}) %copy-start.1) | copy-done | bytes 4194328
  33.9 10.9 %shard_map.60 = (f32[256,512]{1,0:T(8,128)}, bf16[112,512]{1,0:T(8,128)(2,1)S(1)}, bf16[112,512]{1,0:T(8,128)(2,1)S(1)}, bf16[112,512]{1,0:T(8,128)(2,1)S(1)}, b...) custom-call(f32[64,512]{1,0:T(8,128)S(1)} %collective-permute-done.l, ...), custom_call_target="tpu_custom_call" | custom-call | tf_op jit(solution)/shard_map/pallas_call | solution.py:503
  44.8 1.3 %collective-permute-start.2 = (bf16[112,512]{1,0:T(8,128)(2,1)S(1)}, bf16[112,512]{1,0:T(8,128)(2,1)S(1)}, u32[]{:S(2)}, u32[]{:S(2)}) collective-permute-start(bf16[112,512]{1,0:T(8,128)(2,1)S(1)} %get-tuple-element.24), channel_id=1, source_target_pairs={{0,8},{1,9},{2,10},{3,11},{4,12},{5,13},{6,14},{7,15},{8,0},{9,1},... | collective-permute-start | bytes 344072 | tf_op jit(solution)/shard_map/ppermute | solution.py:73
  46.0 1.5 %collective-permute-start.3 = (bf16[112,512]{1,0:T(8,128)(2,1)S(1)}, bf16[112,512]{1,0:T(8,128)(2,1)S(1)}, u32[]{:S(2)}, u32[]{:S(2)}) collective-permute-start(bf16[112,512]{1,0:T(8,128)(2,1)S(1)} %get-tuple-element.25), channel_id=1, source_target_pairs={{0,10},{1,11},{2,8},{3,9},{4,14},{5,15},{6,12},{7,13},{8,2},{9,3},... | collective-permute-start | bytes 344072 | tf_op jit(solution)/shard_map/ppermute | solution.py:73
  47.5 3.3 %collective-permute-start.4 = (bf16[112,512]{1,0:T(8,128)(2,1)S(1)}, bf16[112,512]{1,0:T(8,128)(2,1)S(1)}, u32[]{:S(2)}, u32[]{:S(2)}) collective-permute-start(bf16[112,512]{1,0:T(8,128)(2,1)S(1)} %get-tuple-element.26), channel_id=1, source_target_pairs={{0,12},{1,13},{2,14},{3,15},{4,8},{5,9},{6,10},{7,11},{8,4},{9,5},... | collective-permute-start | bytes 344072 | tf_op jit(solution)/shard_map/ppermute | solution.py:73
  50.7 1.7 %collective-permute-start.5 = (bf16[112,512]{1,0:T(8,128)(2,1)S(1)}, bf16[112,512]{1,0:T(8,128)(2,1)S(1)}, u32[]{:S(2)}, u32[]{:S(2)}) collective-permute-start(bf16[112,512]{1,0:T(8,128)(2,1)S(1)} %get-tuple-element.27), channel_id=1, source_target_pairs={{0,14},{1,15},{2,12},{3,13},{4,10},{5,11},{6,8},{7,9},{8,6},{9,7},... | collective-permute-start | bytes 344072 | tf_op jit(solution)/shard_map/ppermute | solution.py:73
  52.5 0.0 collective-permute-start.6
  52.5 8.2 %collective-permute-done.2.refs_1_ = bf16[112,512]{1,0:T(8,128)(2,1)S(1)} collective-permute-done((bf16[112,512]{1,0:T(8,128)(2,1)S(1)}, bf16[112,512]{1,0:T(8,128)(2,1)S(1)}, u32[]{:S(2)}, u32[]{:S(2)}) %collective-permute-start.2) | collective-permute-done | bytes 114720 | tf_op jit(solution)/shard_map/ppermute | solution.py:73
  60.7 3.0 %collective-permute-done.3.refs_2_ = bf16[112,512]{1,0:T(8,128)(2,1)S(1)} collective-permute-done((bf16[112,512]{1,0:T(8,128)(2,1)S(1)}, bf16[112,512]{1,0:T(8,128)(2,1)S(1)}, u32[]{:S(2)}, u32[]{:S(2)}) %collective-permute-start.3) | collective-permute-done | bytes 114720 | tf_op jit(solution)/shard_map/ppermute | solution.py:73
  63.8 0.8 %collective-permute-start.8 = (bf16[112,512]{1,0:T(8,128)(2,1)S(1)}, bf16[112,512]{1,0:T(8,128)(2,1)S(1)}, u32[]{:S(2)}, u32[]{:S(2)}) collective-permute-start(bf16[112,512]{1,0:T(8,128)(2,1)S(1)} %get-tuple-element.30), channel_id=1, source_target_pairs={{0,2},{1,3},{2,0},{3,1},{4,6},{5,7},{6,4},{7,5},{8,10},{9,11},{10,... | collective-permute-start | bytes 344072 | tf_op jit(solution)/shard_map/ppermute | solution.py:73
  64.6 0.0 collective-permute-done.4.refs_3_
  64.6 2.6 %shard_map.61.before = f32[264,1024]{1,0:T(8,128)S(1)} custom-call(bf16[112,512]{1,0:T(8,128)(2,1)S(1)} %get-tuple-element.23.refs_0_, bf16[112,512]{1,0:T(8,128)(2,1)S(1)} %collective-permute-done.2.refs_1_, bf16[112,512]{1,0:T(8,128)(2,1)S(1)} %collective-permute-done.3.refs_2_, bf16[112,512]{1,0:T(8,128)(2,1)S(1)} %collective-permute-done.4.refs_3_), custom_call_target="tpu_custom_call" | custom-call | flops 1073741824 | bytes 2097152 | tf_op jit(solution)/shard_map/pallas_call | solution.py:539
  67.3 1.3 %collective-permute-done.8.refs_3_ = bf16[112,512]{1,0:T(8,128)(2,1)S(1)} collective-permute-done((bf16[112,512]{1,0:T(8,128)(2,1)S(1)}, bf16[112,512]{1,0:T(8,128)(2,1)S(1)}, u32[]{:S(2)}, u32[]{:S(2)}) %collective-permute-start.8) | collective-permute-done | bytes 114720 | tf_op jit(solution)/shard_map/ppermute | solution.py:73
  68.6 2.7 %shard_map.62 = (f32[136,1024]{1,0:T(8,128)S(1)}, f32[136,1024]{1,0:T(8,128)S(1)}) custom-call(s32[1]{0:T(128)} %bitcast.10.core, f32[264,1024]{1,0:T(8,128)S(1)} %shard_map.61.before, bf16[112,512]{1,0:T(8,128)(2,1)S(1)} %collective-permute-done.5.refs_0_, bf16[112,512]{1,0:T(8,128)(2,1)S(1)} %collective-permute-done.6.refs_1_, ...), custom_call_target="tpu_custom_call" | custom-call | flops 1073741824 | bytes 2097152 | tf_op jit(solution)/shard_map/pallas_call | solution.py:548
  71.3 0.1 collective-permute-start.9
  71.3 1.0 %constant_dynamic-slice_fusion.refs_2_ = bf16[16,64,128]{2,1,0:T(8,128)(2,1)S(1)} fusion(bf16[256,64,128]{2,1,0:T(8,128)(2,1)} %atoms_any.1, s32[]{:T(128)S(6)} %select_n.32), kind=kLoop, calls=%fused_computation | loop fusion | bytes 524292 | tf_op jit(solution)/shard_map/dynamic_slice | solution.py:493
  72.3 1.0 %collective-permute-done.9.refs_1_ = f32[136,1024]{1,0:T(8,128)S(1)} collective-permute-done((f32[136,1024]{1,0:T(8,128)S(1)}, f32[136,1024]{1,0:T(8,128)S(1)}, u32[]{:S(2)}, u32[]{:S(2)}) %collective-permute-start.9) | collective-permute-done | bytes 557088 | tf_op jit(solution)/shard_map/ppermute | solution.py:73
  73.3 1.7 %shard_map.63 = (f32[16,64,128]{2,1,0:T(8,128)}, f32[1]{0:T(128)}) custom-call(f32[136,1024]{1,0:T(8,128)S(1)} %get-tuple-element.31.refs_0_, f32[136,1024]{1,0:T(8,128)S(1)} %collective-permute-done.9.refs_1_, bf16[16,64,128]{2,1,0:T(8,128)(2,1)S(1)} %constant_dynamic-slice_fusion.refs_2_), custom_call_target="tpu_custom_call" | custom-call | tf_op jit(solution)/shard_map/pallas_call | solution.py:559
  (12 shorter events, 0.0 us)
Async XLA Ops:
  0.6 24.2 %copy-start.3 = (f32[64,512]{1,0:T(8,128)S(1)}, f32[64,512]{1,0:T(8,128)}, u32[]{:S(2)}) copy-start(f32[64,512]{1,0:T(8,128)} %middle.5) | copy-start | bytes 393220
  0.6 5.2 %collective-permute-start.1 = (f32[64,512]{1,0:T(8,128)}, f32[64,512]{1,0:T(8,128)S(1)}, u32[]{:S(2)}, u32[]{:S(2)}) collective-permute-start(f32[64,512]{1,0:T(8,128)} %middle.5), channel_id=1, source_target_pairs={{1,0},{2,1},{3,2},{4,3},{5,4},{6,5},{7,6},{8,7},{9,8},{10,9},{11,1... | collective-permute-start | bytes 393224 | tf_op jit(solution)/shard_map/ppermute | solution.py:68
  2.1 22.7 %collective-permute-start = (f32[64,512]{1,0:T(8,128)}, f32[64,512]{1,0:T(8,128)S(1)}, u32[]{:S(2)}, u32[]{:S(2)}) collective-permute-start(f32[64,512]{1,0:T(8,128)} %middle.5), channel_id=1, source_target_pairs={{0,1},{1,2},{2,3},{3,4},{4,5},{5,6},{6,7},{7,8},{8,9},{9,10},{10,1... | collective-permute-start | bytes 393224 | tf_op jit(solution)/shard_map/ppermute | solution.py:68
  5.9 0.7 copy-start.4
  16.5 15.2 %copy-start.6 = (f32[64,512]{1,0:T(8,128)S(1)}, f32[64,512]{1,0:T(8,128)}, u32[]{:S(2)}) copy-start(f32[64,512]{1,0:T(8,128)} %copy-done.4) | copy-start | bytes 393220
  16.5 15.2 %all-to-all-start = ((f32[16,8,128]{2,1,0:T(8,128)}), f32[16,8,128]{2,1,0:T(8,128)S(1)}, u32[]{:S(2)}, u32[]{:S(2)}) async-start(f32[16,8,128]{2,1,0:T(8,128)} %get-tuple-element.21), calls=%async_computation | async-start | bytes 131072 | tf_op jit(solution)/shard_map/all_to_all | solution.py:473
  24.8 2.2 %copy-start = (bf16[8192,256]{1,0:T(8,128)(2,1)S(1)}, bf16[8192,256]{1,0:T(8,128)(2,1)}, u32[]{:S(2)}) copy-start(bf16[8192,256]{1,0:T(8,128)(2,1)} %get-tuple-element.19.lags) | copy-start | bytes 12582916
  27.0 0.9 %copy-start.5 = (f32[64,512]{1,0:T(8,128)S(1)}, f32[64,512]{1,0:T(8,128)}, u32[]{:S(2)}) copy-start(f32[64,512]{1,0:T(8,128)} %copy-done.4) | copy-start | bytes 393220
  27.9 3.8 %copy-start.2 = (f32[512,256]{1,0:T(8,128)S(1)}, f32[512,256]{1,0:T(8,128)}, u32[]{:S(2)}) copy-start(f32[512,256]{1,0:T(8,128)} %get-tuple-element.20.own_gradient) | copy-start | bytes 1572868
  31.7 2.2 %copy-start.1 = (bf16[8192,256]{1,0:T(8,128)(2,1)S(1)}, bf16[8192,256]{1,0:T(8,128)(2,1)}, u32[]{:S(2)}) copy-start(bf16[8192,256]{1,0:T(8,128)(2,1)} %get-tuple-element.19.lags) | copy-start | bytes 12582916
  44.8 16.0 %collective-permute-start.2 = (bf16[112,512]{1,0:T(8,128)(2,1)S(1)}, bf16[112,512]{1,0:T(8,128)(2,1)S(1)}, u32[]{:S(2)}, u32[]{:S(2)}) collective-permute-start(bf16[112,512]{1,0:T(8,128)(2,1)S(1)} %get-tuple-element.24), channel_id=1, source_target_pairs={{0,8},{1,9},{2,10},{3,11},{4,12},{5,13},{6,14},{7,15},{8,0},{9,1},... | collective-permute-start | bytes 344072 | tf_op jit(solution)/shard_map/ppermute | solution.py:73
  46.0 17.8 %collective-permute-start.3 = (bf16[112,512]{1,0:T(8,128)(2,1)S(1)}, bf16[112,512]{1,0:T(8,128)(2,1)S(1)}, u32[]{:S(2)}, u32[]{:S(2)}) collective-permute-start(bf16[112,512]{1,0:T(8,128)(2,1)S(1)} %get-tuple-element.25), channel_id=1, source_target_pairs={{0,10},{1,11},{2,8},{3,9},{4,14},{5,15},{6,12},{7,13},{8,2},{9,3},... | collective-permute-start | bytes 344072 | tf_op jit(solution)/shard_map/ppermute | solution.py:73
  47.5 17.1 %collective-permute-start.4 = (bf16[112,512]{1,0:T(8,128)(2,1)S(1)}, bf16[112,512]{1,0:T(8,128)(2,1)S(1)}, u32[]{:S(2)}, u32[]{:S(2)}) collective-permute-start(bf16[112,512]{1,0:T(8,128)(2,1)S(1)} %get-tuple-element.26), channel_id=1, source_target_pairs={{0,12},{1,13},{2,14},{3,15},{4,8},{5,9},{6,10},{7,11},{8,4},{9,5},... | collective-permute-start | bytes 344072 | tf_op jit(solution)/shard_map/ppermute | solution.py:73
  50.7 16.5 %collective-permute-start.5 = (bf16[112,512]{1,0:T(8,128)(2,1)S(1)}, bf16[112,512]{1,0:T(8,128)(2,1)S(1)}, u32[]{:S(2)}, u32[]{:S(2)}) collective-permute-start(bf16[112,512]{1,0:T(8,128)(2,1)S(1)} %get-tuple-element.27), channel_id=1, source_target_pairs={{0,14},{1,15},{2,12},{3,13},{4,10},{5,11},{6,8},{7,9},{8,6},{9,7},... | collective-permute-start | bytes 344072 | tf_op jit(solution)/shard_map/ppermute | solution.py:73
  52.5 14.8 %collective-permute-start.6 = (bf16[112,512]{1,0:T(8,128)(2,1)S(1)}, bf16[112,512]{1,0:T(8,128)(2,1)S(1)}, u32[]{:S(2)}, u32[]{:S(2)}) collective-permute-start(bf16[112,512]{1,0:T(8,128)(2,1)S(1)} %get-tuple-element.28), channel_id=1, source_target_pairs={{0,6},{1,7},{2,4},{3,5},{4,2},{5,3},{6,0},{7,1},{8,14},{9,15},{10,... | collective-permute-start | bytes 344072 | tf_op jit(solution)/shard_map/ppermute | solution.py:73
  60.7 6.5 %collective-permute-start.7 = (bf16[112,512]{1,0:T(8,128)(2,1)S(1)}, bf16[112,512]{1,0:T(8,128)(2,1)S(1)}, u32[]{:S(2)}, u32[]{:S(2)}) collective-permute-start(bf16[112,512]{1,0:T(8,128)(2,1)S(1)} %get-tuple-element.29), channel_id=1, source_target_pairs={{0,4},{1,5},{2,6},{3,7},{4,0},{5,1},{6,2},{7,3},{8,12},{9,13},{10,... | collective-permute-start | bytes 344072 | tf_op jit(solution)/shard_map/ppermute | solution.py:73
  63.8 4.8 %collective-permute-start.8 = (bf16[112,512]{1,0:T(8,128)(2,1)S(1)}, bf16[112,512]{1,0:T(8,128)(2,1)S(1)}, u32[]{:S(2)}, u32[]{:S(2)}) collective-permute-start(bf16[112,512]{1,0:T(8,128)(2,1)S(1)} %get-tuple-element.30), channel_id=1, source_target_pairs={{0,2},{1,3},{2,0},{3,1},{4,6},{5,7},{6,4},{7,5},{8,10},{9,11},{10,... | collective-permute-start | bytes 344072 | tf_op jit(solution)/shard_map/ppermute | solution.py:73
  71.3 2.0 %collective-permute-start.9 = (f32[136,1024]{1,0:T(8,128)S(1)}, f32[136,1024]{1,0:T(8,128)S(1)}, u32[]{:S(2)}, u32[]{:S(2)}) collective-permute-start(f32[136,1024]{1,0:T(8,128)S(1)} %get-tuple-element.32), channel_id=1, source_target_pairs={{0,1},{1,0},{2,3},{3,2},{4,5},{5,4},{6,7},{7,6},{8,9},{9,8},{10,11... | collective-permute-start | bytes 1671176 | tf_op jit(solution)/shard_map/ppermute | solution.py:73

commit v6 on v5

--- a/solution.py
+++ b/solution.py
@@ -24,7 +24,7 @@
 PITCH = CHANNELS + 8
 CHUNKS = 2
 PEERS = 8
-OWN_LIMIT = 60 * 1024 * 1024
+OWN_LIMIT = 53 * 1024 * 1024
 VMEM_LIMIT = 36 * 1024 * 1024
 
 
@@ -309,6 +309,7 @@
     lane = lax.broadcasted_iota(jnp.int32, (atoms, ATOM_LEN), 1)
     extra = [jnp.zeros((atoms, ATOM_LEN), F32) for _ in range(COARSE)]
     windows[main : main + ATOM_LEN, :] = jnp.zeros((ATOM_LEN, WIDE), BF16)
+    sums = None
     for block in range(blocks):
         piece = jnp.concatenate(
             [resid_of(block).astype(F32), jnp.zeros((CHANNELS, ATOM_LEN), F32)], 1
@@ -337,17 +338,21 @@
             turned = pltpu.roll(held, (FINE * block - (start - FINE)) % length, 1)[:, :ATOM_LEN]
             inside = (lane >= FINE * block) & (lane < FINE * (block + 1))
             extra[coarse] = jnp.where(inside, turned, extra[coarse])
+        if block % 2 == 1 or block == blocks - 1:
+            begin = block // 2 * 2 * width
+            end = (block + 1) * width
+            part = jnp.dot(
+                stack[:, begin:end], windows[begin:end, :], preferred_element_type=F32
+            )
+            sums = part if sums is None else sums + part
     for coarse in range(COARSE):
         stack[coarse * atoms : (coarse + 1) * atoms, main : main + ATOM_LEN] = extra[coarse].astype(
             BF16
         )
-    half = WIDE // 2
-    return jnp.concatenate(
-        [
-            jnp.dot(stack[...], windows[:, low : low + half], preferred_element_type=F32)
-            for low in (0, half)
-        ],
-        1,
+    return sums + jnp.dot(
+        stack[:, main : main + ATOM_LEN],
+        windows[main : main + ATOM_LEN, :],
+        preferred_element_type=F32,
     )
 
 

time: 75.5 us -> 74.9 us (level)
    ppermute x8, waiting for transfers between devices: 13.6 us -> 12.6 us  [swapped(): return lax.ppermute(value, 'tm', [(i, i ^ bit) for i in range(count)])]
    all_to_all x1, waiting for transfers between devices: 1.66 us -> 2.57 us  [body(): peak = lax.all_to_all(peak, 'tm', 0, 0, tiled=False)]
    unnamed x14 -> x8, local copies, waits for them, and re-layouts: 5.94 us -> 5.27 us
  transfers between devices with their start and end apart: 11 -> 11, of which waited for: 5 -> 6; matrix products, arithmetic and copies ran while one was open for 1% -> 1% of each run, Pallas kernels for 20% -> 20%
where the time goes in v6:
time: 74.9 us; the launch traced here: 74.6 us
  Pallas kernels  29.9 us (40%)
  starting transfers between devices  21.6 us (29%)
  waiting for transfers between devices  15.1 us (20%)
  local copies, waits for them, and re-layouts  6.33 us (8%)
  between operations  1.6 us (2%)
    ppermute x8, waiting for transfers between devices, swapped(): return lax.ppermute(value, 'tm', [(i, i ^ bit) for i in range(count)])  12.6 us
    pallas_call x1, Pallas kernels, body(): pl.pallas_call(second_kernel, out_shape=(jax.ShapeDtypeStruct((ATOMS, wid...  10.8 us
    pallas_call x1, Pallas kernels, body(): pl.pallas_call(own_kernel, out_shape=(jax.ShapeDtypeStruct((width, ATOMS)...  10.4 us
    ppermute x8, starting transfers between devices, swapped(): return lax.ppermute(value, 'tm', [(i, i ^ bit) for i in range(count)])  9.09 us
    all_to_all x1, starting transfers between devices, body(): peak = lax.all_to_all(peak, 'tm', 0, 0, tiled=False)  8.15 us
    unnamed x8, local copies, waits for them, and re-layouts  5.27 us
    ppermute x2, starting transfers between devices, shifted(): lax.ppermute(value, axis, [(source, source + steps) for source in range(l...  4.33 us
    all_to_all x1, waiting for transfers between devices, body(): peak = lax.all_to_all(peak, 'tm', 0, 0, tiled=False)  2.57 us
  transfers between devices with their start and end apart: 11, of which 6 were waited for; matrix products, arithmetic and copies ran while one was open for 1% of the time, Pallas kernels for 20%

profile of v6, /device:TPU:0, one launch (start us, length us, event | category | flops | bytes accessed | tf_op | source)
XLA Modules:
  0.0 74.6 jit_solution(8709652093886785512)
XLA Ops:
  0.6 1.3 %collective-permute-start.1 = (f32[64,512]{1,0:T(8,128)}, f32[64,512]{1,0:T(8,128)S(1)}, u32[]{:S(2)}, u32[]{:S(2)}) collective-permute-start(f32[64,512]{1,0:T(8,128)} %middle.5), channel_id=1, source_target_pairs={{1,0},{2,1},{3,2},{4,3},{5,4},{6,5},{7,6},{8,7},{9,8},{10,9},{11,1... | collective-permute-start | bytes 393224 | tf_op jit(solution)/shard_map/ppermute | solution.py:68
  1.9 3.0 %collective-permute-start = (f32[64,512]{1,0:T(8,128)}, f32[64,512]{1,0:T(8,128)S(1)}, u32[]{:S(2)}, u32[]{:S(2)}) collective-permute-start(f32[64,512]{1,0:T(8,128)} %middle.5), channel_id=1, source_target_pairs={{0,1},{1,2},{2,3},{3,4},{4,5},{5,6},{6,7},{7,8},{8,9},{9,10},{10,1... | collective-permute-start | bytes 393224 | tf_op jit(solution)/shard_map/ppermute | solution.py:68
  5.7 0.1 stack.43.valid
  5.7 0.0 collective-permute-done.1.right_any
  5.7 0.0 copy-start.2
  5.8 0.9 %copy-done.2 = f32[64,512]{1,0:T(8,128)S(1)} copy-done((f32[64,512]{1,0:T(8,128)S(1)}, f32[64,512]{1,0:T(8,128)}, u32[]{:S(2)}) %copy-start.2) | copy-done | bytes 131096
  6.7 10.4 %shard_map.58 = (f32[512,256]{1,0:T(8,128)S(1)}, f32[16,8,128]{2,1,0:T(8,128)}, bf16[8192,256]{1,0:T(8,128)(2,1)}) custom-call(f32[64,512]{1,0:T(8,128)S(1)} %copy-done.2, f32[64,512]{1,0:T(8,128)S(1)} %collective-permute-done.1.right_any, bf16[256,64,128]{2,1,0:T(8,128)(2,1)} %atoms_any.1), custom_call_target="tpu_custom_call" | custom-call | flops 2147483648 | bytes 5242880 | tf_op jit(solution)/shard_map/pallas_call | solution.py:459
  17.0 8.1 %all-to-all-start = ((f32[16,8,128]{2,1,0:T(8,128)}), f32[16,8,128]{2,1,0:T(8,128)S(1)}, u32[]{:S(2)}, u32[]{:S(2)}) async-start(f32[16,8,128]{2,1,0:T(8,128)} %get-tuple-element.21), calls=%async_computation | async-start | bytes 131072 | tf_op jit(solution)/shard_map/all_to_all | solution.py:478
  25.2 0.0 collective-permute-done.left_any
  25.2 2.2 %copy-done = bf16[8192,256]{1,0:T(8,128)(2,1)S(1)} copy-done((bf16[8192,256]{1,0:T(8,128)(2,1)S(1)}, bf16[8192,256]{1,0:T(8,128)(2,1)}, u32[]{:S(2)}) %copy-start) | copy-done | bytes 4194328
  27.4 2.1 %shard_map.59.border = f32[384,256]{1,0:T(8,128)S(1)} custom-call(f32[64,512]{1,0:T(8,128)S(1)} %collective-permute-done.left_any, f32[64,512]{1,0:T(8,128)S(1)} %copy-done.3, f32[64,512]{1,0:T(8,128)S(1)} %collective-permute-done.1.right_any, bf16[8192,256]{1,0:T(8,128)(2,1)S(1)} %copy-done), custom_call_target="tpu_custom_call" | custom-call | flops 1610612736 | bytes 5242880 | tf_op jit(solution)/shard_map/pallas_call | solution.py:480
  29.5 2.6 %all-to-all-done.peak = f32[16,8,128]{2,1,0:T(8,128)S(1)} async-done(((f32[16,8,128]{2,1,0:T(8,128)}), f32[16,8,128]{2,1,0:T(8,128)S(1)}, u32[]{:S(2)}, u32[]{:S(2)}) %all-to-all-start) | async-done | bytes 65568 | tf_op jit(solution)/shard_map/all_to_all | solution.py:478
  32.1 2.2 %copy-done.1 = bf16[8192,256]{1,0:T(8,128)(2,1)S(1)} copy-done((bf16[8192,256]{1,0:T(8,128)(2,1)S(1)}, bf16[8192,256]{1,0:T(8,128)(2,1)}, u32[]{:S(2)}) %copy-start.1) | copy-done | bytes 4194328
  34.3 10.8 %shard_map.60 = (f32[256,512]{1,0:T(8,128)}, bf16[112,512]{1,0:T(8,128)(2,1)S(1)}, bf16[112,512]{1,0:T(8,128)(2,1)S(1)}, bf16[112,512]{1,0:T(8,128)(2,1)S(1)}, b...) custom-call(f32[64,512]{1,0:T(8,128)S(1)} %collective-permute-done.l, ...), custom_call_target="tpu_custom_call" | custom-call | tf_op jit(solution)/shard_map/pallas_call | solution.py:508
  45.1 0.3 collective-permute-start.2
  45.5 2.2 %collective-permute-start.3 = (bf16[112,512]{1,0:T(8,128)(2,1)S(1)}, bf16[112,512]{1,0:T(8,128)(2,1)S(1)}, u32[]{:S(2)}, u32[]{:S(2)}) collective-permute-start(bf16[112,512]{1,0:T(8,128)(2,1)S(1)} %get-tuple-element.25), channel_id=1, source_target_pairs={{0,10},{1,11},{2,8},{3,9},{4,14},{5,15},{6,12},{7,13},{8,2},{9,3},... | collective-permute-start | bytes 344072 | tf_op jit(solution)/shard_map/ppermute | solution.py:73
  47.7 2.5 %collective-permute-start.4 = (bf16[112,512]{1,0:T(8,128)(2,1)S(1)}, bf16[112,512]{1,0:T(8,128)(2,1)S(1)}, u32[]{:S(2)}, u32[]{:S(2)}) collective-permute-start(bf16[112,512]{1,0:T(8,128)(2,1)S(1)} %get-tuple-element.26), channel_id=1, source_target_pairs={{0,12},{1,13},{2,14},{3,15},{4,8},{5,9},{6,10},{7,11},{8,4},{9,5},... | collective-permute-start | bytes 344072 | tf_op jit(solution)/shard_map/ppermute | solution.py:73
  50.2 2.7 %collective-permute-start.5 = (bf16[112,512]{1,0:T(8,128)(2,1)S(1)}, bf16[112,512]{1,0:T(8,128)(2,1)S(1)}, u32[]{:S(2)}, u32[]{:S(2)}) collective-permute-start(bf16[112,512]{1,0:T(8,128)(2,1)S(1)} %get-tuple-element.27), channel_id=1, source_target_pairs={{0,14},{1,15},{2,12},{3,13},{4,10},{5,11},{6,8},{7,9},{8,6},{9,7},... | collective-permute-start | bytes 344072 | tf_op jit(solution)/shard_map/ppermute | solution.py:73
  52.8 0.0 collective-permute-start.6
  52.8 8.0 %collective-permute-done.2.refs_1_ = bf16[112,512]{1,0:T(8,128)(2,1)S(1)} collective-permute-done((bf16[112,512]{1,0:T(8,128)(2,1)S(1)}, bf16[112,512]{1,0:T(8,128)(2,1)S(1)}, u32[]{:S(2)}, u32[]{:S(2)}) %collective-permute-start.2) | collective-permute-done | bytes 114720 | tf_op jit(solution)/shard_map/ppermute | solution.py:73
  60.9 0.0 collective-permute-start.7
  60.9 2.6 %collective-permute-done.3.refs_2_ = bf16[112,512]{1,0:T(8,128)(2,1)S(1)} collective-permute-done((bf16[112,512]{1,0:T(8,128)(2,1)S(1)}, bf16[112,512]{1,0:T(8,128)(2,1)S(1)}, u32[]{:S(2)}, u32[]{:S(2)}) %collective-permute-start.3) | collective-permute-done | bytes 114720 | tf_op jit(solution)/shard_map/ppermute | solution.py:73
  63.4 1.3 %collective-permute-start.8 = (bf16[112,512]{1,0:T(8,128)(2,1)S(1)}, bf16[112,512]{1,0:T(8,128)(2,1)S(1)}, u32[]{:S(2)}, u32[]{:S(2)}) collective-permute-start(bf16[112,512]{1,0:T(8,128)(2,1)S(1)} %get-tuple-element.30), channel_id=1, source_target_pairs={{0,2},{1,3},{2,0},{3,1},{4,6},{5,7},{6,4},{7,5},{8,10},{9,11},{10,... | collective-permute-start | bytes 344072 | tf_op jit(solution)/shard_map/ppermute | solution.py:73
  64.7 0.0 collective-permute-done.4.refs_3_
  64.7 2.4 %shard_map.61.before = f32[264,1024]{1,0:T(8,128)S(1)} custom-call(bf16[112,512]{1,0:T(8,128)(2,1)S(1)} %get-tuple-element.23.refs_0_, bf16[112,512]{1,0:T(8,128)(2,1)S(1)} %collective-permute-done.2.refs_1_, bf16[112,512]{1,0:T(8,128)(2,1)S(1)} %collective-permute-done.3.refs_2_, bf16[112,512]{1,0:T(8,128)(2,1)S(1)} %collective-permute-done.4.refs_3_), custom_call_target="tpu_custom_call" | custom-call | flops 1073741824 | bytes 2097152 | tf_op jit(solution)/shard_map/pallas_call | solution.py:544
  67.2 0.6 collective-permute-done.7.refs_2_
  67.8 0.4 collective-permute-done.8.refs_3_
  68.2 2.5 %shard_map.62 = (f32[136,1024]{1,0:T(8,128)S(1)}, f32[136,1024]{1,0:T(8,128)S(1)}) custom-call(s32[1]{0:T(128)} %bitcast.10.core, f32[264,1024]{1,0:T(8,128)S(1)} %shard_map.61.before, bf16[112,512]{1,0:T(8,128)(2,1)S(1)} %collective-permute-done.5.refs_0_, bf16[112,512]{1,0:T(8,128)(2,1)S(1)} %collective-permute-done.6.refs_1_, ...), custom_call_target="tpu_custom_call" | custom-call | flops 1073741824 | bytes 2097152 | tf_op jit(solution)/shard_map/pallas_call | solution.py:553
  70.7 0.1 collective-permute-start.9
  70.8 1.0 %constant_dynamic-slice_fusion.refs_2_ = bf16[16,64,128]{2,1,0:T(8,128)(2,1)S(1)} fusion(bf16[256,64,128]{2,1,0:T(8,128)(2,1)} %atoms_any.1, s32[]{:T(128)S(6)} %select_n.32), kind=kLoop, calls=%fused_computation | loop fusion | bytes 524292 | tf_op jit(solution)/shard_map/dynamic_slice | solution.py:498
  71.8 1.0 %collective-permute-done.9.refs_1_ = f32[136,1024]{1,0:T(8,128)S(1)} collective-permute-done((f32[136,1024]{1,0:T(8,128)S(1)}, f32[136,1024]{1,0:T(8,128)S(1)}, u32[]{:S(2)}, u32[]{:S(2)}) %collective-permute-start.9) | collective-permute-done | bytes 557088 | tf_op jit(solution)/shard_map/ppermute | solution.py:73
  72.7 1.7 %shard_map.63 = (f32[16,64,128]{2,1,0:T(8,128)}, f32[1]{0:T(128)}) custom-call(f32[136,1024]{1,0:T(8,128)S(1)} %get-tuple-element.31.refs_0_, f32[136,1024]{1,0:T(8,128)S(1)} %collective-permute-done.9.refs_1_, bf16[16,64,128]{2,1,0:T(8,128)(2,1)S(1)} %constant_dynamic-slice_fusion.refs_2_), custom_call_target="tpu_custom_call" | custom-call | tf_op jit(solution)/shard_map/pallas_call | solution.py:564
  (6 shorter events, 0.0 us)
Async XLA Ops:
  0.6 5.1 %collective-permute-start.1 = (f32[64,512]{1,0:T(8,128)}, f32[64,512]{1,0:T(8,128)S(1)}, u32[]{:S(2)}, u32[]{:S(2)}) collective-permute-start(f32[64,512]{1,0:T(8,128)} %middle.5), channel_id=1, source_target_pairs={{1,0},{2,1},{3,2},{4,3},{5,4},{6,5},{7,6},{8,7},{9,8},{10,9},{11,1... | collective-permute-start | bytes 393224 | tf_op jit(solution)/shard_map/ppermute | solution.py:68
  1.9 23.3 %collective-permute-start = (f32[64,512]{1,0:T(8,128)}, f32[64,512]{1,0:T(8,128)S(1)}, u32[]{:S(2)}, u32[]{:S(2)}) collective-permute-start(f32[64,512]{1,0:T(8,128)} %middle.5), channel_id=1, source_target_pairs={{0,1},{1,2},{2,3},{3,4},{4,5},{5,6},{6,7},{7,8},{8,9},{9,10},{10,1... | collective-permute-start | bytes 393224 | tf_op jit(solution)/shard_map/ppermute | solution.py:68
  5.7 0.9 %copy-start.2 = (f32[64,512]{1,0:T(8,128)S(1)}, f32[64,512]{1,0:T(8,128)}, u32[]{:S(2)}) copy-start(f32[64,512]{1,0:T(8,128)} %middle.5) | copy-start | bytes 393220
  6.7 18.5 %copy-start.3 = (f32[64,512]{1,0:T(8,128)S(1)}, f32[64,512]{1,0:T(8,128)}, u32[]{:S(2)}) copy-start(f32[64,512]{1,0:T(8,128)} %middle.5) | copy-start | bytes 393220
  17.0 15.1 %all-to-all-start = ((f32[16,8,128]{2,1,0:T(8,128)}), f32[16,8,128]{2,1,0:T(8,128)S(1)}, u32[]{:S(2)}, u32[]{:S(2)}) async-start(f32[16,8,128]{2,1,0:T(8,128)} %get-tuple-element.21), calls=%async_computation | async-start | bytes 131072 | tf_op jit(solution)/shard_map/all_to_all | solution.py:478
  25.2 2.2 %copy-start = (bf16[8192,256]{1,0:T(8,128)(2,1)S(1)}, bf16[8192,256]{1,0:T(8,128)(2,1)}, u32[]{:S(2)}) copy-start(bf16[8192,256]{1,0:T(8,128)(2,1)} %get-tuple-element.19.lags) | copy-start | bytes 12582916
  32.1 2.2 %copy-start.1 = (bf16[8192,256]{1,0:T(8,128)(2,1)S(1)}, bf16[8192,256]{1,0:T(8,128)(2,1)}, u32[]{:S(2)}) copy-start(bf16[8192,256]{1,0:T(8,128)(2,1)} %get-tuple-element.19.lags) | copy-start | bytes 12582916
  45.1 15.7 %collective-permute-start.2 = (bf16[112,512]{1,0:T(8,128)(2,1)S(1)}, bf16[112,512]{1,0:T(8,128)(2,1)S(1)}, u32[]{:S(2)}, u32[]{:S(2)}) collective-permute-start(bf16[112,512]{1,0:T(8,128)(2,1)S(1)} %get-tuple-element.24), channel_id=1, source_target_pairs={{0,8},{1,9},{2,10},{3,11},{4,12},{5,13},{6,14},{7,15},{8,0},{9,1},... | collective-permute-start | bytes 344072 | tf_op jit(solution)/shard_map/ppermute | solution.py:73
  45.5 18.0 %collective-permute-start.3 = (bf16[112,512]{1,0:T(8,128)(2,1)S(1)}, bf16[112,512]{1,0:T(8,128)(2,1)S(1)}, u32[]{:S(2)}, u32[]{:S(2)}) collective-permute-start(bf16[112,512]{1,0:T(8,128)(2,1)S(1)} %get-tuple-element.25), channel_id=1, source_target_pairs={{0,10},{1,11},{2,8},{3,9},{4,14},{5,15},{6,12},{7,13},{8,2},{9,3},... | collective-permute-start | bytes 344072 | tf_op jit(solution)/shard_map/ppermute | solution.py:73
  47.7 17.0 %collective-permute-start.4 = (bf16[112,512]{1,0:T(8,128)(2,1)S(1)}, bf16[112,512]{1,0:T(8,128)(2,1)S(1)}, u32[]{:S(2)}, u32[]{:S(2)}) collective-permute-start(bf16[112,512]{1,0:T(8,128)(2,1)S(1)} %get-tuple-element.26), channel_id=1, source_target_pairs={{0,12},{1,13},{2,14},{3,15},{4,8},{5,9},{6,10},{7,11},{8,4},{9,5},... | collective-permute-start | bytes 344072 | tf_op jit(solution)/shard_map/ppermute | solution.py:73
  50.2 17.0 %collective-permute-start.5 = (bf16[112,512]{1,0:T(8,128)(2,1)S(1)}, bf16[112,512]{1,0:T(8,128)(2,1)S(1)}, u32[]{:S(2)}, u32[]{:S(2)}) collective-permute-start(bf16[112,512]{1,0:T(8,128)(2,1)S(1)} %get-tuple-element.27), channel_id=1, source_target_pairs={{0,14},{1,15},{2,12},{3,13},{4,10},{5,11},{6,8},{7,9},{8,6},{9,7},... | collective-permute-start | bytes 344072 | tf_op jit(solution)/shard_map/ppermute | solution.py:73
  52.8 14.3 %collective-permute-start.6 = (bf16[112,512]{1,0:T(8,128)(2,1)S(1)}, bf16[112,512]{1,0:T(8,128)(2,1)S(1)}, u32[]{:S(2)}, u32[]{:S(2)}) collective-permute-start(bf16[112,512]{1,0:T(8,128)(2,1)S(1)} %get-tuple-element.28), channel_id=1, source_target_pairs={{0,6},{1,7},{2,4},{3,5},{4,2},{5,3},{6,0},{7,1},{8,14},{9,15},{10,... | collective-permute-start | bytes 344072 | tf_op jit(solution)/shard_map/ppermute | solution.py:73
  60.9 6.9 %collective-permute-start.7 = (bf16[112,512]{1,0:T(8,128)(2,1)S(1)}, bf16[112,512]{1,0:T(8,128)(2,1)S(1)}, u32[]{:S(2)}, u32[]{:S(2)}) collective-permute-start(bf16[112,512]{1,0:T(8,128)(2,1)S(1)} %get-tuple-element.29), channel_id=1, source_target_pairs={{0,4},{1,5},{2,6},{3,7},{4,0},{5,1},{6,2},{7,3},{8,12},{9,13},{10,... | collective-permute-start | bytes 344072 | tf_op jit(solution)/shard_map/ppermute | solution.py:73
  63.4 4.8 %collective-permute-start.8 = (bf16[112,512]{1,0:T(8,128)(2,1)S(1)}, bf16[112,512]{1,0:T(8,128)(2,1)S(1)}, u32[]{:S(2)}, u32[]{:S(2)}) collective-permute-start(bf16[112,512]{1,0:T(8,128)(2,1)S(1)} %get-tuple-element.30), channel_id=1, source_target_pairs={{0,2},{1,3},{2,0},{3,1},{4,6},{5,7},{6,4},{7,5},{8,10},{9,11},{10,... | collective-permute-start | bytes 344072 | tf_op jit(solution)/shard_map/ppermute | solution.py:73
  70.7 2.0 %collective-permute-start.9 = (f32[136,1024]{1,0:T(8,128)S(1)}, f32[136,1024]{1,0:T(8,128)S(1)}, u32[]{:S(2)}, u32[]{:S(2)}) collective-permute-start(f32[136,1024]{1,0:T(8,128)S(1)} %get-tuple-element.32), channel_id=1, source_target_pairs={{0,1},{1,0},{2,3},{3,2},{4,5},{5,4},{6,7},{7,6},{8,9},{9,8},{10,11... | collective-permute-start | bytes 1671176 | tf_op jit(solution)/shard_map/ppermute | solution.py:73

commit v7 on v6

--- a/solution.py
+++ b/solution.py
@@ -338,13 +338,9 @@
             turned = pltpu.roll(held, (FINE * block - (start - FINE)) % length, 1)[:, :ATOM_LEN]
             inside = (lane >= FINE * block) & (lane < FINE * (block + 1))
             extra[coarse] = jnp.where(inside, turned, extra[coarse])
-        if block % 2 == 1 or block == blocks - 1:
-            begin = block // 2 * 2 * width
-            end = (block + 1) * width
-            part = jnp.dot(
-                stack[:, begin:end], windows[begin:end, :], preferred_element_type=F32
-            )
-            sums = part if sums is None else sums + part
+        begin, end = block * width, (block + 1) * width
+        part = jnp.dot(stack[:, begin:end], windows[begin:end, :], preferred_element_type=F32)
+        sums = part if sums is None else sums + part
     for coarse in range(COARSE):
         stack[coarse * atoms : (coarse + 1) * atoms, main : main + ATOM_LEN] = extra[coarse].astype(
             BF16

time: 74.9 us -> 75 us (level)
  no operation moved by 1% of the time
where the time goes in v7:
time: 75 us; the launch traced here: 74.7 us
  Pallas kernels  30.1 us (40%)
  starting transfers between devices  21.6 us (29%)
  waiting for transfers between devices  15.1 us (20%)
  local copies, waits for them, and re-layouts  6.33 us (8%)
  between operations  1.6 us (2%)
    ppermute x8, waiting for transfers between devices, swapped(): return lax.ppermute(value, 'tm', [(i, i ^ bit) for i in range(count)])  12.5 us
    pallas_call x1, Pallas kernels, body(): pl.pallas_call(second_kernel, out_shape=(jax.ShapeDtypeStruct((ATOMS, wid...  10.8 us
    pallas_call x1, Pallas kernels, body(): pl.pallas_call(own_kernel, out_shape=(jax.ShapeDtypeStruct((width, ATOMS)...  10.4 us
    ppermute x8, starting transfers between devices, swapped(): return lax.ppermute(value, 'tm', [(i, i ^ bit) for i in range(count)])  9.09 us
    all_to_all x1, starting transfers between devices, body(): peak = lax.all_to_all(peak, 'tm', 0, 0, tiled=False)  8.15 us
    unnamed x8, local copies, waits for them, and re-layouts  5.27 us
    ppermute x2, starting transfers between devices, shifted(): lax.ppermute(value, axis, [(source, source + steps) for source in range(l...  4.33 us
    pallas_call x1, Pallas kernels, body(): pl.pallas_call(shared_second, out_shape=(half_rows, half_rows), in_specs=...  2.58 us
  transfers between devices with their start and end apart: 11, of which 6 were waited for; matrix products, arithmetic and copies ran while one was open for 1% of the time, Pallas kernels for 20%

profile of v7, /device:TPU:0, one launch (start us, length us, event | category | flops | bytes accessed | tf_op | source)
XLA Modules:
  0.0 74.7 jit_solution(15686203552335283610)
XLA Ops:
  0.6 1.3 %collective-permute-start.1 = (f32[64,512]{1,0:T(8,128)}, f32[64,512]{1,0:T(8,128)S(1)}, u32[]{:S(2)}, u32[]{:S(2)}) collective-permute-start(f32[64,512]{1,0:T(8,128)} %middle.5), channel_id=1, source_target_pairs={{1,0},{2,1},{3,2},{4,3},{5,4},{6,5},{7,6},{8,7},{9,8},{10,9},{11,1... | collective-permute-start | bytes 393224 | tf_op jit(solution)/shard_map/ppermute | solution.py:68
  1.9 3.0 %collective-permute-start = (f32[64,512]{1,0:T(8,128)}, f32[64,512]{1,0:T(8,128)S(1)}, u32[]{:S(2)}, u32[]{:S(2)}) collective-permute-start(f32[64,512]{1,0:T(8,128)} %middle.5), channel_id=1, source_target_pairs={{0,1},{1,2},{2,3},{3,4},{4,5},{5,6},{6,7},{7,8},{8,9},{9,10},{10,1... | collective-permute-start | bytes 393224 | tf_op jit(solution)/shard_map/ppermute | solution.py:68
  5.7 0.1 stack.43.valid
  5.7 0.0 collective-permute-done.1.right_any
  5.7 0.0 copy-start.2
  5.8 0.9 %copy-done.2 = f32[64,512]{1,0:T(8,128)S(1)} copy-done((f32[64,512]{1,0:T(8,128)S(1)}, f32[64,512]{1,0:T(8,128)}, u32[]{:S(2)}) %copy-start.2) | copy-done | bytes 131096
  6.7 10.4 %shard_map.58 = (f32[512,256]{1,0:T(8,128)S(1)}, f32[16,8,128]{2,1,0:T(8,128)}, bf16[8192,256]{1,0:T(8,128)(2,1)}) custom-call(f32[64,512]{1,0:T(8,128)S(1)} %copy-done.2, f32[64,512]{1,0:T(8,128)S(1)} %collective-permute-done.1.right_any, bf16[256,64,128]{2,1,0:T(8,128)(2,1)} %atoms_any.1), custom_call_target="tpu_custom_call" | custom-call | flops 2147483648 | bytes 5242880 | tf_op jit(solution)/shard_map/pallas_call | solution.py:455
  17.0 8.1 %all-to-all-start = ((f32[16,8,128]{2,1,0:T(8,128)}), f32[16,8,128]{2,1,0:T(8,128)S(1)}, u32[]{:S(2)}, u32[]{:S(2)}) async-start(f32[16,8,128]{2,1,0:T(8,128)} %get-tuple-element.21), calls=%async_computation | async-start | bytes 131072 | tf_op jit(solution)/shard_map/all_to_all | solution.py:474
  25.2 2.2 %copy-done = bf16[8192,256]{1,0:T(8,128)(2,1)S(1)} copy-done((bf16[8192,256]{1,0:T(8,128)(2,1)S(1)}, bf16[8192,256]{1,0:T(8,128)(2,1)}, u32[]{:S(2)}) %copy-start) | copy-done | bytes 4194328
  27.4 2.1 %shard_map.59.border = f32[384,256]{1,0:T(8,128)S(1)} custom-call(f32[64,512]{1,0:T(8,128)S(1)} %collective-permute-done.left_any, f32[64,512]{1,0:T(8,128)S(1)} %copy-done.3, f32[64,512]{1,0:T(8,128)S(1)} %collective-permute-done.1.right_any, bf16[8192,256]{1,0:T(8,128)(2,1)S(1)} %copy-done), custom_call_target="tpu_custom_call" | custom-call | flops 1610612736 | bytes 5242880 | tf_op jit(solution)/shard_map/pallas_call | solution.py:476
  29.5 2.6 %all-to-all-done.peak = f32[16,8,128]{2,1,0:T(8,128)S(1)} async-done(((f32[16,8,128]{2,1,0:T(8,128)}), f32[16,8,128]{2,1,0:T(8,128)S(1)}, u32[]{:S(2)}, u32[]{:S(2)}) %all-to-all-start) | async-done | bytes 65568 | tf_op jit(solution)/shard_map/all_to_all | solution.py:474
  32.1 2.2 %copy-done.1 = bf16[8192,256]{1,0:T(8,128)(2,1)S(1)} copy-done((bf16[8192,256]{1,0:T(8,128)(2,1)S(1)}, bf16[8192,256]{1,0:T(8,128)(2,1)}, u32[]{:S(2)}) %copy-start.1) | copy-done | bytes 4194328
  34.3 10.8 %shard_map.60 = (f32[256,512]{1,0:T(8,128)}, bf16[112,512]{1,0:T(8,128)(2,1)S(1)}, bf16[112,512]{1,0:T(8,128)(2,1)S(1)}, bf16[112,512]{1,0:T(8,128)(2,1)S(1)}, b...) custom-call(f32[64,512]{1,0:T(8,128)S(1)} %collective-permute-done.l, ...), custom_call_target="tpu_custom_call" | custom-call | tf_op jit(solution)/shard_map/pallas_call | solution.py:504
  45.1 0.3 collective-permute-start.2
  45.5 2.2 %collective-permute-start.3 = (bf16[112,512]{1,0:T(8,128)(2,1)S(1)}, bf16[112,512]{1,0:T(8,128)(2,1)S(1)}, u32[]{:S(2)}, u32[]{:S(2)}) collective-permute-start(bf16[112,512]{1,0:T(8,128)(2,1)S(1)} %get-tuple-element.25), channel_id=1, source_target_pairs={{0,10},{1,11},{2,8},{3,9},{4,14},{5,15},{6,12},{7,13},{8,2},{9,3},... | collective-permute-start | bytes 344072 | tf_op jit(solution)/shard_map/ppermute | solution.py:73
  47.7 2.5 %collective-permute-start.4 = (bf16[112,512]{1,0:T(8,128)(2,1)S(1)}, bf16[112,512]{1,0:T(8,128)(2,1)S(1)}, u32[]{:S(2)}, u32[]{:S(2)}) collective-permute-start(bf16[112,512]{1,0:T(8,128)(2,1)S(1)} %get-tuple-element.26), channel_id=1, source_target_pairs={{0,12},{1,13},{2,14},{3,15},{4,8},{5,9},{6,10},{7,11},{8,4},{9,5},... | collective-permute-start | bytes 344072 | tf_op jit(solution)/shard_map/ppermute | solution.py:73
  50.2 2.7 %collective-permute-start.5 = (bf16[112,512]{1,0:T(8,128)(2,1)S(1)}, bf16[112,512]{1,0:T(8,128)(2,1)S(1)}, u32[]{:S(2)}, u32[]{:S(2)}) collective-permute-start(bf16[112,512]{1,0:T(8,128)(2,1)S(1)} %get-tuple-element.27), channel_id=1, source_target_pairs={{0,14},{1,15},{2,12},{3,13},{4,10},{5,11},{6,8},{7,9},{8,6},{9,7},... | collective-permute-start | bytes 344072 | tf_op jit(solution)/shard_map/ppermute | solution.py:73
  52.8 0.0 collective-permute-start.6
  52.8 8.0 %collective-permute-done.2.refs_1_ = bf16[112,512]{1,0:T(8,128)(2,1)S(1)} collective-permute-done((bf16[112,512]{1,0:T(8,128)(2,1)S(1)}, bf16[112,512]{1,0:T(8,128)(2,1)S(1)}, u32[]{:S(2)}, u32[]{:S(2)}) %collective-permute-start.2) | collective-permute-done | bytes 114720 | tf_op jit(solution)/shard_map/ppermute | solution.py:73
  60.9 2.6 %collective-permute-done.3.refs_2_ = bf16[112,512]{1,0:T(8,128)(2,1)S(1)} collective-permute-done((bf16[112,512]{1,0:T(8,128)(2,1)S(1)}, bf16[112,512]{1,0:T(8,128)(2,1)S(1)}, u32[]{:S(2)}, u32[]{:S(2)}) %collective-permute-start.3) | collective-permute-done | bytes 114720 | tf_op jit(solution)/shard_map/ppermute | solution.py:73
  63.4 1.3 %collective-permute-start.8 = (bf16[112,512]{1,0:T(8,128)(2,1)S(1)}, bf16[112,512]{1,0:T(8,128)(2,1)S(1)}, u32[]{:S(2)}, u32[]{:S(2)}) collective-permute-start(bf16[112,512]{1,0:T(8,128)(2,1)S(1)} %get-tuple-element.30), channel_id=1, source_target_pairs={{0,2},{1,3},{2,0},{3,1},{4,6},{5,7},{6,4},{7,5},{8,10},{9,11},{10,... | collective-permute-start | bytes 344072 | tf_op jit(solution)/shard_map/ppermute | solution.py:73
  64.7 0.0 collective-permute-done.4.refs_3_
  64.7 2.5 %shard_map.61.before = f32[264,1024]{1,0:T(8,128)S(1)} custom-call(bf16[112,512]{1,0:T(8,128)(2,1)S(1)} %get-tuple-element.23.refs_0_, bf16[112,512]{1,0:T(8,128)(2,1)S(1)} %collective-permute-done.2.refs_1_, bf16[112,512]{1,0:T(8,128)(2,1)S(1)} %collective-permute-done.3.refs_2_, bf16[112,512]{1,0:T(8,128)(2,1)S(1)} %collective-permute-done.4.refs_3_), custom_call_target="tpu_custom_call" | custom-call | flops 1073741824 | bytes 2097152 | tf_op jit(solution)/shard_map/pallas_call | solution.py:540
  67.2 0.0 collective-permute-done.5.refs_0_
  67.2 0.0 collective-permute-done.6.refs_1_
  67.3 0.5 collective-permute-done.7.refs_2_
  67.8 0.4 collective-permute-done.8.refs_3_
  68.2 2.6 %shard_map.62 = (f32[136,1024]{1,0:T(8,128)S(1)}, f32[136,1024]{1,0:T(8,128)S(1)}) custom-call(s32[1]{0:T(128)} %bitcast.10.core, f32[264,1024]{1,0:T(8,128)S(1)} %shard_map.61.before, bf16[112,512]{1,0:T(8,128)(2,1)S(1)} %collective-permute-done.5.refs_0_, bf16[112,512]{1,0:T(8,128)(2,1)S(1)} %collective-permute-done.6.refs_1_, ...), custom_call_target="tpu_custom_call" | custom-call | flops 1073741824 | bytes 2097152 | tf_op jit(solution)/shard_map/pallas_call | solution.py:549
  70.8 0.1 collective-permute-start.9
  70.9 1.0 %constant_dynamic-slice_fusion.refs_2_ = bf16[16,64,128]{2,1,0:T(8,128)(2,1)S(1)} fusion(bf16[256,64,128]{2,1,0:T(8,128)(2,1)} %atoms_any.1, s32[]{:T(128)S(6)} %select_n.32), kind=kLoop, calls=%fused_computation | loop fusion | bytes 524292 | tf_op jit(solution)/shard_map/dynamic_slice | solution.py:494
  71.9 1.0 %collective-permute-done.9.refs_1_ = f32[136,1024]{1,0:T(8,128)S(1)} collective-permute-done((f32[136,1024]{1,0:T(8,128)S(1)}, f32[136,1024]{1,0:T(8,128)S(1)}, u32[]{:S(2)}, u32[]{:S(2)}) %collective-permute-start.9) | collective-permute-done | bytes 557088 | tf_op jit(solution)/shard_map/ppermute | solution.py:73
  72.8 1.7 %shard_map.63 = (f32[16,64,128]{2,1,0:T(8,128)}, f32[1]{0:T(128)}) custom-call(f32[136,1024]{1,0:T(8,128)S(1)} %get-tuple-element.31.refs_0_, f32[136,1024]{1,0:T(8,128)S(1)} %collective-permute-done.9.refs_1_, bf16[16,64,128]{2,1,0:T(8,128)(2,1)S(1)} %constant_dynamic-slice_fusion.refs_2_), custom_call_target="tpu_custom_call" | custom-call | tf_op jit(solution)/shard_map/pallas_call | solution.py:560
  (6 shorter events, 0.0 us)
Async XLA Ops:
  0.6 5.1 %collective-permute-start.1 = (f32[64,512]{1,0:T(8,128)}, f32[64,512]{1,0:T(8,128)S(1)}, u32[]{:S(2)}, u32[]{:S(2)}) collective-permute-start(f32[64,512]{1,0:T(8,128)} %middle.5), channel_id=1, source_target_pairs={{1,0},{2,1},{3,2},{4,3},{5,4},{6,5},{7,6},{8,7},{9,8},{10,9},{11,1... | collective-permute-start | bytes 393224 | tf_op jit(solution)/shard_map/ppermute | solution.py:68
  1.9 23.3 %collective-permute-start = (f32[64,512]{1,0:T(8,128)}, f32[64,512]{1,0:T(8,128)S(1)}, u32[]{:S(2)}, u32[]{:S(2)}) collective-permute-start(f32[64,512]{1,0:T(8,128)} %middle.5), channel_id=1, source_target_pairs={{0,1},{1,2},{2,3},{3,4},{4,5},{5,6},{6,7},{7,8},{8,9},{9,10},{10,1... | collective-permute-start | bytes 393224 | tf_op jit(solution)/shard_map/ppermute | solution.py:68
  5.7 0.9 %copy-start.2 = (f32[64,512]{1,0:T(8,128)S(1)}, f32[64,512]{1,0:T(8,128)}, u32[]{:S(2)}) copy-start(f32[64,512]{1,0:T(8,128)} %middle.5) | copy-start | bytes 393220
  6.7 18.5 %copy-start.3 = (f32[64,512]{1,0:T(8,128)S(1)}, f32[64,512]{1,0:T(8,128)}, u32[]{:S(2)}) copy-start(f32[64,512]{1,0:T(8,128)} %middle.5) | copy-start | bytes 393220
  17.0 15.1 %all-to-all-start = ((f32[16,8,128]{2,1,0:T(8,128)}), f32[16,8,128]{2,1,0:T(8,128)S(1)}, u32[]{:S(2)}, u32[]{:S(2)}) async-start(f32[16,8,128]{2,1,0:T(8,128)} %get-tuple-element.21), calls=%async_computation | async-start | bytes 131072 | tf_op jit(solution)/shard_map/all_to_all | solution.py:474
  25.2 2.2 %copy-start = (bf16[8192,256]{1,0:T(8,128)(2,1)S(1)}, bf16[8192,256]{1,0:T(8,128)(2,1)}, u32[]{:S(2)}) copy-start(bf16[8192,256]{1,0:T(8,128)(2,1)} %get-tuple-element.19.lags) | copy-start | bytes 12582916
  32.1 2.2 %copy-start.1 = (bf16[8192,256]{1,0:T(8,128)(2,1)S(1)}, bf16[8192,256]{1,0:T(8,128)(2,1)}, u32[]{:S(2)}) copy-start(bf16[8192,256]{1,0:T(8,128)(2,1)} %get-tuple-element.19.lags) | copy-start | bytes 12582916
  45.1 15.7 %collective-permute-start.2 = (bf16[112,512]{1,0:T(8,128)(2,1)S(1)}, bf16[112,512]{1,0:T(8,128)(2,1)S(1)}, u32[]{:S(2)}, u32[]{:S(2)}) collective-permute-start(bf16[112,512]{1,0:T(8,128)(2,1)S(1)} %get-tuple-element.24), channel_id=1, source_target_pairs={{0,8},{1,9},{2,10},{3,11},{4,12},{5,13},{6,14},{7,15},{8,0},{9,1},... | collective-permute-start | bytes 344072 | tf_op jit(solution)/shard_map/ppermute | solution.py:73
  45.5 18.0 %collective-permute-start.3 = (bf16[112,512]{1,0:T(8,128)(2,1)S(1)}, bf16[112,512]{1,0:T(8,128)(2,1)S(1)}, u32[]{:S(2)}, u32[]{:S(2)}) collective-permute-start(bf16[112,512]{1,0:T(8,128)(2,1)S(1)} %get-tuple-element.25), channel_id=1, source_target_pairs={{0,10},{1,11},{2,8},{3,9},{4,14},{5,15},{6,12},{7,13},{8,2},{9,3},... | collective-permute-start | bytes 344072 | tf_op jit(solution)/shard_map/ppermute | solution.py:73
  47.7 17.0 %collective-permute-start.4 = (bf16[112,512]{1,0:T(8,128)(2,1)S(1)}, bf16[112,512]{1,0:T(8,128)(2,1)S(1)}, u32[]{:S(2)}, u32[]{:S(2)}) collective-permute-start(bf16[112,512]{1,0:T(8,128)(2,1)S(1)} %get-tuple-element.26), channel_id=1, source_target_pairs={{0,12},{1,13},{2,14},{3,15},{4,8},{5,9},{6,10},{7,11},{8,4},{9,5},... | collective-permute-start | bytes 344072 | tf_op jit(solution)/shard_map/ppermute | solution.py:73
  50.2 17.0 %collective-permute-start.5 = (bf16[112,512]{1,0:T(8,128)(2,1)S(1)}, bf16[112,512]{1,0:T(8,128)(2,1)S(1)}, u32[]{:S(2)}, u32[]{:S(2)}) collective-permute-start(bf16[112,512]{1,0:T(8,128)(2,1)S(1)} %get-tuple-element.27), channel_id=1, source_target_pairs={{0,14},{1,15},{2,12},{3,13},{4,10},{5,11},{6,8},{7,9},{8,6},{9,7},... | collective-permute-start | bytes 344072 | tf_op jit(solution)/shard_map/ppermute | solution.py:73
  52.8 14.4 %collective-permute-start.6 = (bf16[112,512]{1,0:T(8,128)(2,1)S(1)}, bf16[112,512]{1,0:T(8,128)(2,1)S(1)}, u32[]{:S(2)}, u32[]{:S(2)}) collective-permute-start(bf16[112,512]{1,0:T(8,128)(2,1)S(1)} %get-tuple-element.28), channel_id=1, source_target_pairs={{0,6},{1,7},{2,4},{3,5},{4,2},{5,3},{6,0},{7,1},{8,14},{9,15},{10,... | collective-permute-start | bytes 344072 | tf_op jit(solution)/shard_map/ppermute | solution.py:73
  60.9 6.9 %collective-permute-start.7 = (bf16[112,512]{1,0:T(8,128)(2,1)S(1)}, bf16[112,512]{1,0:T(8,128)(2,1)S(1)}, u32[]{:S(2)}, u32[]{:S(2)}) collective-permute-start(bf16[112,512]{1,0:T(8,128)(2,1)S(1)} %get-tuple-element.29), channel_id=1, source_target_pairs={{0,4},{1,5},{2,6},{3,7},{4,0},{5,1},{6,2},{7,3},{8,12},{9,13},{10,... | collective-permute-start | bytes 344072 | tf_op jit(solution)/shard_map/ppermute | solution.py:73
  63.4 4.8 %collective-permute-start.8 = (bf16[112,512]{1,0:T(8,128)(2,1)S(1)}, bf16[112,512]{1,0:T(8,128)(2,1)S(1)}, u32[]{:S(2)}, u32[]{:S(2)}) collective-permute-start(bf16[112,512]{1,0:T(8,128)(2,1)S(1)} %get-tuple-element.30), channel_id=1, source_target_pairs={{0,2},{1,3},{2,0},{3,1},{4,6},{5,7},{6,4},{7,5},{8,10},{9,11},{10,... | collective-permute-start | bytes 344072 | tf_op jit(solution)/shard_map/ppermute | solution.py:73
  70.8 2.0 %collective-permute-start.9 = (f32[136,1024]{1,0:T(8,128)S(1)}, f32[136,1024]{1,0:T(8,128)S(1)}, u32[]{:S(2)}, u32[]{:S(2)}) collective-permute-start(f32[136,1024]{1,0:T(8,128)S(1)} %get-tuple-element.32), channel_id=1, source_target_pairs={{0,1},{1,0},{2,3},{3,2},{4,5},{5,4},{6,7},{7,6},{8,9},{9,8},{10,11... | collective-permute-start | bytes 1671176 | tf_op jit(solution)/shard_map/ppermute | solution.py:73
